TPU v7x, 32 devices: a whole 2x2x4 slice. The times are simulated.
32 devices in a mesh: dp: 8 (over z, x), tensor: 4 (over y, core).
Axes of the slice: x: 2, y: 2, z: 4, core: 2. Of those that a mesh axis runs over, the one named last changes fastest.
Arguments:
- tokens: bfloat16 [32768, 768], P(('dp', 'tensor')), may hold values from -6 to 6
- segment_ids: int32 [64, 512], P(('dp', 'tensor')), may hold values from 0 to 3, never falling along the last dimension, each value on 1 to 256 neighbouring positions
- w_qkv: bfloat16 [768, 2304], replicated, may hold values from -0.21875 to 0.21875
- b_qkv: float32 [2304], replicated, may hold values from -3 to 3
- conv_kernel: float32 [12, 35], replicated, may hold values from -0.125 to 0.125
- w_out: bfloat16 [768, 768], replicated, may hold values from -1.75 to 1.75
- b_out: float32 [768], replicated, may hold values from -3 to 3
- norm1_gain: float32 [768], replicated, may hold values from 0.5 to 1.5
- norm1_bias: float32 [768], replicated, may hold values from -3 to 3
- w_up: bfloat16 [768, 3072], P(None, 'tensor'), may hold values from -0.21875 to 0.21875
- b_up: bfloat16 [3072], P('tensor'), may hold values from -3 to 3
- w_down: bfloat16 [3072, 768], P('tensor'), may hold values from -0.109375 to 0.109375
- b_down: float32 [768], replicated, may hold values from -3 to 3
- norm2_gain: float32 [768], replicated, may hold values from 0.5 to 1.5
- norm2_bias: float32 [768], replicated, may hold values from -3 to 3
- cotangent: bfloat16 [32768, 768], P(('dp', 'tensor')), may hold values from -6 to 6
Outputs:
- output: bfloat16 [32768, 768], P(('dp', 'tensor'))
- grad_tokens: bfloat16 [32768, 768], P(('dp', 'tensor'))
- grad_w_qkv: float32 [768, 2304], replicated
- grad_b_qkv: float32 [2304], replicated
- grad_conv: float32 [12, 35], replicated
- grad_w_out: float32 [768, 768], replicated
- grad_b_out: float32 [768], replicated
- grad_norm1_gain: float32 [768], replicated
- grad_norm1_bias: float32 [768], replicated
- grad_w_up: float32 [768, 3072], P(None, 'tensor')
- grad_b_up: float32 [3072], P('tensor')
- grad_w_down: float32 [3072, 768], P('tensor')
- grad_b_down: float32 [768], replicated
- grad_norm2_gain: float32 [768], replicated
- grad_norm2_bias: float32 [768], replicated
Inputs may be any that keep to these rules, and one draw needn't show every extreme that they name: `segment_ids`: within a packed row segment ids never fall; attention and the convolution connect only tokens of equal id in the same packed row.
All inputs are finite; a program needn't handle non-finite values.
Results may differ from a plain program's by a relative error of at most 0.015.
Values may be sent and summed in bfloat16 or wider, within the bound.
A program may use at most 320 MiB of HBM per device.

v0:
```python
import math

import jax
import jax.numpy as jnp
from jax import lax
from jax.sharding import PartitionSpec as P

TAU = 8


eps_norm = 1e-05
eps_unit = 1e-06
shrink = 0.95


def norm_forward(rows_in, norm_gain, norm_shift):
    centred = rows_in - jnp.mean(rows_in, -1, keepdims=True)
    scaling = lax.rsqrt(jnp.mean(centred * centred, -1, keepdims=True) + eps_norm)
    unit_part = centred * scaling
    return (unit_part * norm_gain + norm_shift, unit_part, scaling)


def norm_backward(grad_out, unit_part, scaling, norm_gain):
    grad_unit = grad_out * norm_gain
    grad_rows = scaling * (
        grad_unit
        - jnp.mean(grad_unit, -1, keepdims=True)
        - unit_part * jnp.mean(grad_unit * unit_part, -1, keepdims=True)
    )
    return (grad_rows, jnp.sum(grad_out * unit_part, 0), jnp.sum(grad_out, 0))


def unit_heads(vectors):
    scaling = lax.rsqrt(jnp.sum(vectors * vectors, -1, keepdims=True) + eps_unit)
    return (vectors * scaling, scaling)


def unit_back(grad_unit, unit_vec, scaling):
    return scaling * (grad_unit - unit_vec * jnp.sum(grad_unit * unit_vec, -1, keepdims=True))


def conv_forward(values, seg_ids, kernel):
    radius = kernel.shape[1] // 2
    length = values.shape[1]
    padded = jnp.pad(values, ((0, 0), (radius, radius), (0, 0), (0, 0)))
    padded_ids = jnp.pad(seg_ids, ((0, 0), (radius, radius)), constant_values=-1)
    summed = jnp.zeros_like(values)
    for offset in range(kernel.shape[1]):
        matched = (padded_ids[:, offset : offset + length] == seg_ids)[:, :, None, None]
        summed = (
            summed
            + jnp.where(matched, padded[:, offset : offset + length], 0.0)
            * kernel[:, offset][:, None]
        )
    return summed


def conv_backward(grad_ctx, values, seg_ids, kernel):
    kernel_span = kernel.shape[1]
    radius = kernel_span // 2
    length = values.shape[1]
    pad_spec = ((0, 0), (radius, radius), (0, 0), (0, 0))
    padded_vals = jnp.pad(values, pad_spec)
    padded_grad = jnp.pad(grad_ctx, pad_spec)
    padded_ids = jnp.pad(seg_ids, ((0, 0), (radius, radius)), constant_values=-1)
    grad_values = jnp.zeros_like(values)
    kernel_cols = []
    for offset in range(kernel_span):
        matched = (padded_ids[:, offset : offset + length] == seg_ids)[:, :, None, None]
        shifted = jnp.where(matched, padded_vals[:, offset : offset + length], 0.0)
        kernel_cols.append(jnp.sum(shifted * grad_ctx, axis=(0, 1, 3)))
        back_slot = kernel_span - 1 - offset
        matched_back = (padded_ids[:, back_slot : back_slot + length] == seg_ids)[:, :, None, None]
        grad_values = (
            grad_values
            + jnp.where(matched_back, padded_grad[:, back_slot : back_slot + length], 0.0)
            * kernel[:, offset][:, None]
        )
    return (grad_values, jnp.stack(kernel_cols, 1))


def attend(pieces):
    q_rows, k_rows, v_rows, seg_ids = pieces
    cosine = shrink * jnp.einsum("qhd,khd->hqk", q_rows, k_rows, preferred_element_type=jnp.float32)
    matched = (seg_ids[:, None] == seg_ids[None, :])[None]
    weight = jnp.where(matched, (1.0 - jnp.arccos(cosine) / math.pi) ** TAU, 0.0)
    totals = 1.0 + jnp.sum(weight, -1)
    summed = jnp.einsum(
        "hqk,khd->qhd", weight.astype(jnp.bfloat16), v_rows, preferred_element_type=jnp.float32
    )
    return (summed, totals.T)


def attend_back(pieces):
    q_rows, k_rows, v_rows, seg_ids, grad_sum, grad_totals = pieces
    cosine = shrink * jnp.einsum("qhd,khd->hqk", q_rows, k_rows, preferred_element_type=jnp.float32)
    matched = (seg_ids[:, None] == seg_ids[None, :])[None]
    closeness = 1.0 - jnp.arccos(cosine) / math.pi
    weight = jnp.where(matched, closeness**TAU, 0.0)
    grad_weight = (
        jnp.einsum("qhd,khd->hqk", grad_sum, v_rows, preferred_element_type=jnp.float32)
        + grad_totals.T[:, :, None]
    )
    slope = TAU / math.pi * closeness ** (TAU - 1) * lax.rsqrt(1.0 - cosine * cosine)
    grad_cos = jnp.where(matched, grad_weight * slope, 0.0).astype(jnp.bfloat16)
    grad_query = shrink * jnp.einsum(
        "hqk,khd->qhd", grad_cos, k_rows, preferred_element_type=jnp.float32
    )
    grad_key = shrink * jnp.einsum(
        "hqk,qhd->khd", grad_cos, q_rows, preferred_element_type=jnp.float32
    )
    grad_value = jnp.einsum(
        "hqk,qhd->khd", weight.astype(jnp.bfloat16), grad_sum, preferred_element_type=jnp.float32
    )
    return (grad_query, grad_key, grad_value)


def gelu_tanh(preact):
    return jax.nn.gelu(preact, approximate=True)


def body(
    tokens,
    segment_ids,
    w_qkv,
    b_qkv,
    conv_kernel,
    w_out,
    b_out,
    norm1_gain,
    norm1_bias,
    w_up,
    b_up,
    w_down,
    b_down,
    norm2_gain,
    norm2_bias,
    cotangent,
):
    row_count, model_width = tokens.shape
    seq_count, length = segment_ids.shape
    head_count = conv_kernel.shape[0]
    head_size = model_width // head_count
    rows_f32 = tokens.astype(jnp.float32)
    projected = jnp.dot(tokens, w_qkv, preferred_element_type=jnp.float32) + b_qkv
    split_parts = projected.reshape(seq_count, length, 3, head_count, head_size)
    q_unit, q_scale = unit_heads(split_parts[:, :, 0])
    k_unit, k_scale = unit_heads(split_parts[:, :, 1])
    values = split_parts[:, :, 2]
    q_low = q_unit.astype(jnp.bfloat16)
    k_low = k_unit.astype(jnp.bfloat16)
    v_low = values.astype(jnp.bfloat16)
    summed, totals = lax.map(attend, (q_low, k_low, v_low, segment_ids))
    attended = summed / totals[..., None]
    context = (attended + conv_forward(values, segment_ids, conv_kernel)).reshape(
        row_count, model_width
    )
    context_low = context.astype(jnp.bfloat16)
    resid_one = rows_f32 + jnp.dot(context_low, w_out, preferred_element_type=jnp.float32) + b_out
    first, unit_one, scale_one = norm_forward(resid_one, norm1_gain, norm1_bias)
    first_low = first.astype(jnp.bfloat16)
    gathered = lax.all_gather(first_low, "tensor", axis=0, tiled=True)
    preact = jnp.dot(gathered, w_up, preferred_element_type=jnp.float32) + b_up.astype(jnp.float32)
    activated, gelu_pull = jax.vjp(gelu_tanh, preact)
    hidden_low = activated.astype(jnp.bfloat16)
    ffn_out = (
        lax.psum_scatter(
            jnp.dot(hidden_low, w_down, preferred_element_type=jnp.float32),
            "tensor",
            scatter_dimension=0,
            tiled=True,
        )
        + b_down
    )
    output, unit_two, scale_two = norm_forward(first + ffn_out, norm2_gain, norm2_bias)
    grad_out = cotangent.astype(jnp.float32)
    d_resid_two, grad_gain_two, grad_shift_two = norm_backward(
        grad_out, unit_two, scale_two, norm2_gain
    )
    d_ffn = d_resid_two.astype(jnp.bfloat16)
    grad_b_down = jnp.sum(d_ffn.astype(jnp.float32), 0)
    gathered_grad = lax.all_gather(d_ffn, "tensor", axis=0, tiled=True)
    grad_down_part = jnp.einsum(
        "nf,nd->fd", hidden_low, gathered_grad, preferred_element_type=jnp.float32
    )
    d_hidden = jnp.einsum("nd,fd->nf", gathered_grad, w_down, preferred_element_type=jnp.float32)
    d_pre = gelu_pull(d_hidden)[0].astype(jnp.bfloat16)
    grad_bias_part = jnp.sum(d_pre.astype(jnp.float32), 0)
    grad_up_part = jnp.einsum("nd,nf->df", gathered, d_pre, preferred_element_type=jnp.float32)
    d_first_ffn = lax.psum_scatter(
        jnp.einsum("nf,df->nd", d_pre, w_up, preferred_element_type=jnp.float32),
        "tensor",
        scatter_dimension=0,
        tiled=True,
    )
    grad_w_up, grad_b_up, grad_w_down = (
        lax.psum(grad_up_part.astype(jnp.bfloat16), "dp").astype(jnp.float32),
        lax.psum(grad_bias_part.astype(jnp.bfloat16), "dp").astype(jnp.float32),
        lax.psum(grad_down_part.astype(jnp.bfloat16), "dp").astype(jnp.float32),
    )
    d_resid_one, grad_gain_one, grad_shift_one = norm_backward(
        d_resid_two + d_first_ffn, unit_one, scale_one, norm1_gain
    )
    d_proj_out = d_resid_one.astype(jnp.bfloat16)
    grad_b_out = jnp.sum(d_proj_out.astype(jnp.float32), 0)
    grad_w_out = jnp.einsum(
        "nc,nd->cd", context_low, d_proj_out, preferred_element_type=jnp.float32
    )
    d_context = jnp.einsum(
        "nd,cd->nc", d_proj_out, w_out, preferred_element_type=jnp.float32
    ).reshape(seq_count, length, head_count, head_size)
    d_summed = (d_context / totals[..., None]).astype(jnp.bfloat16)
    d_totals = -jnp.sum(d_context * attended, -1) / totals
    d_q_unit, d_k_unit, d_v_attend = lax.map(
        attend_back, (q_low, k_low, v_low, segment_ids, d_summed, d_totals)
    )
    d_v_conv, grad_conv = conv_backward(d_context, values, segment_ids, conv_kernel)
    d_queries = unit_back(d_q_unit, q_unit, q_scale)
    d_keys = unit_back(d_k_unit, k_unit, k_scale)
    d_projected = (
        jnp.stack((d_queries, d_keys, d_v_attend + d_v_conv), 2)
        .reshape(row_count, 3 * model_width)
        .astype(jnp.bfloat16)
    )
    grad_b_qkv = jnp.sum(d_projected.astype(jnp.float32), 0)
    grad_w_qkv = jnp.einsum("nd,ne->de", tokens, d_projected, preferred_element_type=jnp.float32)
    grad_tokens = (
        jnp.einsum("ne,de->nd", d_projected, w_qkv, preferred_element_type=jnp.float32)
        + d_resid_one
    ).astype(jnp.bfloat16)
    summed_grads = lax.psum(
        (
            grad_w_qkv,
            grad_b_qkv,
            grad_conv,
            grad_w_out,
            grad_b_out,
            grad_gain_one,
            grad_shift_one,
            grad_b_down,
            grad_gain_two,
            grad_shift_two,
        ),
        ("dp", "tensor"),
    )
    return (
        output.astype(jnp.bfloat16),
        grad_tokens,
        summed_grads[0],
        summed_grads[1],
        summed_grads[2],
        summed_grads[3],
        summed_grads[4],
        summed_grads[5],
        summed_grads[6],
        grad_w_up,
        grad_b_up,
        grad_w_down,
        summed_grads[7],
        summed_grads[8],
        summed_grads[9],
    )


def solution(mesh):
    placed = (
        P(("dp", "tensor"), None),
        P(("dp", "tensor"), None),
        P(),
        P(),
        P(),
        P(),
        P(),
        P(),
        P(),
        P(None, "tensor"),
        P("tensor"),
        P("tensor", None),
        P(),
        P(),
        P(),
        P(("dp", "tensor"), None),
    )
    return jax.shard_map(
        body,
        mesh=mesh,
        in_specs=placed,
        out_specs=(
            P(("dp", "tensor"), None),
            P(("dp", "tensor"), None),
            P(),
            P(),
            P(),
            P(),
            P(),
            P(),
            P(),
            P(None, "tensor"),
            P("tensor"),
            P("tensor", None),
            P(),
            P(),
            P(),
        ),
        check_vma=False,
    )
```

profile of v0, /device:TPU:0, one launch (start us, length us, event | category | flops | bytes accessed | tf_op | source)
XLA Modules:
  0.0 1084.1 jit_solution(11766021954833736426)
XLA Ops:
  17.3 8.0 convolution_add_fusion
  25.3 9.6 copy.252
  34.9 13.3 %reshape.239 = f32[2,512,3,12,64]{1,0,4,3,2:T(2,128)} reshape(f32[1024,2304]{0,1:T(8,128)} %copy.252) | data formatting | bytes 18874368 | tf_op jit(solution)/shard_map/reshape | solution.py:146
  48.2 8.8 fusion.227
  74.8 67.2 %while.26 = (s32[]{:T(128)}, f32[2,512,12,64]{1,3,2,0:T(8,128)}, f32[2,512,12]{1,2,0:T(8,128)}, bf16[2,512,12,64]{1,3,2,0:T(8,128)(2,1)}, s32[2,512]{1,0:T(2,128...) while((s32[]{:T(128)}, f32[2,512,12,64]{1,3,2,0:T(8,128)}, ...), condition=%wide.region_4.5_spmd, body=%wide.region_2.4_spmd.sunk | while | flops 843317248 | bytes 48587436 | solution.py:153
  75.2 29.6 %fusion.270 = (f32[12,512]{1,0:T(8,128)S(1)}, bf16[12,512,512]{1,2,0:T(8,128)(2,1)S(1)}) fusion(bf16[2,512,12,64]{1,3,2,0:T(8,128)(2,1)} %get-tuple-element.563, s32[]{:T(128)} %get-tuple-element.549, bf16[2,512,12,64]{1,3,2,0:T(8,128)(2,1)} %get-tuple-element.562, pred[512,512]{0,1:T(8,128)(4,1)S(1)} %broadcast_compare_fusion.4), kind=kOutput, calls=%fused_computation.454.clone.1 | convolution fusion | flops 440395776 | bytes 8152064 | tf_op jit(solution)/shard_map/while/body/eval_jaxpr/qhd,khd->hqk/dot_general | solution.py:84
  108.5 29.6 %fusion.270 = (f32[12,512]{1,0:T(8,128)S(1)}, bf16[12,512,512]{1,2,0:T(8,128)(2,1)S(1)}) fusion(bf16[2,512,12,64]{1,3,2,0:T(8,128)(2,1)} %get-tuple-element.563, s32[]{:T(128)} %get-tuple-element.549, bf16[2,512,12,64]{1,3,2,0:T(8,128)(2,1)} %get-tuple-element.562, pred[512,512]{0,1:T(8,128)(4,1)S(1)} %broadcast_compare_fusion.4), kind=kOutput, calls=%fused_computation.454.clone.1 | convolution fusion | flops 440395776 | bytes 8152064 | tf_op jit(solution)/shard_map/while/body/eval_jaxpr/qhd,khd->hqk/dot_general | solution.py:84
  142.0 58.4 %add_convert_fusion.2 = bf16[2,512,12,64]{1,3,2,0:T(8,128)(2,1)S(1)} fusion(f32[2,512,12,64]{1,3,2,0:T(8,128)} %bitcast.223, f32[12]{0:T(128)} %get-tuple-element.324, f32[12]{0:T(128)} %get-tuple-element.325, f32[12]{0:T(128)} %get-tuple-element.292, f32[12]{0:T(128)} %get-tuple-element.293, f32[12]{0:T(128)} %get-tuple-element.294, ...), kind=kLoop, calls=%fused_computation.346 | loop fusion | flops 83361792 | bytes 7949968 | tf_op jit(solution)/shard_map/convert_element_type | solution.py:158
  208.8 47.9 %all-gather.3.cloned.1.call-done = bf16[4096,768]{0,1:T(8,128)(2,1)} async-done(((bf16[1024,768]{0,1:T(8,128)(2,1)}), bf16[4096,768]{0,1:T(8,128)(2,1)}) %all-gather.3.cloned.1.call-update) | async-done | bytes 6291472 | tf_op jit(solution)/shard_map/all_gather | solution.py:162
  256.7 8.0 fusion.229
  269.3 9.1 fusion.220
  281.1 96.6 %reduce-scatter.3.cloned.1.call-done = f32[1024,768]{0,1:T(8,128)} async-done(((f32[4096,768]{0,1:T(8,128)}), f32[1024,768]{0,1:T(8,128)}) %reduce-scatter.3.cloned.1.call-update) | async-done | bytes 3145744 | tf_op jit(solution)/shard_map/reduce_scatter | solution.py:167
  388.9 46.5 %all-gather.5.cloned.1.call-done = bf16[4096,768]{0,1:T(8,128)(2,1)} async-done(((bf16[1024,768]{0,1:T(8,128)(2,1)}), bf16[4096,768]{0,1:T(8,128)(2,1)}) %all-gather.5.cloned.1.call-update) | async-done | bytes 6291472 | tf_op jit(solution)/shard_map/all_gather | solution.py:182
  435.4 18.7 %fusion.221 = (bf16[768]{0:T(1024)(128)(2,1)}, bf16[4096,768]{1,0:T(8,128)(2,1)S(1)}) fusion(f32[4096,768]{1,0:T(8,128)} %copy-done.80, f32[768]{0:T(1024)} %convert_element_type.102, bf16[4096,768]{0,1:T(8,128)(2,1)} %all-gather.5.cloned.1.call-done, bf16[768,768]{1,0:T(8,128)(2,1)} %param.31), kind=kOutput, calls=%fused_computation.452 | convolution fusion | flops 4901043200 | bytes 26350080 | tf_op jit(solution)/shard_map/nd,fd->nf/dot_general | solution.py:186
  473.9 17.5 %convolution_convert_fusion = bf16[768,768]{1,0:T(8,128)(2,1)} fusion(bf16[4096,768]{0,1:T(8,128)(2,1)} %all-gather.5.cloned.1.call-done, f32[4096,768]{1,0:T(8,128)} %copy-done.80, f32[768]{0:T(1024)} %convert_element_type.102), kind=kOutput, calls=%fused_computation.361 | convolution fusion | flops 4863885312 | bytes 20057088 | tf_op jit(solution)/shard_map/nf,nd->fd/dot_general | solution.py:183
  491.4 10.8 convolution_convert_fusion.1
  502.2 61.7 %reduce-scatter.5.cloned.1.call-done = f32[1024,768]{0,1:T(8,128)} async-done(((f32[4096,768]{0,1:T(8,128)}), f32[1024,768]{0,1:T(8,128)}) %reduce-scatter.5.cloned.1.call-update) | async-done | bytes 3145744 | tf_op jit(solution)/shard_map/reduce_scatter | solution.py:190
  587.3 18.4 %multiply_reduce_fusion.3 = (f32[12]{0:T(128)}, f32[12]{0:T(128)}, f32[12]{0:T(128)}, f32[12]{0:T(128)}, f32[12]{0:T(128)}, /*index=5*/f32[12]{0:T(128)}, f32[12...) fusion(f32[2,512,12,64]{1,3,2,0:T(8,128)} %bitcast.224, pred[2,512]{1,0:T(4,128)(4,1)S(1)} %copy-done.65, ...), kind=kLoop, calls=%fused_computation.296 | loop fusion | flops 21233556 | bytes 9446832 | tf_op jit(solution)/shard_map/reduce_sum | solution.py:71
  605.9 8.9 multiply_reduce_fusion.4
  622.6 159.7 %while.27 = (s32[]{:T(128)}, f32[2,512,12,64]{1,3,2,0:T(8,128)}, f32[2,512,12,64]{1,3,2,0:T(8,128)}, f32[2,512,12,64]{1,3,2,0:T(8,128)}, bf16[2,512,12,64]{1,3,2...) while((s32[]{:T(128)}, f32[2,512,12,64]{1,3,2,0:T(8,128)}, ...), condition=%wide.region_17.18_spmd, body=%wide.region_16.17_spmd.sunk | while | flops 2105540608 | bytes 119352664 | solution.py:214
  644.0 32.8 %fusion.281 = bf16[12,512,512]{2,1,0:T(8,128)(2,1)S(1)} fusion(f32[12,512,512]{2,1,0:T(8,128)S(1)} %fusion.280, f32[12,512]{1,0:T(8,128)S(1)} %bitcast.237, pred[512,512]{1,0:T(8,128)(4,1)} %broadcast_compare_fusion.5, bf16[2,512,12,64]{1,3,2,0:T(8,128)(2,1)S(1)} %copy-done.20, s32[]{:T(128)} %get-tuple-element.576, ...), kind=kOutput, calls=%fused_computation.22.clone.1 | convolution fusion | flops 459276288 | bytes 20743168 | tf_op jit(solution)/shard_map/while/body/eval_jaxpr/qhd,khd->hqk/dot_general | solution.py:101
  683.4 27.4 %bitcast_dynamic-update-slice_fusion.14 = f32[2,512,12,64]{1,3,2,0:T(8,128)} fusion(f32[2,512,12,64]{1,3,2,0:T(8,128)} %get-tuple-element.579, s32[]{:T(128)} %get-tuple-element.576, f32[12,512,512]{2,1,0:T(8,128)S(1)} %fusion.280, pred[512,512]{1,0:T(8,128)(4,1)S(1)} %copy-done.27, bf16[2,512,12,64]{1,3,2,0:T(8,128)(2,1)S(1)} %copy-done.34), kind=kOutput, calls=%fused_computation.26.clone.1 | convolution fusion | flops 437256192 | bytes 15205376 | tf_op jit(solution)/shard_map/while/body/eval_jaxpr/hqk,qhd->khd/dot_general | solution.py:112
  715.1 32.8 %fusion.281 = bf16[12,512,512]{2,1,0:T(8,128)(2,1)S(1)} fusion(f32[12,512,512]{2,1,0:T(8,128)S(1)} %fusion.280, f32[12,512]{1,0:T(8,128)S(1)} %bitcast.237, pred[512,512]{1,0:T(8,128)(4,1)} %broadcast_compare_fusion.5, bf16[2,512,12,64]{1,3,2,0:T(8,128)(2,1)S(1)} %copy-done.20, s32[]{:T(128)} %get-tuple-element.576, ...), kind=kOutput, calls=%fused_computation.22.clone.1 | convolution fusion | flops 459276288 | bytes 20743168 | tf_op jit(solution)/shard_map/while/body/eval_jaxpr/qhd,khd->hqk/dot_general | solution.py:101
  754.5 27.4 %bitcast_dynamic-update-slice_fusion.14 = f32[2,512,12,64]{1,3,2,0:T(8,128)} fusion(f32[2,512,12,64]{1,3,2,0:T(8,128)} %get-tuple-element.579, s32[]{:T(128)} %get-tuple-element.576, f32[12,512,512]{2,1,0:T(8,128)S(1)} %fusion.280, pred[512,512]{1,0:T(8,128)(4,1)S(1)} %copy-done.27, bf16[2,512,12,64]{1,3,2,0:T(8,128)(2,1)S(1)} %copy-done.34), kind=kOutput, calls=%fused_computation.26.clone.1 | convolution fusion | flops 437256192 | bytes 15205376 | tf_op jit(solution)/shard_map/while/body/eval_jaxpr/hqk,qhd->khd/dot_general | solution.py:112
  782.3 60.2 %fusion.198 = bf16[2,512,1,12,64]{1,4,3,0,2:T(8,128)(2,1)} fusion(f32[2,512,12,64]{1,3,2,0:T(8,128)} %get-tuple-element.111, f32[2,512,12,64]{1,3,2,0:T(8,128)} %get-tuple-element.390, f32[12]{0:T(128)} %get-tuple-element.324, f32[12]{0:T(128)} %get-tuple-element.325, f32[12]{0:T(128)} %get-tuple-element.292, f32[12]{0:T(128)} %get-tuple-element.293, ...), kind=kLoop, calls=%fused_computation.349 | loop fusion | flops 82575360 | bytes 7900816 | tf_op jit(solution)/shard_map/stack | solution.py:221
  852.0 9.4 copy.268
  874.2 22.0 %psum.99 = bf16[768]{0:T(1024)(128)(2,1)S(1)} all-reduce(bf16[768]{0:T(1024)(128)(2,1)} %get-tuple-element.372), channel_id=1, replica_groups=mesh['dp'=8,'tensor'=4] {'dp'}, use_global_device_ids=true, to_apply=%region_69.70 | all-reduce | flops 768 | bytes 3072 | tf_op jit(solution)/shard_map/psum | solution.py:198
  903.0 9.2 multiply_reduce_fusion.2
  924.1 17.3 %multiply_reduce_fusion.1 = (f32[12]{0:T(128)}, f32[12]{0:T(128)}, f32[12]{0:T(128)}, f32[12]{0:T(128)}, f32[12]{0:T(128)}, /*index=5*/f32[12]{0:T(128)}, f32[12]{0:T(128)}, f32[12]{0:T(128)}, f32[12]{0:T(128)}) fusion(f32[2,512,12,64]{1,3,2,0:T(8,128)} %bitcast.225, pred[2,512]{1,0:T(4,128)(4,1)} %get-tuple-element.424, f32[2,512,12,64]{1,0,3,2:T(2,128)} %reshape.240, ...), kind=kLoop, calls=%fused_computation.294 | loop fusion | flops 21233556 | bytes 6301104 | tf_op jit(solution)/shard_map/reduce_sum | solution.py:71
  991.2 39.2 %all-reduce.3 = (f32[2304]{0:T(1024)}, f32[12,35]{1,0:T(8,128)}, f32[768]{0:T(1024)}, f32[768]{0:T(1024)}, f32[768]{0:T(1024)}, /*index=5*/f32[768]{0:T(1024)}, f32[768]{0:T(1024)}, f32[768]{0:T(1024)}) all-reduce(f32[2304]{0:T(1024)S(1)} %reduce_sum.539, f32[12,35]{1,0:T(8,128)} %stack.159, ...), channel_id=1, replica_groups=mesh['dp'=8,'tensor'=4] {'dp','tensor'}, use_global_device_ids=true, to_apply=%region_22.23 | all-reduce | flops 7332 | bytes 58656 | tf_op jit(solution)/shard_map/psum | solution.py:231
  1030.4 35.5 %all-reduce.9.cloned.1.call-done = (f32[768,2304]{0,1:T(8,128)}, f32[768,768]{1,0:T(8,128)}) async-done(((f32[768,2304]{0,1:T(8,128)}, f32[768,768]{1,0:T(8,128)}), (f32[768,2304]{0,1:T(8,128)}, f32[768,768]{1,0:T(8,128)})) %all-reduce.9.cloned.1.call-update) | async-done | bytes 9437200 | tf_op jit(solution)/shard_map/psum | solution.py:231
  1065.9 8.0 copy.343
  (320 shorter events, 228.3 us)
Async XLA Ops:
  7.2 249.5 %all-gather.3.cloned.1.call-start = ((), (), s32[]{:S(2)}) async-start(), calls=%async_computation.2 | async-start | bytes 7864320 | tf_op jit(solution)/shard_map/all_gather | solution.py:162
  61.9 80.2 %copy-start.48 = (pred[2,512]{1,0:T(4,128)(4,1)}, pred[2,512]{1,0:T(4,128)(4,1)S(1)}, u32[]{:S(2)}) copy-start(pred[2,512]{1,0:T(4,128)(4,1)S(1)} %get-tuple-element.418) | copy-start | bytes 3076
  61.9 80.2 %copy-start.50 = (pred[2,512]{1,0:T(4,128)(4,1)}, pred[2,512]{1,0:T(4,128)(4,1)S(1)}, u32[]{:S(2)}) copy-start(pred[2,512]{1,0:T(4,128)(4,1)S(1)} %get-tuple-element.419) | copy-start | bytes 3076
  61.9 80.2 %copy-start.52 = (pred[2,512]{1,0:T(4,128)(4,1)}, pred[2,512]{1,0:T(4,128)(4,1)S(1)}, u32[]{:S(2)}) copy-start(pred[2,512]{1,0:T(4,128)(4,1)S(1)} %get-tuple-element.420) | copy-start | bytes 3076
  75.2 29.7 %copy-start.15 = (f32[2,512,12,64]{1,3,2,0:T(8,128)S(1)}, f32[2,512,12,64]{1,3,2,0:T(8,128)}, u32[]{:S(2)}) copy-start(f32[2,512,12,64]{1,3,2,0:T(8,128)} %get-tuple-element.550) | copy-start | bytes 9437188 | tf_op jit(solution)/shard_map/while
  75.2 29.7 %copy-start.19 = (bf16[2,512,12,64]{1,3,2,0:T(8,128)(2,1)S(1)}, bf16[2,512,12,64]{1,3,2,0:T(8,128)(2,1)}, u32[]{:S(2)}) copy-start(bf16[2,512,12,64]{1,3,2,0:T(8,128)(2,1)} %get-tuple-element.560) | copy-start | bytes 4718596 | tf_op jit(solution)/shard_map/while
  108.5 29.7 %copy-start.15 = (f32[2,512,12,64]{1,3,2,0:T(8,128)S(1)}, f32[2,512,12,64]{1,3,2,0:T(8,128)}, u32[]{:S(2)}) copy-start(f32[2,512,12,64]{1,3,2,0:T(8,128)} %get-tuple-element.550) | copy-start | bytes 9437188 | tf_op jit(solution)/shard_map/while
  108.5 29.7 %copy-start.19 = (bf16[2,512,12,64]{1,3,2,0:T(8,128)(2,1)S(1)}, bf16[2,512,12,64]{1,3,2,0:T(8,128)(2,1)}, u32[]{:S(2)}) copy-start(bf16[2,512,12,64]{1,3,2,0:T(8,128)(2,1)} %get-tuple-element.560) | copy-start | bytes 4718596 | tf_op jit(solution)/shard_map/while
  207.5 170.2 %reduce-scatter.3.cloned.1.call-start = ((), (), s32[]{:S(2)}) async-start(), calls=%async_computation.3 | async-start | bytes 15728640 | tf_op jit(solution)/shard_map/reduce_scatter | solution.py:167
  256.7 12.6 %copy-start.77 = (bf16[768,768]{1,0:T(8,128)(2,1)S(1)}, bf16[768,768]{1,0:T(8,128)(2,1)}, u32[]{:S(2)}) copy-start(bf16[768,768]{1,0:T(8,128)(2,1)} %param.31) | copy-start | bytes 3538948
  278.5 157.0 %all-gather.5.cloned.1.call-start = ((), (), s32[]{:S(2)}) async-start(), calls=%async_computation.4 | async-start | bytes 7864320 | tf_op jit(solution)/shard_map/all_gather | solution.py:182
  388.9 175.1 %reduce-scatter.5.cloned.1.call-start = ((), (), s32[]{:S(2)}) async-start(), calls=%async_computation.5 | async-start | bytes 15728640 | tf_op jit(solution)/shard_map/reduce_scatter | solution.py:190
  435.4 21.4 %copy-start.78 = (bf16[768,768]{1,0:T(8,128)(2,1)S(1)}, bf16[768,768]{1,0:T(8,128)(2,1)}, u32[]{:S(2)}) copy-start(bf16[768,768]{1,0:T(8,128)(2,1)} %param.29) | copy-start | bytes 3538948
  464.8 432.0 %all-reduce.11.cloned.1.call-start = ((), (), s32[]{:S(2)}) async-start(), calls=%async_computation.7 | async-start | bytes 4718592 | tf_op jit(solution)/shard_map/psum | solution.py:197
  502.2 563.7 %all-reduce.9.cloned.1.call-start = ((), (), s32[]{:S(2)}) async-start(), calls=%async_computation.6 | async-start | bytes 18874368 | tf_op jit(solution)/shard_map/psum | solution.py:231
  587.2 18.5 %copy-start.1 = (f32[2,512,1,12,64]{1,4,3,0,2:T(8,128)S(1)}, f32[2,512,1,12,64]{1,4,3,0,2:T(8,128)}, u32[]{:S(2)}) copy-start(f32[2,512,1,12,64]{1,4,3,0,2:T(8,128)} %copy.432) | copy-start | bytes 9437188
  587.3 18.5 %copy-start.3 = (f32[2,512,12,64]{1,0,3,2:T(2,128)S(1)}, f32[2,512,12,64]{1,0,3,2:T(2,128)}, u32[]{:S(2)}) copy-start(f32[2,512,12,64]{1,0,3,2:T(2,128)} %reshape.240) | copy-start | bytes 9437188
  587.3 18.5 %copy-start.17 = (f32[2,512,12,64]{1,3,2,0:T(8,128)S(1)}, f32[2,512,12,64]{1,3,2,0:T(8,128)}, u32[]{:S(2)}) copy-start(f32[2,512,12,64]{1,3,2,0:T(8,128)} %get-tuple-element.107) | copy-start | bytes 9437188
  587.3 18.5 %copy-start.64 = (pred[2,512]{1,0:T(4,128)(4,1)S(1)}, pred[2,512]{1,0:T(4,128)(4,1)}, u32[]{:S(2)}) copy-start(pred[2,512]{1,0:T(4,128)(4,1)} %get-tuple-element.391) | copy-start | bytes 3076
  587.3 18.5 %copy-start.66 = (pred[2,512]{1,0:T(4,128)(4,1)S(1)}, pred[2,512]{1,0:T(4,128)(4,1)}, u32[]{:S(2)}) copy-start(pred[2,512]{1,0:T(4,128)(4,1)} %get-tuple-element.393) | copy-start | bytes 3076
  587.3 18.5 %copy-start.67 = (pred[2,512]{1,0:T(4,128)(4,1)S(1)}, pred[2,512]{1,0:T(4,128)(4,1)}, u32[]{:S(2)}) copy-start(pred[2,512]{1,0:T(4,128)(4,1)} %get-tuple-element.394) | copy-start | bytes 3076
  587.3 18.5 %copy-start.68 = (pred[2,512]{1,0:T(4,128)(4,1)S(1)}, pred[2,512]{1,0:T(4,128)(4,1)}, u32[]{:S(2)}) copy-start(pred[2,512]{1,0:T(4,128)(4,1)} %get-tuple-element.395) | copy-start | bytes 3076
  587.3 18.5 %copy-start.69 = (pred[2,512]{1,0:T(4,128)(4,1)S(1)}, pred[2,512]{1,0:T(4,128)(4,1)}, u32[]{:S(2)}) copy-start(pred[2,512]{1,0:T(4,128)(4,1)} %get-tuple-element.396) | copy-start | bytes 3076
  587.3 18.5 %copy-start.70 = (pred[2,512]{1,0:T(4,128)(4,1)S(1)}, pred[2,512]{1,0:T(4,128)(4,1)}, u32[]{:S(2)}) copy-start(pred[2,512]{1,0:T(4,128)(4,1)} %get-tuple-element.397) | copy-start | bytes 3076
  587.3 18.5 %copy-start.73 = (pred[2,512]{1,0:T(4,128)(4,1)S(1)}, pred[2,512]{1,0:T(4,128)(4,1)}, u32[]{:S(2)}) copy-start(pred[2,512]{1,0:T(4,128)(4,1)} %get-tuple-element.400) | copy-start | bytes 3076
  622.6 159.7 %copy-start.49 = (pred[2,512]{1,0:T(4,128)(4,1)S(1)}, pred[2,512]{1,0:T(4,128)(4,1)}, u32[]{:S(2)}) copy-start(pred[2,512]{1,0:T(4,128)(4,1)} %copy-done.48) | copy-start | bytes 3076
  622.6 159.7 %copy-start.51 = (pred[2,512]{1,0:T(4,128)(4,1)S(1)}, pred[2,512]{1,0:T(4,128)(4,1)}, u32[]{:S(2)}) copy-start(pred[2,512]{1,0:T(4,128)(4,1)} %copy-done.50) | copy-start | bytes 3076
  622.6 159.7 %copy-start.53 = (pred[2,512]{1,0:T(4,128)(4,1)S(1)}, pred[2,512]{1,0:T(4,128)(4,1)}, u32[]{:S(2)}) copy-start(pred[2,512]{1,0:T(4,128)(4,1)} %copy-done.52) | copy-start | bytes 3076
  644.0 32.8 %copy-start.9 = (bf16[2,512,12,64]{1,3,2,0:T(8,128)(2,1)S(1)}, bf16[2,512,12,64]{1,3,2,0:T(8,128)(2,1)}, u32[]{:S(2)}) copy-start(bf16[2,512,12,64]{1,3,2,0:T(8,128)(2,1)} %get-tuple-element.596) | copy-start | bytes 4718596 | tf_op jit(solution)/shard_map/while
  715.1 32.8 %copy-start.9 = (bf16[2,512,12,64]{1,3,2,0:T(8,128)(2,1)S(1)}, bf16[2,512,12,64]{1,3,2,0:T(8,128)(2,1)}, u32[]{:S(2)}) copy-start(bf16[2,512,12,64]{1,3,2,0:T(8,128)(2,1)} %get-tuple-element.596) | copy-start | bytes 4718596 | tf_op jit(solution)/shard_map/while
  782.3 60.2 %copy-start.13 = (f32[2,512,1,12,64]{1,0,4,3,2:T(2,128)S(1)}, f32[2,512,1,12,64]{1,0,4,3,2:T(2,128)}, u32[]{:S(2)}) copy-start(f32[2,512,1,12,64]{1,0,4,3,2:T(2,128)} %get-tuple-element.386) | copy-start | bytes 9437188
  903.0 21.1 %copy-start.54 = (pred[2,512]{1,0:T(4,128)(4,1)S(1)}, pred[2,512]{1,0:T(4,128)(4,1)}, u32[]{:S(2)}) copy-start(pred[2,512]{1,0:T(4,128)(4,1)} %get-tuple-element.421) | copy-start | bytes 3076
  (67 other events, 272.7 us)
Sparse Core Ops, SparseCore 0:
  207.6 49.0 all-gather.2
  278.6 99.0 reduce-scatter.2
  389.0 46.3 all-gather.4
  464.9 99.0 reduce-scatter.4
  567.4 109.0 all-reduce.10
  874.3 191.5 all-reduce.8
where the time goes:
time: 1090 us; the launch traced here: 1080 us
  matrix products  299 us (27%)
  waiting for transfers between devices  288 us (26%)
  other arithmetic  228 us (21%)
  local copies, waits for them, and re-layouts  174 us (16%)
  blocking collectives  61.2 us (6%)
  loops' own time  18.3 us (2%)
  between operations  15.2 us (1%)
    reduce_scatter x1, waiting for transfers between devices, body(): lax.psum_scatter(jnp.dot(hidden_low, w_down, preferred_element_type=jnp.f...  96.6 us
    dot_general x2, matrix products, attend_back(): jnp.einsum('qhd,khd->hqk', grad_sum, v_rows, preferred_element_type=jnp.f...  65.5 us
    reduce_scatter x1, waiting for transfers between devices, body(): lax.psum_scatter(jnp.einsum('nf,df->nd', d_pre, w_up, preferred_element_t...  61.7 us
    another operation x1, other arithmetic, body(): jnp.stack((d_queries, d_keys, d_v_attend + d_v_conv), 2)  60.2 us
    dot_general x2, matrix products, attend(): jnp.einsum('qhd,khd->hqk', q_rows, k_rows, preferred_element_type=jnp.flo...  59.3 us
    convert_element_type x1, other arithmetic, body(): context_low = context.astype(jnp.bfloat16)  58.4 us
    dot_general x2, matrix products, attend_back(): jnp.einsum('hqk,qhd->khd', weight.astype(jnp.bfloat16), grad_sum, preferr...  54.8 us
    reduce_sum x5, other arithmetic, conv_backward(): kernel_cols.append(jnp.sum(shifted * grad_ctx, axis=(0, 1, 3)))  54 us
  transfers between devices with their start and end apart: 6, of which 5 were waited for; matrix products, arithmetic and copies ran while one was open for 39% of the time, Pallas kernels for 0%

commit v1 on v0

v1 whole, which is shorter than its diff:
```python
import functools
import math

import jax
import jax.numpy as jnp
from jax import lax
from jax.experimental import pallas as pl
from jax.experimental.pallas import tpu as pltpu
from jax.sharding import PartitionSpec as P

F32 = jnp.float32
BF16 = jnp.bfloat16
EPS_NORM = 1e-5
EPS_UNIT = 1e-6
SHRINK = 0.95
TAU = 8
SLOPE = TAU / math.pi
ARC = (0.49999996, -0.06830509, 0.02825875, -0.01557005, 0.00864352, -0.00363107, 0.00076235)
QUAD = 256
PAIR = 128
HEAD = 64
BLK = 128
HALO = 64


def dot_nn(a, b):
    return lax.dot_general(a, b, (((1,), (0,)), ((), ())), preferred_element_type=F32)


def dot_nt(a, b):
    return lax.dot_general(a, b, (((1,), (1,)), ((), ())), preferred_element_type=F32)


def dot_tn(a, b):
    return lax.dot_general(a, b, (((0,), (0,)), ((), ())), preferred_element_type=F32)


def lanes(shape):
    return lax.broadcasted_iota(jnp.int32, shape, len(shape) - 1)


def rows(shape):
    return lax.broadcasted_iota(jnp.int32, shape, len(shape) - 2)


def head_sum(values):
    width = values.shape[-1]
    ones = (rows((width, width)) // HEAD == lanes((width, width)) // HEAD).astype(BF16)
    high = values.astype(BF16)
    low = (values - high.astype(F32)).astype(BF16)
    return dot_nn(high, ones) + dot_nn(low, ones)


def closeness_terms(cosine):
    size = jnp.abs(cosine)
    room = 1.0 - size
    inverse = lax.rsqrt(room)
    poly = jnp.full_like(size, ARC[-1])
    for coefficient in ARC[-2::-1]:
        poly = poly * size + coefficient
    small = room * inverse * poly
    close = jnp.where(cosine >= 0.0, 1.0 - small, small)
    two = close * close
    four = two * two
    slope = (four * two) * (close * inverse) * lax.rsqrt(1.0 + size)
    return four * four, slope


def head_mask(half, shape):
    return (lanes(shape) // HEAD == half).astype(BF16)


def window_of(block, blocks):
    low = max(0, block * BLK - 256)
    high = min(blocks * BLK, block * BLK + BLK + 256)
    return low, high


def band(taps, count):
    spread = jnp.broadcast_to(taps, (count, taps.shape[1]))
    return pltpu.roll(spread, 0, 1, stride=1, stride_axis=0)


def norm_stats(values):
    centred = values - jnp.mean(values, -1, keepdims=True)
    scaling = lax.rsqrt(jnp.mean(centred * centred, -1, keepdims=True) + EPS_NORM)
    return centred * scaling, scaling


def build_masks(seg_col, seg_pad, same_ref, near_ref):
    length = seg_col.shape[0]
    for start in range(0, length, BLK):
        own = seg_col[start : start + BLK]
        same_ref[start : start + BLK, :] = jnp.where(
            own == seg_pad[:, HALO : HALO + length], 1.0, 0.0
        ).astype(BF16)
        near_ref[start // BLK] = jnp.where(
            own == seg_pad[:, start : start + 2 * BLK], 1.0, 0.0
        ).astype(BF16)


def build_near(seg_col, seg_pad, near_ref):
    length = seg_col.shape[0]
    for start in range(0, length, BLK):
        own = seg_col[start : start + BLK]
        near_ref[start // BLK] = jnp.where(
            own == seg_pad[:, start : start + 2 * BLK], 1.0, 0.0
        ).astype(BF16)


def attend_kernel(
    x_ref, col_ref, pad_ref, wq_ref, wk_ref, wv_ref, bq_ref, bk_ref, bv_ref, tap_ref, wo_ref, bo_ref,
    q_ref, k_ref, v_ref, sq_ref, sk_ref, w_ref, s_ref, att_ref, inv_ref, ctx_ref, res_ref,
    same_ref, near_ref, vv_ref,
):
    quad = pl.program_id(1)
    length = x_ref.shape[0]
    blocks = length // BLK

    @pl.when(quad == 0)
    def _():
        build_masks(col_ref[...], pad_ref[0], same_ref, near_ref)
        for half in range(2):
            edge = jnp.zeros((HALO, 2 * PAIR), BF16)
            vv_ref[half, :HALO] = edge
            vv_ref[half, HALO + length :] = edge
            vv_ref[half, HALO : HALO + length, PAIR:] = head_mask(half, (length, PAIR))

    for start in range(0, length, BLK):
        here = slice(start, start + BLK)
        x = x_ref[here]
        for w, b, unit, scale, factor in (
            (wq_ref, bq_ref, q_ref, sq_ref, SHRINK),
            (wk_ref, bk_ref, k_ref, sk_ref, 1.0),
        ):
            part = dot_nn(x, w[...]) + b[...]
            scaling = lax.rsqrt(head_sum(part * part) + EPS_UNIT)
            unit[here] = (part * (scaling * factor)).astype(BF16)
            scale[here] = scaling.astype(BF16)
        v_ref[here] = (dot_nn(x, wv_ref[...]) + bv_ref[...]).astype(BF16)

    def one_pair(pair, carry):
        at = pl.ds(pl.multiple_of(pair * PAIR, PAIR), PAIR)
        v = v_ref[:, at]
        for half in range(2):
            vv_ref[half, HALO : HALO + length, :PAIR] = v * head_mask(half, (length, PAIR))
        for block in range(blocks):
            here = slice(block * BLK, block * BLK + BLK)
            low, high = window_of(block, blocks)
            q = q_ref[here, at]
            total = jnp.zeros((BLK, 2 * PAIR), F32)
            near = jnp.zeros((BLK, PAIR), F32)
            for half in range(2):
                head = pair * 2 + half
                q_half = q * head_mask(half, (BLK, PAIR))
                for start in range(low, high, KCH):
                    stop = min(start + KCH, high)
                    cosine = dot_nt(q_half, k_ref[start:stop, at])
                    weight, slope = closeness_terms(cosine)
                    same = same_ref[here, start:stop]
                    weight = weight.astype(BF16) * same
                    w_ref[0, head, here, start:stop] = weight
                    s_ref[0, head, here, start:stop] = slope.astype(BF16) * same
                    total += dot_nn(weight, vv_ref[half, HALO + start : HALO + stop])
                if low > 0:
                    w_ref[0, head, here, :low] = jnp.zeros((BLK, low), BF16)
                if high < length:
                    w_ref[0, head, here, high:] = jnp.zeros((BLK, length - high), BF16)
                taps = band(tap_ref[0, pl.ds(head, 1)], BLK).astype(BF16) * near_ref[block]
                near += dot_nn(taps, vv_ref[half, block * BLK : block * BLK + 2 * BLK, :PAIR])
            inverse = 1.0 / (1.0 + total[:, PAIR:])
            attended = total[:, :PAIR] * inverse
            att_ref[here, at] = attended.astype(BF16)
            inv_ref[here, at] = inverse.astype(BF16)
            ctx_ref[here, at] = (attended + near).astype(BF16)
        return carry

    lax.fori_loop(0, QUAD // PAIR, one_pair, 0)

    for start in range(0, length, BLK):
        here = slice(start, start + BLK)
        grown = dot_nn(ctx_ref[here], wo_ref[...])

        @pl.when(quad == 0)
        def _():
            res_ref[here] = grown + x_ref[here].astype(F32) + bo_ref[...]

        @pl.when(quad > 0)
        def _():
            res_ref[here] += grown


KCH = 256


def attend(tokens, seg_col, seg_pad, w_qkv, b_qkv, taps, w_out, b_out, length):
    count, width = tokens.shape
    seqs = count // length
    quads = width // QUAD
    heads = width // HEAD
    per = QUAD // HEAD
    blocks = length // BLK
    own = pl.BlockSpec((length, QUAD), lambda r, p: (r, p))
    act = jax.ShapeDtypeStruct((count, width), BF16)
    big = jax.ShapeDtypeStruct((seqs, heads, length, length), BF16)
    big_spec = pl.BlockSpec((1, per, length, length), lambda r, p: (r, p, 0, 0))

    def part(rows_of, k):
        return pl.BlockSpec((rows_of, QUAD), lambda r, p, k=k: (0, p + k * quads))

    return pl.pallas_call(
        attend_kernel,
        grid=(seqs, quads),
        in_specs=[
            pl.BlockSpec((length, width), lambda r, p: (r, 0)),
            pl.BlockSpec((length, 1), lambda r, p: (r, 0)),
            pl.BlockSpec((1, 1, length + 2 * HALO), lambda r, p: (r, 0, 0)),
            part(width, 0), part(width, 1), part(width, 2),
            part(1, 0), part(1, 1), part(1, 2),
            pl.BlockSpec((1, per, 2 * BLK), lambda r, p: (p, 0, 0)),
            pl.BlockSpec((QUAD, width), lambda r, p: (p, 0)),
            pl.BlockSpec((1, width), lambda r, p: (0, 0)),
        ],
        out_specs=[own] * 5 + [big_spec] * 2 + [own] * 3 + [pl.BlockSpec((length, width), lambda r, p: (r, 0))],
        out_shape=[act] * 5 + [big] * 2 + [act] * 3 + [jax.ShapeDtypeStruct((count, width), F32)],
        scratch_shapes=[
            pltpu.VMEM((length, length), BF16),
            pltpu.VMEM((blocks, BLK, 2 * BLK), BF16),
            pltpu.VMEM((2, length + 2 * HALO, 2 * PAIR), BF16),
        ],
        compiler_params=pltpu.CompilerParams(vmem_limit_bytes=56 * 2**20),
        name="attend_forward",
    )(tokens, seg_col, seg_pad, w_qkv, w_qkv, w_qkv, b_qkv, b_qkv, b_qkv, taps, w_out, b_out)

GELU_A = math.sqrt(2.0 / math.pi)
GELU_B = 0.044715
TILE = 256


def gelu_terms(pre):
    square = pre * pre
    swing = jnp.tanh(pre * (GELU_A + GELU_A * GELU_B * square))
    gate = 0.5 + 0.5 * swing
    steep = GELU_A + 3.0 * GELU_A * GELU_B * square
    return pre * gate, gate + 0.5 * pre * (1.0 - swing * swing) * steep


def norm_backward(grad_out, unit, scaling, gain):
    grad_unit = grad_out * gain
    return scaling * (
        grad_unit
        - jnp.mean(grad_unit, -1, keepdims=True)
        - unit * jnp.mean(grad_unit * unit, -1, keepdims=True)
    )


def column_sum(values):
    return jnp.sum(values, 0, keepdims=True)


def ffn_kernel(
    res_ref, cot_ref, ctx_ref, wo_ref, gain1_ref, shift1_ref, gain2_ref, shift2_ref, bd_ref, bu_ref, wu_ref, wd_ref,
    out_ref, dproj_ref, dctx_ref, gwo_ref, gu_ref, gd_ref, gbu_ref, gbd_ref, gg2_ref, gs2_ref, gg1_ref, gs1_ref, gbo_ref,
    low_ref, acc_ref, hid_ref, slope_ref, dffn_ref, dpre_ref,
):
    parts = pl.num_programs(0) // 2
    step = pl.program_id(0)
    count, width = res_ref.shape
    tiles = count // TILE
    f = lax.rem(step, parts)

    def at(t):
        return pl.ds(pl.multiple_of(t * TILE, TILE), TILE)

    @pl.when(step == 0)
    def _():
        def one(t, carry):
            unit, _ = norm_stats(res_ref[at(t)])
            low_ref[at(t)] = (unit * gain1_ref[...] + shift1_ref[...]).astype(BF16)
            return carry

        lax.fori_loop(0, tiles, one, 0)

    @pl.when(step < parts)
    def _():
        def one(t, carry):
            pre = dot_nn(low_ref[at(t)], wu_ref[0]) + bu_ref[0].astype(F32)
            hidden, slope = gelu_terms(pre)
            hidden = hidden.astype(BF16)
            hid_ref[f, at(t)] = hidden
            slope_ref[f, at(t)] = slope.astype(BF16)
            grown = dot_nn(hidden, wd_ref[0])

            @pl.when(step == 0)
            def _():
                acc_ref[at(t)] = grown

            @pl.when(step > 0)
            def _():
                acc_ref[at(t)] += grown

            return carry

        lax.fori_loop(0, tiles, one, 0)

    @pl.when(step == parts)
    def _():
        def one(t, sums):
            unit, _ = norm_stats(res_ref[at(t)])
            first = unit * gain1_ref[...] + shift1_ref[...]
            unit, scaling = norm_stats(first + acc_ref[at(t)] + bd_ref[...])
            out_ref[at(t)] = (unit * gain2_ref[...] + shift2_ref[...]).astype(BF16)
            grad = cot_ref[at(t)].astype(F32)
            d_res = norm_backward(grad, unit, scaling, gain2_ref[...])
            d_ffn = d_res.astype(BF16)
            acc_ref[at(t)] = d_res
            dffn_ref[at(t)] = d_ffn
            return (
                sums[0] + column_sum(grad * unit),
                sums[1] + column_sum(grad),
                sums[2] + column_sum(d_ffn.astype(F32)),
            )

        zero = jnp.zeros((1, width), F32)
        gg2_ref[...], gs2_ref[...], gbd_ref[...] = lax.fori_loop(0, tiles, one, (zero, zero, zero))

    @pl.when(step >= parts)
    def _():
        def one(t, total):
            d_hidden = dot_nt(dffn_ref[at(t)], wd_ref[0])
            d_pre = (d_hidden * slope_ref[f, at(t)].astype(F32)).astype(BF16)
            dpre_ref[at(t)] = d_pre
            acc_ref[at(t)] += dot_nt(d_pre, wu_ref[0])
            return total + column_sum(d_pre.astype(F32))

        share = dpre_ref.shape[1]
        gbu_ref[0] = lax.fori_loop(0, tiles, one, jnp.zeros((1, share), F32))
        for start in range(0, width, TILE):
            cut = slice(start, start + TILE)
            gu_ref[0, cut] = dot_tn(low_ref[:, cut], dpre_ref[...]).astype(BF16)
        piece = min(TILE, share)
        for start in range(0, share, piece):
            cut = slice(start, start + piece)
            gd_ref[0, cut] = dot_tn(hid_ref[f, :, cut], dffn_ref[...]).astype(BF16)

    @pl.when(step == 2 * parts - 1)
    def _():
        def one(t, sums):
            unit, scaling = norm_stats(res_ref[at(t)])
            grad = acc_ref[at(t)]
            d_proj = norm_backward(grad, unit, scaling, gain1_ref[...]).astype(BF16)
            dproj_ref[at(t)] = d_proj
            dctx_ref[at(t)] = dot_nt(d_proj, wo_ref[...]).astype(BF16)
            return (
                sums[0] + column_sum(grad * unit),
                sums[1] + column_sum(grad),
                sums[2] + column_sum(d_proj.astype(F32)),
            )

        zero = jnp.zeros((1, width), F32)
        gg1_ref[...], gs1_ref[...], gbo_ref[...] = lax.fori_loop(0, tiles, one, (zero, zero, zero))
        for start in range(0, width, TILE):
            cut = slice(start, start + TILE)
            gwo_ref[cut] = dot_tn(ctx_ref[:, cut], dproj_ref[...]).astype(BF16)


def feed_forward(res, cot, ctx, w_out, gain1, shift1, gain2, shift2, b_down, b_up, w_up, w_down):
    count, width = res.shape
    parts, _, share = w_up.shape

    def whole(*shape):
        return pl.BlockSpec(shape, lambda s: (0,) * len(shape), pipeline_mode=pl.Buffered(1))

    def per_part(*shape):
        return pl.BlockSpec((1,) + shape, lambda s: (lax.rem(s, parts),) + (0,) * len(shape))

    def late_part(*shape):
        return pl.BlockSpec((1,) + shape, lambda s: (jnp.maximum(s - parts, 0),) + (0,) * len(shape))

    act = jax.ShapeDtypeStruct((count, width), BF16)
    row = jax.ShapeDtypeStruct((1, width), F32)
    return pl.pallas_call(
        ffn_kernel,
        grid=(2 * parts,),
        in_specs=[whole(count, width)] * 3
        + [whole(width, width)]
        + [whole(1, width)] * 5
        + [per_part(1, share), per_part(width, share), per_part(share, width)],
        out_specs=[whole(count, width)] * 3
        + [whole(width, width), late_part(width, share), late_part(share, width), late_part(1, share)]
        + [whole(1, width)] * 6,
        out_shape=[act] * 3
        + [
            jax.ShapeDtypeStruct((width, width), BF16),
            jax.ShapeDtypeStruct((parts, width, share), BF16),
            jax.ShapeDtypeStruct((parts, share, width), BF16),
            jax.ShapeDtypeStruct((parts, 1, share), F32),
        ]
        + [row] * 6,
        scratch_shapes=[
            pltpu.VMEM((count, width), BF16),
            pltpu.VMEM((count, width), F32),
            pltpu.VMEM((parts, count, share), BF16),
            pltpu.VMEM((parts, count, share), BF16),
            pltpu.VMEM((count, width), BF16),
            pltpu.VMEM((count, share), BF16),
        ],
        compiler_params=pltpu.CompilerParams(vmem_limit_bytes=60 * 2**20),
        name="feed_forward",
    )(res, cot, ctx, w_out, gain1, shift1, gain2, shift2, b_down, b_up, w_up, w_down)


def attend_back_kernel(
    dctx_ref, att_ref, inv_ref, q_ref, k_ref, v_ref, sq_ref, sk_ref, w_ref, s_ref, x_ref, col_ref, pad_ref,
    wq_ref, wk_ref, wv_ref, tap_ref, flip_ref, dproj_ref,
    gw_ref, gb_ref, gconv_ref, gt_ref,
    near_ref, vv_ref, dpad_ref, dcos_ref, dq_ref, dk_ref, dv_ref, joined_ref, gwacc_ref, gtacc_ref, conv_ref,
):
    quad, row = pl.program_id(0), pl.program_id(1)
    quads, seqs = pl.num_programs(0), pl.num_programs(1)
    length = x_ref.shape[0]
    blocks = length // BLK
    inside = slice(HALO, HALO + length)

    build_near(col_ref[...], pad_ref[0], near_ref)
    for half in range(2):
        edge = jnp.zeros((HALO, PAIR), BF16)
        for ref in (vv_ref, dpad_ref):
            ref[half, :HALO, :PAIR] = edge
            ref[half, HALO + length :, :PAIR] = edge
        vv_ref[half, inside, PAIR:] = head_mask(half, (length, PAIR))

    @pl.when(row == 0)
    def _():
        conv_ref[...] = jnp.zeros_like(conv_ref)
        gwacc_ref[...] = jnp.zeros_like(gwacc_ref)
        gb_ref[...] = jnp.zeros_like(gb_ref)

    def one_pair(pair, carry):
        at = pl.ds(pl.multiple_of(pair * PAIR, PAIR), PAIR)
        inverse = inv_ref[:, at].astype(F32)
        d_ctx = dctx_ref[:, at]
        d_summed = (d_ctx.astype(F32) * inverse).astype(BF16)
        d_total = (-d_summed.astype(F32) * att_ref[:, at].astype(F32)).astype(BF16)
        both = jnp.concatenate([d_summed, d_total], 1)
        dk = jnp.zeros((length, PAIR), F32)
        dv = jnp.zeros((length, PAIR), F32)
        for half in range(2):
            head = pair * 2 + half
            mask = head_mask(half, (length, PAIR))
            vv_ref[half, inside, :PAIR] = v_ref[:, at] * mask
            dpad_ref[half, inside] = d_ctx * mask
            k_half = k_ref[:, at] * mask
            for block in range(blocks):
                here = slice(block * BLK, block * BLK + BLK)
                low, high = window_of(block, blocks)
                d_weight = dot_nt(both[here], vv_ref[half, HALO + low : HALO + high])
                d_cos = d_weight.astype(BF16) * s_ref[0, head, here, low:high]
                dcos_ref[here, low:high] = d_cos
                if low > 0:
                    dcos_ref[here, :low] = jnp.zeros((BLK, low), BF16)
                if high < length:
                    dcos_ref[here, high:] = jnp.zeros((BLK, length - high), BF16)
                grown = dot_nn(d_cos, k_half[low:high])
                if half == 0:
                    dq_ref[here] = grown
                else:
                    dq_ref[here] += grown
                window = slice(block * BLK, block * BLK + 2 * BLK)
                near = near_ref[block]
                taps = band(flip_ref[0, pl.ds(head, 1)], BLK).astype(BF16) * near
                grown = dot_nn(taps, dpad_ref[half, window])
                if half == 0:
                    dv_ref[here] = grown
                else:
                    dv_ref[here] += grown
                conv_ref[head] += near.astype(F32) * dot_nt(d_ctx[here], vv_ref[half, window, :PAIR])
            dk += dot_tn(dcos_ref[...], q_ref[:, at] * mask)
            dv += dot_tn(w_ref[0, head], d_summed * mask)
        dv_ref[...] += dv
        grad = SLOPE * dq_ref[...]
        unit = q_ref[:, at].astype(F32)
        d_query = sq_ref[:, at].astype(F32) * (SHRINK * grad - unit * (head_sum(grad * unit) / SHRINK))
        grad = SLOPE * dk
        unit = k_ref[:, at].astype(F32)
        d_key = sk_ref[:, at].astype(F32) * (grad - unit * head_sum(grad * unit))
        for part, values in enumerate((d_query, d_key, dv_ref[...])):
            joined_ref[:, pl.ds(pl.multiple_of(part * QUAD + pair * PAIR, PAIR), PAIR)] = values.astype(BF16)
        return carry

    lax.fori_loop(0, QUAD // PAIR, one_pair, 0)

    gb_ref[0] += column_sum(joined_ref[...].astype(F32))
    for start in range(0, gwacc_ref.shape[0], TILE):
        cut = slice(start, start + TILE)
        gwacc_ref[cut] += dot_tn(x_ref[:, cut], joined_ref[...])
    for start in range(0, length, TILE):
        here = pl.ds(pl.multiple_of(row * length + start, TILE), TILE)
        cut = slice(start, start + TILE)
        grown = (
            dot_nt(joined_ref[cut, :QUAD], wq_ref[...])
            + dot_nt(joined_ref[cut, QUAD : 2 * QUAD], wk_ref[...])
            + dot_nt(joined_ref[cut, 2 * QUAD :], wv_ref[...])
        )

        @pl.when(quad == 0)
        def _():
            gtacc_ref[here] = grown + dproj_ref[cut].astype(F32)

        @pl.when(quad > 0)
        def _():
            gtacc_ref[here] += grown

    @pl.when(quad == quads - 1)
    def _():
        gt_ref[...] = gtacc_ref[pl.ds(pl.multiple_of(row * length, TILE), length)].astype(BF16)

    @pl.when(row == seqs - 1)
    def _():
        gw_ref[0] = gwacc_ref[...].astype(BF16)
        for head in range(QUAD // HEAD):
            sums = conv_ref[head]
            high = sums.astype(BF16)
            turn = (rows((BLK, BLK)) + lanes((BLK, BLK)) == BLK - 1).astype(BF16)
            turned = dot_nn(turn, high) + dot_nn(turn, (sums - high.astype(F32)).astype(BF16))
            turned = pltpu.roll(turned, 0, 1, stride=1, stride_axis=0)
            gconv_ref[0, head : head + 1] = column_sum(turned)


def attend_back(dctx, att, inv, q, k, v, sq, sk, weight, slope, tokens, seg_col, seg_pad, w_qkv, taps, flipped, dproj, length):
    count, width = tokens.shape
    seqs = count // length
    quads = width // QUAD
    per = QUAD // HEAD
    blocks = length // BLK
    own = pl.BlockSpec((length, QUAD), lambda p, r: (r, p))
    big = pl.BlockSpec((1, per, length, length), lambda p, r: (r, p, 0, 0))
    wide = pl.BlockSpec((length, width), lambda p, r: (r, 0))

    def part(k):
        return pl.BlockSpec((width, QUAD), lambda p, r, k=k: (0, p + k * quads))

    taps_spec = pl.BlockSpec((1, per, 2 * BLK), lambda p, r: (p, 0, 0))
    return pl.pallas_call(
        attend_back_kernel,
        grid=(quads, seqs),
        in_specs=[own] * 8
        + [big] * 2
        + [
            wide,
            pl.BlockSpec((length, 1), lambda p, r: (r, 0)),
            pl.BlockSpec((1, 1, length + 2 * HALO), lambda p, r: (r, 0, 0)),
            part(0), part(1), part(2),
            taps_spec, taps_spec,
            wide,
        ],
        out_specs=[
            pl.BlockSpec((1, width, 3 * QUAD), lambda p, r: (p, 0, 0)),
            pl.BlockSpec((1, 1, 3 * QUAD), lambda p, r: (p, 0, 0)),
            pl.BlockSpec((1, per, 2 * BLK), lambda p, r: (p, 0, 0)),
            pl.BlockSpec((length, width), lambda p, r: (jnp.where(p == quads - 1, r, 0), 0)),
        ],
        out_shape=[
            jax.ShapeDtypeStruct((quads, width, 3 * QUAD), BF16),
            jax.ShapeDtypeStruct((quads, 1, 3 * QUAD), F32),
            jax.ShapeDtypeStruct((quads, per, 2 * BLK), F32),
            jax.ShapeDtypeStruct((count, width), BF16),
        ],
        scratch_shapes=[
            pltpu.VMEM((blocks, BLK, 2 * BLK), BF16),
            pltpu.VMEM((2, length + 2 * HALO, 2 * PAIR), BF16),
            pltpu.VMEM((2, length + 2 * HALO, PAIR), BF16),
            pltpu.VMEM((length, length), BF16),
            pltpu.VMEM((length, PAIR), F32),
            pltpu.VMEM((length, PAIR), F32),
            pltpu.VMEM((length, PAIR), F32),
            pltpu.VMEM((length, 3 * QUAD), BF16),
            pltpu.VMEM((width, 3 * QUAD), F32),
            pltpu.VMEM((count, width), F32),
            pltpu.VMEM((per, BLK, 2 * BLK), F32),
        ],
        compiler_params=pltpu.CompilerParams(vmem_limit_bytes=60 * 2**20),
        name="attend_backward",
    )(dctx, att, inv, q, k, v, sq, sk, weight, slope, tokens, seg_col, seg_pad, w_qkv, w_qkv, w_qkv, taps, flipped, dproj)


def body(
    tokens, segment_ids, w_qkv, b_qkv, conv_kernel, w_out, b_out, norm1_gain, norm1_bias,
    w_up, b_up, w_down, b_down, norm2_gain, norm2_bias, cotangent,
):
    seqs, length = segment_ids.shape
    width = tokens.shape[1]
    heads, span = conv_kernel.shape
    per = QUAD // HEAD
    radius = span // 2
    first_tap = HALO - radius

    def spread(kernel):
        padded = jnp.pad(kernel, ((0, 0), (first_tap, 2 * BLK - first_tap - span)))
        return padded.reshape(heads // per, per, 2 * BLK)

    seg_col = segment_ids.reshape(-1, 1)
    seg_pad = jnp.pad(segment_ids, ((0, 0), (HALO, HALO)), constant_values=-1)[:, None, :]
    taps, flipped = spread(conv_kernel), spread(conv_kernel[:, ::-1])

    up_all = lax.all_gather(w_up, "tensor")
    down_all = lax.all_gather(w_down, "tensor")
    bias_all = lax.all_gather(b_up, "tensor")[:, None, :]

    q, k, v, sq, sk, weight, slope, att, inv, ctx, res = attend(
        tokens, seg_col, seg_pad, w_qkv, b_qkv[None], taps, w_out, b_out[None], length
    )
    out, dproj, dctx, gwo, gu, gd, gbu, gbd, gg2, gs2, gg1, gs1, gbo = feed_forward(
        res, cotangent, ctx, w_out, norm1_gain[None], norm1_bias[None], norm2_gain[None], norm2_bias[None],
        b_down[None], bias_all, up_all, down_all,
    )
    gw, gb, gconv, gt = attend_back(
        dctx, att, inv, q, k, v, sq, sk, weight, slope, tokens, seg_col, seg_pad, w_qkv, taps, flipped, dproj, length
    )
    grad_up = lax.psum(lax.psum_scatter(gu, "tensor"), "dp").astype(F32)
    grad_down = lax.psum(lax.psum_scatter(gd, "tensor"), "dp").astype(F32)
    first_lane = first_tap + BLK - 1
    grad_conv = gconv.reshape(heads, 2 * BLK)[:, first_lane : first_lane + span]
    gw, gwo = lax.psum((gw, gwo), ("dp", "tensor"))
    gb, grad_conv, gbo, gg1, gs1, gbd, gg2, gs2, gbu = lax.psum(
        (gb, grad_conv, gbo, gg1, gs1, gbd, gg2, gs2, gbu), ("dp", "tensor")
    )
    quads = gw.shape[0]
    gw = gw.reshape(quads, width, 3, QUAD).transpose(1, 2, 0, 3).reshape(width, 3 * width).astype(F32)
    gb = gb.reshape(quads, 3, QUAD).transpose(1, 0, 2).reshape(3 * width)
    grad_b_up = lax.dynamic_index_in_dim(gbu, lax.axis_index("tensor"), 0, False)[0]
    return (
        out, gt, gw, gb, grad_conv, gwo.astype(F32), gbo[0], gg1[0], gs1[0],
        grad_up, grad_b_up, grad_down, gbd[0], gg2[0], gs2[0],
    )


def solution(mesh):
    placed = (
        P(("dp", "tensor"), None),
        P(("dp", "tensor"), None),
        P(), P(), P(), P(), P(), P(), P(),
        P(None, "tensor"),
        P("tensor"),
        P("tensor", None),
        P(), P(), P(),
        P(("dp", "tensor"), None),
    )
    return jax.shard_map(
        body,
        mesh=mesh,
        in_specs=placed,
        out_specs=(
            P(("dp", "tensor"), None),
            P(("dp", "tensor"), None),
            P(), P(), P(), P(), P(), P(), P(),
            P(None, "tensor"),
            P("tensor"),
            P("tensor", None),
            P(), P(), P(),
        ),
        check_vma=False,
    )
```

time: 1090 us -> 526 us (0.48)
  matrix products: 299 us -> 0 us
  other arithmetic: 228 us -> 6.22 us
  Pallas kernels: 0 us -> 175 us
  local copies, waits for them, and re-layouts: 174 us -> 20.8 us
  waiting for transfers between devices: 288 us -> 260 us
  loops' own time: 18.3 us -> 0 us
  blocking collectives: 61.2 us -> 48.7 us
    dot_general x26 -> x0, matrix products: 299 us -> none  [the longest x2 65.5 us: attend_back(): jnp.einsum('qhd,khd->hqk', grad_sum, v_rows, preferred_element_type=jnp.f...]
    psum x2, waiting for transfers between devices: 35.5 us -> 212 us  [the longest x1 108 us: body(): gw, gwo = lax.psum((gw, gwo), ('dp', 'tensor'))]
    pallas_call x0 -> x3, Pallas kernels: none -> 175 us  [the longest x1 63.8 us: feed_forward(): pl.pallas_call(ffn_kernel, grid=(2 * parts,), in_specs=[whole(count, widt...]
    reduce_scatter x2, waiting for transfers between devices: 158 us -> 35.7 us  [the longest x1 35.7 us: body(): grad_down = lax.psum(lax.psum_scatter(gd, 'tensor'), 'dp').astype(F32)]
    all_gather x2, waiting for transfers between devices: 94.4 us -> 9.78 us  [the longest x1 9.78 us: body(): down_all = lax.all_gather(w_down, 'tensor')]
    reduce_sum x14 -> x0, other arithmetic: 79.9 us -> none  [the longest x5 54 us: conv_backward(): kernel_cols.append(jnp.sum(shifted * grad_ctx, axis=(0, 1, 3)))]
    convert_element_type x8 -> x3, other arithmetic: 71.4 us -> 6.09 us  [the longest x1 2.94 us: body(): grad_up = lax.psum(lax.psum_scatter(gu, 'tensor'), 'dp').astype(F32)]
    another operation x1 -> x0, other arithmetic: 60.2 us -> none  [body(): jnp.stack((d_queries, d_keys, d_v_attend + d_v_conv), 2)]
  transfers between devices with their start and end apart: 6 -> 6, of which waited for: 5 -> 4; matrix products, arithmetic and copies ran while one was open for 39% -> 4% of each run, Pallas kernels for 0% -> 21%
where the time goes in v1:
time: 526 us; the launch traced here: 525 us
  waiting for transfers between devices  260 us (49%)
  Pallas kernels  175 us (33%)
  blocking collectives  48.7 us (9%)
  local copies, waits for them, and re-layouts  20.8 us (4%)
  between operations  14.4 us (3%)
  other arithmetic  6.22 us (1%)
    psum x1, waiting for transfers between devices, body(): gw, gwo = lax.psum((gw, gwo), ('dp', 'tensor'))  108 us
    psum x1, waiting for transfers between devices, body(): grad_up = lax.psum(lax.psum_scatter(gu, 'tensor'), 'dp').astype(F32)  104 us
    pallas_call x1, Pallas kernels, feed_forward(): pl.pallas_call(ffn_kernel, grid=(2 * parts,), in_specs=[whole(count, widt...  63.8 us
    pallas_call x1, Pallas kernels, attend(): pl.pallas_call(attend_kernel, grid=(seqs, quads), in_specs=[pl.BlockSpec(...  56.9 us
    pallas_call x1, Pallas kernels, attend_back(): pl.pallas_call(attend_back_kernel, grid=(quads, seqs), in_specs=[own] * 8...  54.3 us
    psum x1, blocking collectives, body(): lax.psum((gb, grad_conv, gbo, gg1, gs1, gbd, gg2, gs2, gbu), ('dp', 'tens...  41.7 us
    reduce_scatter x1, waiting for transfers between devices, body(): grad_down = lax.psum(lax.psum_scatter(gd, 'tensor'), 'dp').astype(F32)  35.7 us
  transfers between devices with their start and end apart: 6, of which 4 were waited for; matrix products, arithmetic and copies ran while one was open for 4% of the time, Pallas kernels for 21%

profile of v1, /device:TPU:0, one launch (start us, length us, event | category | flops | bytes accessed | tf_op | source)
XLA Modules:
  0.0 525.4 jit_solution(16744570081353063717)
XLA Ops:
  7.3 0.7 all-gather.7.cloned.1.call-update
  8.1 0.7 all-gather.9.cloned.1.call-update
  8.8 1.0 copy.45
  9.9 0.6 reshape.56.tap_ref
  10.6 0.6 broadcast_in_dim.27.pad_ref
  11.2 0.6 broadcast_in_dim.28.bq_ref.bk_ref.bv_ref
  11.8 0.6 broadcast_in_dim.29.bo_ref
  12.4 0.6 broadcast_in_dim.30.gain1_ref
  13.0 0.6 broadcast_in_dim.31.shift1_ref
  13.6 0.6 broadcast_in_dim.32.gain2_ref
  14.2 0.6 broadcast_in_dim.33.shift2_ref
  14.8 0.6 broadcast_in_dim.34.bd_ref
  15.4 56.9 %attend_forward.1 = (bf16[1024,768]{1,0:T(8,128)(2,1)}, bf16[1024,768]{1,0:T(8,128)(2,1)}, bf16[1024,768]{1,0:T(8,128)(2,1)}, bf16[1024,768]{1,0:T(8,128)(2,1)},...) custom-call(bf16[1024,768]{1,0:T(8,128)(2,1)} %x_ref.3, ...), custom_call_target="tpu_custom_call" | custom-call | tf_op jit(solution)/shard_map/attend_forward/pallas_call | solution.py:211
  72.3 6.9 %all-gather.3.bu_ref = bf16[4,1,768]{2,1,0:T(2,128)(2,1)} all-gather(bf16[1,1,768]{2,1,0:T(2,128)(2,1)S(1)} %reshape.65), channel_id=2, replica_groups=mesh['dp'=8,'tensor'=4] {'tensor'}, dimensions={0}, use_global_device_ids=true | all-gather | bytes 7680 | tf_op jit(solution)/shard_map/all_gather | solution.py:608
  79.2 9.8 %all-gather.9.cloned.1.call-done = bf16[3072,768]{1,0:T(8,128)(2,1)} async-done(((bf16[768,768]{1,0:T(8,128)(2,1)}), bf16[3072,768]{1,0:T(8,128)(2,1)}) %all-gather.9.cloned.1.call-update) | async-done | bytes 4718608 | tf_op jit(solution)/shard_map/all_gather | solution.py:607
  89.0 63.8 %feed_forward.1 = (bf16[1024,768]{1,0:T(8,128)(2,1)}, bf16[1024,768]{1,0:T(8,128)(2,1)}, bf16[1024,768]{1,0:T(8,128)(2,1)}, bf16[768,768]{1,0:T(8,128)(2,1)}, bf...) custom-call(f32[1024,768]{1,0:T(8,128)} %get-tuple-element.43.res_re, ...), custom_call_target="tpu_custom_call" | custom-call | tf_op jit(solution)/shard_map/feed_forward/pallas_call | solution.py:382
  152.9 0.5 reduce-scatter.5.cloned.1.call-update
  153.4 0.3 all-reduce.9.cloned.1.call-start
  153.7 0.1 pad.13
  153.8 0.6 reshape.57.flip_ref
  154.4 54.3 %attend_backward.1 = (bf16[3,768,768]{2,1,0:T(8,128)(2,1)}, f32[3,1,768]{2,1,0:T(1,128)}, f32[3,4,256]{2,1,0:T(4,128)}, bf16[1024,768]{1,0:T(8,128)(2,1)}) custom-call(bf16[1024,768]{1,0:T(8,128)(2,1)} %get-tuple-element.46.dctx_ref, bf16[1024,768]{1,0:T(8,128)(2,1)} %get-tuple-element.47.att_ref, bf16[1024,768]{1,0:T(8,128)(2,1)} %get-tuple-element.48.inv_ref, ...), custom_call_target="tpu_custom_call" | custom-call | tf_op jit(solution)/shard_map/attend_backward/pallas_call | solution.py:544
  208.7 4.6 copy.40
  213.3 2.1 copy.41
  215.6 35.7 %reduce-scatter.5.cloned.1.call-done = bf16[1,768,768]{2,1,0:T(8,128)(2,1)} async-done(((bf16[4,768,768]{2,1,0:T(8,128)(2,1)}), bf16[1,768,768]{2,1,0:T(8,128)(2,1)}) %reduce-scatter.5.cloned.1.call-update) | async-done | bytes 1179664 | tf_op jit(solution)/shard_map/reduce_scatter | solution.py:621
  251.7 41.7 %all-reduce.3 = (f32[2304]{0:T(1024)}, f32[12,35]{1,0:T(8,128)}, f32[768]{0:T(1024)}, f32[768]{0:T(1024)}, f32[768]{0:T(1024)}, /*index=5*/f32[4,1,768]{2,1,0:T(...) all-reduce(f32[2304]{0:T(1024)S(1)} %reshape.59, ...), channel_id=1, replica_groups=mesh['dp'=8,'tensor'=4] {'dp','tensor'}, use_global_device_ids=true, to_apply=%region_1.2 | all-reduce | flops 10404 | bytes 83232 | tf_op jit(solution)/shard_map/psum | solution.py:625
  293.4 0.6 dynamic-slice_reduce_fusion
  294.0 108.2 %all-reduce.9.cloned.1.call-done = (bf16[768,2304]{0,1:T(8,128)(2,1)}, bf16[768,768]{1,0:T(8,128)(2,1)}) async-done(((bf16[768,2304]{0,1:T(8,128)(2,1)}, bf16[768,768]{1,0:T(8,128)(2,1)}), (bf16[768,2304]{0,1:T(8,128)(2,1)}, bf16[768,768]{1,0:T(8,128)(2,1)})) %all-reduce.9.cloned.1.call-update) | async-done | bytes 4718608 | tf_op jit(solution)/shard_map/psum | solution.py:624
  402.2 6.0 %copy.43 = f32[768,2304]{1,0:T(8,128)} copy(bf16[768,2304]{0,1:T(8,128)(2,1)} %get-tuple-element.110) | data formatting | bytes 10616832
  408.2 1.6 convert_element_type.28
  409.8 104.2 %all-reduce.11.cloned.1.call-done = (bf16[768,768]{1,0:T(8,128)(2,1)}, bf16[768,768]{1,0:T(8,128)(2,1)}) async-done(((bf16[768,768]{1,0:T(8,128)(2,1)}, bf16[768,768]{1,0:T(8,128)(2,1)}), (bf16[768,768]{1,0:T(8,128)(2,1)}, bf16[768,768]{1,0:T(8,128)(2,1)})) %all-reduce.11.cloned.1.call-update) | async-done | bytes 2359312 | tf_op jit(solution)/shard_map/psum | solution.py:620
  514.0 2.9 convert_element_type.29
  517.0 1.6 convert_element_type.30
  (67 shorter events, 0.8 us)
Async XLA Ops:
  7.2 1.6 copy-start.3
  7.2 2.7 copy-start.2
  7.2 4.0 copy-start.6
  7.2 4.6 copy-start.8
  7.2 5.2 copy-start.20
  7.2 5.2 copy-start.9
  7.2 5.8 %copy-start.10 = (f32[768]{0:T(1024)S(1)}, f32[768]{0:T(1024)}, u32[]{:S(2)}) copy-start(f32[768]{0:T(1024)} %param.24) | copy-start | bytes 9220
  7.3 6.4 %copy-start.11 = (f32[768]{0:T(1024)S(1)}, f32[768]{0:T(1024)}, u32[]{:S(2)}) copy-start(f32[768]{0:T(1024)} %param.29) | copy-start | bytes 9220
  7.3 6.9 %copy-start.12 = (f32[768]{0:T(1024)S(1)}, f32[768]{0:T(1024)}, u32[]{:S(2)}) copy-start(f32[768]{0:T(1024)} %param.30) | copy-start | bytes 9220
  7.3 7.5 %copy-start.13 = (f32[768]{0:T(1024)S(1)}, f32[768]{0:T(1024)}, u32[]{:S(2)}) copy-start(f32[768]{0:T(1024)} %param.28) | copy-start | bytes 9220
  7.3 71.9 %all-gather.7.cloned.1.call-start = ((), (), s32[]{:S(2)}) async-start(), calls=%async_computation.4 | async-start | bytes 5898240 | tf_op jit(solution)/shard_map/all_gather | solution.py:606
  8.0 81.0 %all-gather.9.cloned.1.call-start = ((), (), s32[]{:S(2)}) async-start(), calls=%async_computation.5 | async-start | bytes 5898240 | tf_op jit(solution)/shard_map/all_gather | solution.py:607
  8.8 206.8 %reduce-scatter.3.cloned.1.call-start = ((), (), s32[]{:S(2)}) async-start(), calls=%async_computation.2 | async-start | bytes 5898240 | tf_op jit(solution)/shard_map/reduce_scatter | solution.py:620
  152.8 98.5 %reduce-scatter.5.cloned.1.call-start = ((), (), s32[]{:S(2)}) async-start(), calls=%async_computation.3 | async-start | bytes 5898240 | tf_op jit(solution)/shard_map/reduce_scatter | solution.py:621
  153.4 248.8 %all-reduce.9.cloned.1.call-start = ((), (), s32[]{:S(2)}) async-start(), calls=%async_computation.6 | async-start | bytes 9437184 | tf_op jit(solution)/shard_map/psum | solution.py:624
  215.4 35.9 %copy-start.7 = (f32[3,1,768]{2,1,0:T(1,128)S(1)}, f32[3,1,768]{2,1,0:T(1,128)}, u32[]{:S(2)}) copy-start(f32[3,1,768]{2,1,0:T(1,128)} %get-tuple-element.59) | copy-start | bytes 27652
  215.4 36.0 %copy-start.5 = (f32[3,4,256]{2,1,0:T(4,128)S(1)}, f32[3,4,256]{2,1,0:T(4,128)}, u32[]{:S(2)}) copy-start(f32[3,4,256]{2,1,0:T(4,128)} %get-tuple-element.60) | copy-start | bytes 36868
  215.4 36.0 %copy-start.19 = (f32[1,768]{1,0:T(1,128)S(1)}, f32[1,768]{1,0:T(1,128)}, u32[]{:S(2)}) copy-start(f32[1,768]{1,0:T(1,128)} %get-tuple-element.62) | copy-start | bytes 9220
  215.4 36.1 %copy-start.18 = (f32[1,768]{1,0:T(1,128)S(1)}, f32[1,768]{1,0:T(1,128)}, u32[]{:S(2)}) copy-start(f32[1,768]{1,0:T(1,128)} %get-tuple-element.63) | copy-start | bytes 9220
  215.5 36.1 %copy-start.17 = (f32[1,768]{1,0:T(1,128)S(1)}, f32[1,768]{1,0:T(1,128)}, u32[]{:S(2)}) copy-start(f32[1,768]{1,0:T(1,128)} %get-tuple-element.64) | copy-start | bytes 9220
  215.5 36.1 %copy-start.16 = (f32[1,768]{1,0:T(1,128)S(1)}, f32[1,768]{1,0:T(1,128)}, u32[]{:S(2)}) copy-start(f32[1,768]{1,0:T(1,128)} %get-tuple-element.68) | copy-start | bytes 9220
  215.5 36.1 %copy-start.15 = (f32[1,768]{1,0:T(1,128)S(1)}, f32[1,768]{1,0:T(1,128)}, u32[]{:S(2)}) copy-start(f32[1,768]{1,0:T(1,128)} %get-tuple-element.69) | copy-start | bytes 9220
  215.5 36.1 %copy-start.14 = (f32[1,768]{1,0:T(1,128)S(1)}, f32[1,768]{1,0:T(1,128)}, u32[]{:S(2)}) copy-start(f32[1,768]{1,0:T(1,128)} %get-tuple-element.70) | copy-start | bytes 9220
  215.5 36.2 %copy-start.4 = (f32[4,1,768]{2,1,0:T(1,128)S(1)}, f32[4,1,768]{2,1,0:T(1,128)}, u32[]{:S(2)}) copy-start(f32[4,1,768]{2,1,0:T(1,128)} %get-tuple-element.66) | copy-start | bytes 36868
  215.5 298.5 %all-reduce.11.cloned.1.call-start = ((), (), s32[]{:S(2)}) async-start(), calls=%async_computation.7 | async-start | bytes 4718592 | tf_op jit(solution)/shard_map/psum | solution.py:620
  402.2 6.0 %copy-start = (bf16[768,768]{1,0:T(8,128)(2,1)S(1)}, bf16[768,768]{1,0:T(8,128)(2,1)}, u32[]{:S(2)}) copy-start(bf16[768,768]{1,0:T(8,128)(2,1)} %get-tuple-element.111) | copy-start | bytes 3538948
  514.0 2.9 copy-start.1
Sparse Core Ops, SparseCore 0:
  9.7 40.1 all-gather.6
  51.5 37.4 all-gather.8
  152.9 47.8 reduce-scatter.2
  203.4 47.8 reduce-scatter.4
  257.0 145.1 all-reduce.8
  406.1 107.9 all-reduce.10

commit v2 on v1

--- a/solution.py
+++ b/solution.py
@@ -260,14 +260,45 @@
 
 def ffn_kernel(
     res_ref, cot_ref, ctx_ref, wo_ref, gain1_ref, shift1_ref, gain2_ref, shift2_ref, bd_ref, bu_ref, wu_ref, wd_ref,
-    out_ref, dproj_ref, dctx_ref, gwo_ref, gu_ref, gd_ref, gbu_ref, gbd_ref, gg2_ref, gs2_ref, gg1_ref, gs1_ref, gbo_ref,
-    low_ref, acc_ref, hid_ref, slope_ref, dffn_ref, dpre_ref,
+    out_ref, dproj_ref, dctx_ref, gwo_ref, pu_ref, pd_ref, small_ref,
+    low_ref, acc_ref, hid_ref, slope_ref, dffn_ref, dpre_ref, sendu_ref, sendd_ref, recvu_ref, recvd_ref,
+    send_sem, recv_sem,
 ):
     parts = pl.num_programs(0) // 2
     step = pl.program_id(0)
     count, width = res_ref.shape
+    share = dpre_ref.shape[1]
     tiles = count // TILE
-    f = lax.rem(step, parts)
+    f = part_order(step, parts)
+    late = jnp.maximum(step - parts, 0)
+    heights = parts // 2
+    slot = lax.rem(late, heights)
+    tensor = lax.axis_index("tensor")
+    mate = (lax.axis_index("dp"), tensor + 1 - 2 * lax.rem(tensor, 2))
+
+    def to_mate(which):
+        return (
+            pltpu.make_async_remote_copy(
+                src_ref=sendu_ref.at[which], dst_ref=recvu_ref.at[which],
+                send_sem=send_sem.at[0, which], recv_sem=recv_sem.at[0, which],
+                device_id=mate, device_id_type=pl.DeviceIdType.MESH,
+            ),
+            pltpu.make_async_remote_copy(
+                src_ref=sendd_ref.at[which], dst_ref=recvd_ref.at[which],
+                send_sem=send_sem.at[1, which], recv_sem=recv_sem.at[1, which],
+                device_id=mate, device_id_type=pl.DeviceIdType.MESH,
+            ),
+        )
+
+    @pl.when(step == 0)
+    def _():
+        barrier = pltpu.get_barrier_semaphore()
+        pl.semaphore_signal(barrier, inc=1, device_id=mate, device_id_type=pl.DeviceIdType.MESH)
+        pl.semaphore_wait(barrier, 1)
+
+    def put_row(row, values):
+        for i in range(values.shape[1] // PAIR):
+            small_ref[pl.ds(row + i, 1)] = values[:, i * PAIR : (i + 1) * PAIR]
 
     def at(t):
         return pl.ds(pl.multiple_of(t * TILE, TILE), TILE)
@@ -322,7 +353,10 @@
             )
 
         zero = jnp.zeros((1, width), F32)
-        gg2_ref[...], gs2_ref[...], gbd_ref[...] = lax.fori_loop(0, tiles, one, (zero, zero, zero))
+        sums = lax.fori_loop(0, tiles, one, (zero, zero, zero))
+        small_ref[...] = jnp.zeros_like(small_ref)
+        for i, values in enumerate(sums):
+            put_row(i * (width // PAIR), values)
 
     @pl.when(step >= parts)
     def _():
@@ -333,15 +367,42 @@
             acc_ref[at(t)] += dot_nt(d_pre, wu_ref[0])
             return total + column_sum(d_pre.astype(F32))
 
-        share = dpre_ref.shape[1]
-        gbu_ref[0] = lax.fori_loop(0, tiles, one, jnp.zeros((1, share), F32))
-        for start in range(0, width, TILE):
-            cut = slice(start, start + TILE)
-            gu_ref[0, cut] = dot_tn(low_ref[:, cut], dpre_ref[...]).astype(BF16)
-        piece = min(TILE, share)
-        for start in range(0, share, piece):
-            cut = slice(start, start + piece)
-            gd_ref[0, cut] = dot_tn(hid_ref[f, :, cut], dffn_ref[...]).astype(BF16)
+        bias = lax.fori_loop(0, tiles, one, jnp.zeros((1, share), F32))
+        put_row(6 * (width // PAIR) + f * (share // PAIR), bias)
+
+        def grads(store_up, store_down):
+            for start in range(0, width, TILE):
+                cut = slice(start, start + TILE)
+                store_up(cut, dot_tn(low_ref[:, cut], dpre_ref[...]))
+            piece = math.gcd(TILE, share)
+            for start in range(0, share, piece):
+                cut = slice(start, start + piece)
+                store_down(cut, dot_tn(hid_ref[f, :, cut], dffn_ref[...]))
+
+        @pl.when(late < heights)
+        def _():
+            def up(cut, values):
+                sendu_ref[slot, cut] = values.astype(BF16)
+
+            def down(cut, values):
+                sendd_ref[slot, cut] = values.astype(BF16)
+
+            grads(up, down)
+            for copy in to_mate(slot):
+                copy.start()
+
+        @pl.when(late >= heights)
+        def _():
+            for copy in to_mate(slot):
+                copy.wait()
+
+            def up(cut, values):
+                pu_ref[slot, cut] = (values + recvu_ref[slot, cut].astype(F32)).astype(BF16)
+
+            def down(cut, values):
+                pd_ref[slot, cut] = (values + recvd_ref[slot, cut].astype(F32)).astype(BF16)
+
+            grads(up, down)
 
     @pl.when(step == 2 * parts - 1)
     def _():
@@ -358,27 +419,39 @@
             )
 
         zero = jnp.zeros((1, width), F32)
-        gg1_ref[...], gs1_ref[...], gbo_ref[...] = lax.fori_loop(0, tiles, one, (zero, zero, zero))
+        sums = lax.fori_loop(0, tiles, one, (zero, zero, zero))
+        for i, values in enumerate(sums):
+            put_row((3 + i) * (width // PAIR), values)
         for start in range(0, width, TILE):
-            cut = slice(start, start + TILE)
-            gwo_ref[cut] = dot_tn(ctx_ref[:, cut], dproj_ref[...]).astype(BF16)
+            values = dot_tn(ctx_ref[:, start : start + TILE], dproj_ref[...]).astype(BF16)
+            gwo_ref[start : start + TILE] = values[:, : width // 2]
+            gwo_ref[width + start : width + start + TILE] = values[:, width // 2 :]
+
+
+def part_order(step, parts):
+    tensor = lax.axis_index("tensor")
+    height, core = tensor // 2, lax.rem(tensor, 2)
+    heights = parts // 2
+    late = jnp.maximum(step - parts, 0)
+    there = lax.rem(height + 1 + lax.rem(late, heights), heights)
+    whose = jnp.where(late < heights, 1 - core, core)
+    return jnp.where(step < parts, step, there * 2 + whose)
 
 
 def feed_forward(res, cot, ctx, w_out, gain1, shift1, gain2, shift2, b_down, b_up, w_up, w_down):
     count, width = res.shape
     parts, _, share = w_up.shape
+    heights = parts // 2
+    smalls = 6 * width // PAIR + parts * share // PAIR
+    smalls = -(-smalls // 8) * 8
 
     def whole(*shape):
         return pl.BlockSpec(shape, lambda s: (0,) * len(shape), pipeline_mode=pl.Buffered(1))
 
     def per_part(*shape):
-        return pl.BlockSpec((1,) + shape, lambda s: (lax.rem(s, parts),) + (0,) * len(shape))
-
-    def late_part(*shape):
-        return pl.BlockSpec((1,) + shape, lambda s: (jnp.maximum(s - parts, 0),) + (0,) * len(shape))
+        return pl.BlockSpec((1,) + shape, lambda s: (part_order(s, parts),) + (0,) * len(shape))
 
     act = jax.ShapeDtypeStruct((count, width), BF16)
-    row = jax.ShapeDtypeStruct((1, width), F32)
     return pl.pallas_call(
         ffn_kernel,
         grid=(2 * parts,),
@@ -387,16 +460,14 @@
         + [whole(1, width)] * 5
         + [per_part(1, share), per_part(width, share), per_part(share, width)],
         out_specs=[whole(count, width)] * 3
-        + [whole(width, width), late_part(width, share), late_part(share, width), late_part(1, share)]
-        + [whole(1, width)] * 6,
+        + [whole(2 * width, width // 2), whole(heights, width, share), whole(heights, share, width), whole(smalls, PAIR)],
         out_shape=[act] * 3
         + [
-            jax.ShapeDtypeStruct((width, width), BF16),
-            jax.ShapeDtypeStruct((parts, width, share), BF16),
-            jax.ShapeDtypeStruct((parts, share, width), BF16),
-            jax.ShapeDtypeStruct((parts, 1, share), F32),
-        ]
-        + [row] * 6,
+            jax.ShapeDtypeStruct((2 * width, width // 2), BF16),
+            jax.ShapeDtypeStruct((heights, width, share), BF16),
+            jax.ShapeDtypeStruct((heights, share, width), BF16),
+            jax.ShapeDtypeStruct((smalls, PAIR), F32),
+        ],
         scratch_shapes=[
             pltpu.VMEM((count, width), BF16),
             pltpu.VMEM((count, width), F32),
@@ -404,23 +475,200 @@
             pltpu.VMEM((parts, count, share), BF16),
             pltpu.VMEM((count, width), BF16),
             pltpu.VMEM((count, share), BF16),
+            pltpu.VMEM((heights, width, share), BF16),
+            pltpu.VMEM((heights, share, width), BF16),
+            pltpu.VMEM((heights, width, share), BF16),
+            pltpu.VMEM((heights, share, width), BF16),
+            pltpu.SemaphoreType.DMA((2, heights)),
+            pltpu.SemaphoreType.DMA((2, heights)),
         ],
-        compiler_params=pltpu.CompilerParams(vmem_limit_bytes=60 * 2**20),
+        compiler_params=pltpu.CompilerParams(vmem_limit_bytes=60 * 2**20, collective_id=0, has_side_effects=True),
         name="feed_forward",
     )(res, cot, ctx, w_out, gain1, shift1, gain2, shift2, b_down, b_up, w_up, w_down)
 
 
+DEPTH = 4
+CORES = 2
+
+
+class Axis:
+    def __init__(self, size, place, device):
+        self.size, self.place, self.device = size, place, device
+
+    def ahead(self, j):
+        return lax.rem(self.place + j, self.size)
+
+
+def slice_axes(dp_size, tensor_size):
+    dp, tensor = lax.axis_index("dp"), lax.axis_index("tensor")
+    across = dp_size // DEPTH
+    z, x = dp // across, lax.rem(dp, across)
+    y, core = tensor // CORES, lax.rem(tensor, CORES)
+    return {
+        "core": Axis(CORES, core, lambda p: (dp, y * CORES + p)),
+        "y": Axis(tensor_size // CORES, y, lambda p: (dp, p * CORES + core)),
+        "x": Axis(across, x, lambda p: (z * across + p, tensor)),
+        "z": Axis(DEPTH, z, lambda p: (p * across + x, tensor)),
+    }
+
+
+def greet(axes):
+    barrier = pltpu.get_barrier_semaphore()
+    count = 0
+    for axis in axes.values():
+        for j in range(1, axis.size):
+            pl.semaphore_signal(
+                barrier, inc=1, device_id=axis.device(axis.ahead(j)), device_id_type=pl.DeviceIdType.MESH
+            )
+            count += 1
+    pl.semaphore_wait(barrier, count)
+
+
+def send(source, target, sems, at, device):
+    return pltpu.make_async_remote_copy(
+        src_ref=source, dst_ref=target, send_sem=sems[0].at[at], recv_sem=sems[1].at[at],
+        device_id=device, device_id_type=pl.DeviceIdType.MESH,
+    )
+
+
+def span(start, size):
+    if isinstance(start, int):
+        return pl.ds(start, size)
+    return pl.ds(pl.multiple_of(start, math.gcd(size, 16)), size)
+
+
+def add_rows(target, target_at, terms, size):
+    tile = next(t for t in (64, 48, 32, 24, 16, 12, 8) if size % t == 0)
+
+    def one(i, carry):
+        total = None
+        for ref, start in terms:
+            rows_of = ref[span(start + i * tile, tile)].astype(F32)
+            total = rows_of if total is None else total + rows_of
+        target[span(target_at + i * tile, tile)] = total.astype(target.dtype)
+        return carry
+
+    lax.fori_loop(0, size // tile, one, 0)
+
+
+class Reduction:
+    def __init__(self, axes, order, back, source, source_at, size, final, final_at, landings, sems, first_sem=0):
+        self.axes, self.order, self.back = axes, order, back
+        self.source, self.source_at, self.size = source, source_at, size
+        self.final, self.final_at = final, final_at
+        self.landings, self.sems = landings, sems
+        self.first_sem = first_sem
+
+    def plan(self):
+        size, at, out = self.size, self.final_at, []
+        for name in self.order:
+            axis = self.axes[name]
+            size //= axis.size
+            at = at + axis.place * size
+            out.append((axis, size, at))
+        return out
+
+    def copies(self, stage):
+        stages = self.plan()
+        sem = self.first_sem
+        for axis, _, _ in stages[:stage]:
+            sem += axis.size - 1
+        axis, size, _ = stages[stage]
+        held, held_at = (self.source, self.source_at) if stage == 0 else (self.landings[stage - 1].at[0], 0)
+        return [
+            send(
+                held.at[span(held_at + axis.ahead(j) * size, size)], self.landings[stage].at[j - 1],
+                self.sems, sem + j - 1, axis.device(axis.ahead(j)),
+            )
+            for j in range(1, axis.size)
+        ]
+
+    def settle(self, stage):
+        for copy in self.copies(stage):
+            copy.wait()
+        axis, size, final_at = self.plan()[stage]
+        held, held_at = (self.source, self.source_at) if stage == 0 else (self.landings[stage - 1].at[0], 0)
+        terms = [(held, held_at + axis.place * size)]
+        terms += [(self.landings[stage].at[j - 1], 0) for j in range(1, axis.size)]
+        if stage == len(self.order) - 1:
+            add_rows(self.final, final_at, terms, size)
+        else:
+            add_rows(self.landings[stage].at[0], 0, terms, size)
+
+    def gathers(self, which):
+        stages = self.plan()
+        sem = self.first_sem + sum(axis.size - 1 for axis, _, _ in stages)
+        for name in self.back[:which]:
+            sem += self.axes[name].size - 1
+        depth = self.order.index(self.back[which])
+        axis, size, at = stages[depth]
+        block = self.final.at[span(at, size)]
+        return [send(block, block, self.sems, sem + j - 1, axis.device(axis.ahead(j))) for j in range(1, axis.size)]
+
+    def events(self):
+        out = []
+        count = len(self.order)
+
+        def begin(copies):
+            for copy in copies:
+                copy.start()
+
+        for stage in range(count):
+            def event(stage=stage):
+                if stage > 0:
+                    self.settle(stage - 1)
+                begin(self.copies(stage))
+
+            out.append(event)
+        for which in range(len(self.back)):
+            def event(which=which):
+                if which == 0:
+                    self.settle(count - 1)
+                else:
+                    for copy in self.gathers(which - 1):
+                        copy.wait()
+                begin(self.gathers(which))
+
+            out.append(event)
+
+        def last():
+            for copy in self.gathers(len(self.back) - 1):
+                copy.wait()
+
+        out.append(last)
+        return out
+
+
+def landing_shapes(order, sizes, size, columns, dtype):
+    shapes = []
+    for name in order:
+        size //= sizes[name]
+        shapes.append(pltpu.VMEM((sizes[name] - 1, size, columns), dtype))
+    return shapes
+
+
+def copies_of(order, back, sizes):
+    return sum(sizes[name] - 1 for name in order) + sum(sizes[name] - 1 for name in back)
+
+
 def attend_back_kernel(
     dctx_ref, att_ref, inv_ref, q_ref, k_ref, v_ref, sq_ref, sk_ref, w_ref, s_ref, x_ref, col_ref, pad_ref,
-    wq_ref, wk_ref, wv_ref, tap_ref, flip_ref, dproj_ref,
-    gw_ref, gb_ref, gconv_ref, gt_ref,
+    wq_ref, wk_ref, wv_ref, flip_ref, dproj_ref, gwo_ref, pu_ref, pd_ref, small_ref,
+    gt_ref, all_out, up_out, down_out, few_out,
     near_ref, vv_ref, dpad_ref, dcos_ref, dq_ref, dk_ref, dv_ref, joined_ref, gwacc_ref, gtacc_ref, conv_ref,
+    gwlow_ref, gb_ref, mini_ref, all_ref, up_ref, down_ref, few_ref, out_sem, *links,
+    plan, quads, seqs,
 ):
     quad, row = pl.program_id(0), pl.program_id(1)
-    quads, seqs = pl.num_programs(0), pl.num_programs(1)
     length = x_ref.shape[0]
     blocks = length // BLK
     inside = slice(HALO, HALO + length)
+
+    _, sizes, dp_size, tensor_size = plan
+    axes = slice_axes(dp_size, tensor_size)
+    ticks = schedule(axes, sizes, quads, seqs, gwo_ref, pu_ref, pd_ref, gwlow_ref, mini_ref, all_ref, up_ref, down_ref, few_ref, links,
+        (all_out, up_out, down_out, few_out, out_sem))
+    calls = quads * seqs * (QUAD // PAIR)
 
     build_near(col_ref[...], pad_ref[0], near_ref)
     for half in range(2):
@@ -434,9 +682,26 @@
     def _():
         conv_ref[...] = jnp.zeros_like(conv_ref)
         gwacc_ref[...] = jnp.zeros_like(gwacc_ref)
+
+    @pl.when((quad == 0) & (row == 0))
+    def _():
         gb_ref[...] = jnp.zeros_like(gb_ref)
+        mini_ref[...] = jnp.zeros_like(mini_ref)
+        mini_ref[: small_ref.shape[0]] = small_ref[...]
+        filled = 2 * gwacc_ref.shape[0]
+        if gwlow_ref.shape[1] > filled:
+            gwlow_ref[:, filled:] = jnp.zeros((quads, gwlow_ref.shape[1] - filled, gwlow_ref.shape[2]), BF16)
 
     def one_pair(pair, carry):
+        tick = (quad * seqs + row) * (QUAD // PAIR) + pair
+        for when in range(calls):
+            if ticks.get(when):
+
+                @pl.when(tick == when)
+                def _(when=when):
+                    for event in ticks[when]:
+                        event()
+
         at = pl.ds(pl.multiple_of(pair * PAIR, PAIR), PAIR)
         inverse = inv_ref[:, at].astype(F32)
         d_ctx = dctx_ref[:, at]
@@ -490,10 +755,39 @@
 
     lax.fori_loop(0, QUAD // PAIR, one_pair, 0)
 
-    gb_ref[0] += column_sum(joined_ref[...].astype(F32))
-    for start in range(0, gwacc_ref.shape[0], TILE):
+    gb_ref[quad, :1] += column_sum(joined_ref[...].astype(F32))
+    width = gwacc_ref.shape[0]
+    for start in range(0, width, TILE):
         cut = slice(start, start + TILE)
         gwacc_ref[cut] += dot_tn(x_ref[:, cut], joined_ref[...])
+
+    @pl.when(row == seqs - 1)
+    def _():
+        half = gwacc_ref.shape[1] // 2
+        for start in range(0, width, TILE):
+            for side in range(2):
+                values = gwacc_ref[start : start + TILE, side * half : (side + 1) * half]
+                gwlow_ref[quad, side * width + start : side * width + start + TILE] = values.astype(BF16)
+        base = small_ref.shape[0]
+        lines = gb_ref.shape[2] // PAIR
+        for i in range(lines):
+            mini_ref[pl.ds(base + quad * lines + i, 1)] = gb_ref[quad, :1, i * PAIR : (i + 1) * PAIR]
+        base += quads * lines
+        for head in range(QUAD // HEAD):
+            sums = conv_ref[head]
+            high = sums.astype(BF16)
+            turn = (rows((BLK, BLK)) + lanes((BLK, BLK)) == BLK - 1).astype(BF16)
+            turned = dot_nn(turn, high) + dot_nn(turn, (sums - high.astype(F32)).astype(BF16))
+            turned = pltpu.roll(turned, BLK, 1, stride=1, stride_axis=0)
+            mini_ref[pl.ds(base + quad * (QUAD // HEAD) + head, 1)] = column_sum(turned)[:, :PAIR]
+
+    last = (quad == quads - 1) & (row == seqs - 1)
+
+    @pl.when(last)
+    def _():
+        for event in ticks[calls]:
+            event()
+
     for start in range(0, length, TILE):
         here = pl.ds(pl.multiple_of(row * length + start, TILE), TILE)
         cut = slice(start, start + TILE)
@@ -515,19 +809,131 @@
     def _():
         gt_ref[...] = gtacc_ref[pl.ds(pl.multiple_of(row * length, TILE), length)].astype(BF16)
 
-    @pl.when(row == seqs - 1)
-    def _():
-        gw_ref[0] = gwacc_ref[...].astype(BF16)
-        for head in range(QUAD // HEAD):
-            sums = conv_ref[head]
-            high = sums.astype(BF16)
-            turn = (rows((BLK, BLK)) + lanes((BLK, BLK)) == BLK - 1).astype(BF16)
-            turned = dot_nn(turn, high) + dot_nn(turn, (sums - high.astype(F32)).astype(BF16))
-            turned = pltpu.roll(turned, 0, 1, stride=1, stride_axis=0)
-            gconv_ref[0, head : head + 1] = column_sum(turned)
-
-
-def attend_back(dctx, att, inv, q, k, v, sq, sk, weight, slope, tokens, seg_col, seg_pad, w_qkv, taps, flipped, dproj, length):
+    @pl.when(last)
+    def _():
+        for when in sorted(ticks):
+            if when > calls:
+                for event in ticks[when]:
+                    event()
+
+
+FFN_ROWS = 384
+FFN_ORDER = ("y", "x", "z")
+FFN_BACK = ("z", "x")
+ORDERS = (("core", "x", "y", "z"), ("core", "y", "x", "z"))
+
+
+def all_order(index):
+    order = ORDERS[index % 2]
+    return order, order[::-1]
+
+
+class FfnReduction(Reduction):
+    def copies(self, stage):
+        if stage > 0:
+            return super().copies(stage)
+        axis = self.axes["y"]
+        return [
+            send(
+                self.source.at[j - 1, span(self.source_at, self.size)], self.landings[0].at[j - 1],
+                self.sems, self.first_sem + j - 1, axis.device(axis.ahead(j)),
+            )
+            for j in range(1, axis.size)
+        ]
+
+    def plan(self):
+        size, at = self.size, self.final_at
+        out = [(self.axes["y"], size, at)]
+        for name in self.order[1:]:
+            axis = self.axes[name]
+            size //= axis.size
+            at = at + axis.place * size
+            out.append((axis, size, at))
+        return out
+
+    def settle(self, stage):
+        if stage > 0:
+            return super().settle(stage)
+        axis = self.axes["y"]
+        for copy in self.copies(0):
+            copy.wait()
+        terms = [(self.source.at[axis.size - 1], self.source_at)]
+        terms += [(self.landings[0].at[j - 1], 0) for j in range(1, axis.size)]
+        add_rows(self.landings[0].at[0], 0, terms, self.size)
+
+
+def link_plan(sizes, width, share, quads):
+    out = []
+    devices = math.prod(sizes.values())
+    y = sizes["y"]
+    for height, columns in ((width, share), (share, width)):
+        for _ in range(height // FFN_ROWS):
+            shapes = [pltpu.VMEM((y - 1, FFN_ROWS, columns), BF16)]
+            shapes += landing_shapes(FFN_ORDER[1:], sizes, FFN_ROWS, columns, BF16)
+            out.append((shapes, copies_of(FFN_ORDER, FFN_BACK, sizes)))
+    for index in range(quads + 1):
+        order, back = all_order(index)
+        out.append((landing_shapes(order, sizes, padded(2 * width, devices), width // 2, BF16), copies_of(order, back, sizes)))
+    order, back = all_order(quads)
+    out.append((landing_shapes(order, sizes, 8 * devices, PAIR, F32), copies_of(order, back, sizes)))
+    return out
+
+
+def padded(size, devices):
+    return -(-size // (16 * devices)) * 16 * devices
+
+
+def schedule(axes, sizes, quads, seqs, gwo_ref, pu_ref, pd_ref, gwlow_ref, mini_ref, all_ref, up_ref, down_ref, few_ref, links, outs):
+    all_out, up_out, down_out, few_out, out_sem = outs
+    calls = quads * seqs * (QUAD // PAIR)
+    per_quad = seqs * (QUAD // PAIR)
+    width, share = pu_ref.shape[1], pu_ref.shape[2]
+    devices = math.prod(sizes.values())
+    groups = link_plan(sizes, width, share, quads)
+    taken, position = [], 0
+    for shapes, _ in groups:
+        taken.append((links[position : position + len(shapes)], links[position + len(shapes) : position + len(shapes) + 2]))
+        position += len(shapes) + 2
+    ticks = {0: [lambda: greet(axes)]}
+
+    stores = []
+
+    def enlist(reduction, times, done, place):
+        for time, event in zip(times, reduction.events(), strict=True):
+            ticks.setdefault(time, []).append(event)
+        store = pltpu.make_async_copy(done, place, out_sem.at[len(stores)])
+        ticks[times[-1]].append(store.start)
+        stores.append(store)
+
+    number = 0
+    begin = (0, 0, 3, 6)
+    for source, final, place in ((pu_ref, up_ref, up_out), (pd_ref, down_ref, down_out)):
+        for start in range(0, source.shape[1], FFN_ROWS):
+            landings, sems = taken[number]
+            reduction = FfnReduction(axes, FFN_ORDER, FFN_BACK, source, start, FFN_ROWS, final, start, landings, sems)
+            done = 3 * (number + 1)
+            enlist(reduction, (begin[number], done, done + 2, done + 4, done + 6, done + 8),
+                   final.at[span(start, FFN_ROWS)], place.at[span(start, FFN_ROWS)])
+            number += 1
+    size = padded(2 * width, devices)
+    for index in range(quads + 1):
+        landings, sems = taken[number]
+        order, back = all_order(index)
+        source = gwo_ref if index == 0 else gwlow_ref.at[index - 1]
+        reduction = Reduction(axes, order, back, source, 0, size, all_ref.at[index], 0, landings, sems)
+        first = index * per_quad
+        enlist(reduction, (first, first + 1, first + 3, first + 5, first + 6, first + 7, first + 9, first + 11, first + 12),
+               all_ref.at[index], all_out.at[index])
+        number += 1
+    landings, sems = taken[number]
+    order, back = all_order(quads)
+    reduction = Reduction(axes, order, back, mini_ref, 0, 8 * devices, few_ref, 0, landings, sems)
+    enlist(reduction, (calls, calls + 1, calls + 3, calls + 5, calls + 6, calls + 7, calls + 9, calls + 11, calls + 12), few_ref, few_out)
+    ticks[max(ticks) + 1] = [store.wait for store in stores]
+    return ticks
+
+
+def attend_back(dctx, att, inv, q, k, v, sq, sk, weight, slope, tokens, seg_col, seg_pad, w_qkv, flipped, dproj, gwo, pu, pd, small, dp_size, tensor_size, length):
     count, width = tokens.shape
     seqs = count // length
     quads = width // QUAD
@@ -540,9 +946,22 @@
     def part(k):
         return pl.BlockSpec((width, QUAD), lambda p, r, k=k: (0, p + k * quads))
 
+    sizes = {"core": CORES, "y": tensor_size // CORES, "x": dp_size // DEPTH, "z": DEPTH}
+    devices = dp_size * tensor_size
+    share = pu.shape[2]
+    grown = padded(2 * width, devices)
+    gwo = jnp.pad(gwo, ((0, grown - gwo.shape[0]), (0, 0)))
+    minis = 8 * devices
+    scratch = []
+    for shapes, count_of in link_plan(sizes, width, share, quads):
+        scratch += shapes + [pltpu.SemaphoreType.DMA((count_of,)), pltpu.SemaphoreType.DMA((count_of,))]
+
+    def whole(*shape):
+        return pl.BlockSpec(shape, lambda p, r: (0,) * len(shape), pipeline_mode=pl.Buffered(1))
+
     taps_spec = pl.BlockSpec((1, per, 2 * BLK), lambda p, r: (p, 0, 0))
     return pl.pallas_call(
-        attend_back_kernel,
+        functools.partial(attend_back_kernel, plan=(None, sizes, dp_size, tensor_size), quads=quads, seqs=seqs),
         grid=(quads, seqs),
         in_specs=[own] * 8
         + [big] * 2
@@ -551,20 +970,20 @@
             pl.BlockSpec((length, 1), lambda p, r: (r, 0)),
             pl.BlockSpec((1, 1, length + 2 * HALO), lambda p, r: (r, 0, 0)),
             part(0), part(1), part(2),
-            taps_spec, taps_spec,
+            taps_spec,
             wide,
+            whole(*gwo.shape), whole(*pu.shape), whole(*pd.shape), whole(*small.shape),
         ],
         out_specs=[
-            pl.BlockSpec((1, width, 3 * QUAD), lambda p, r: (p, 0, 0)),
-            pl.BlockSpec((1, 1, 3 * QUAD), lambda p, r: (p, 0, 0)),
-            pl.BlockSpec((1, per, 2 * BLK), lambda p, r: (p, 0, 0)),
             pl.BlockSpec((length, width), lambda p, r: (jnp.where(p == quads - 1, r, 0), 0)),
-        ],
+        ]
+        + [pl.BlockSpec(memory_space=pl.ANY)] * 4,
         out_shape=[
-            jax.ShapeDtypeStruct((quads, width, 3 * QUAD), BF16),
-            jax.ShapeDtypeStruct((quads, 1, 3 * QUAD), F32),
-            jax.ShapeDtypeStruct((quads, per, 2 * BLK), F32),
             jax.ShapeDtypeStruct((count, width), BF16),
+            jax.ShapeDtypeStruct((quads + 1, grown, width // 2), BF16),
+            jax.ShapeDtypeStruct((width, share), BF16),
+            jax.ShapeDtypeStruct((share, width), BF16),
+            jax.ShapeDtypeStruct((minis, PAIR), F32),
         ],
         scratch_shapes=[
             pltpu.VMEM((blocks, BLK, 2 * BLK), BF16),
@@ -578,10 +997,19 @@
             pltpu.VMEM((width, 3 * QUAD), F32),
             pltpu.VMEM((count, width), F32),
             pltpu.VMEM((per, BLK, 2 * BLK), F32),
-        ],
-        compiler_params=pltpu.CompilerParams(vmem_limit_bytes=60 * 2**20),
+            pltpu.VMEM((quads, grown, width // 2), BF16),
+            pltpu.VMEM((quads, 8, 3 * QUAD), F32),
+            pltpu.VMEM((minis, PAIR), F32),
+            pltpu.VMEM((quads + 1, grown, width // 2), BF16),
+            pltpu.VMEM((width, share), BF16),
+            pltpu.VMEM((share, width), BF16),
+            pltpu.VMEM((minis, PAIR), F32),
+            pltpu.SemaphoreType.DMA((quads + 2 + (width + share) // FFN_ROWS,)),
+        ]
+        + scratch,
+        compiler_params=pltpu.CompilerParams(vmem_limit_bytes=60 * 2**20, collective_id=1, has_side_effects=True),
         name="attend_backward",
-    )(dctx, att, inv, q, k, v, sq, sk, weight, slope, tokens, seg_col, seg_pad, w_qkv, w_qkv, w_qkv, taps, flipped, dproj)
+    )(dctx, att, inv, q, k, v, sq, sk, weight, slope, tokens, seg_col, seg_pad, w_qkv, w_qkv, w_qkv, flipped, dproj, gwo, pu, pd, small)
 
 
 def body(
@@ -590,13 +1018,13 @@
 ):
     seqs, length = segment_ids.shape
     width = tokens.shape[1]
-    heads, span = conv_kernel.shape
+    heads, span_of = conv_kernel.shape
     per = QUAD // HEAD
-    radius = span // 2
+    radius = span_of // 2
     first_tap = HALO - radius
 
     def spread(kernel):
-        padded = jnp.pad(kernel, ((0, 0), (first_tap, 2 * BLK - first_tap - span)))
+        padded = jnp.pad(kernel, ((0, 0), (first_tap, 2 * BLK - first_tap - span_of)))
         return padded.reshape(heads // per, per, 2 * BLK)
 
     seg_col = segment_ids.reshape(-1, 1)
@@ -606,32 +1034,37 @@
     up_all = lax.all_gather(w_up, "tensor")
     down_all = lax.all_gather(w_down, "tensor")
     bias_all = lax.all_gather(b_up, "tensor")[:, None, :]
+    dp_size, tensor_size = lax.axis_size("dp"), lax.axis_size("tensor")
+    share = w_up.shape[1]
 
     q, k, v, sq, sk, weight, slope, att, inv, ctx, res = attend(
         tokens, seg_col, seg_pad, w_qkv, b_qkv[None], taps, w_out, b_out[None], length
     )
-    out, dproj, dctx, gwo, gu, gd, gbu, gbd, gg2, gs2, gg1, gs1, gbo = feed_forward(
+    out, dproj, dctx, gwo, pu, pd, small = feed_forward(
         res, cotangent, ctx, w_out, norm1_gain[None], norm1_bias[None], norm2_gain[None], norm2_bias[None],
         b_down[None], bias_all, up_all, down_all,
     )
-    gw, gb, gconv, gt = attend_back(
-        dctx, att, inv, q, k, v, sq, sk, weight, slope, tokens, seg_col, seg_pad, w_qkv, taps, flipped, dproj, length
+    gt, grads, grad_up, grad_down, few = attend_back(
+        dctx, att, inv, q, k, v, sq, sk, weight, slope, tokens, seg_col, seg_pad, w_qkv, flipped, dproj,
+        gwo, pu, pd, small, dp_size, tensor_size, length,
     )
-    grad_up = lax.psum(lax.psum_scatter(gu, "tensor"), "dp").astype(F32)
-    grad_down = lax.psum(lax.psum_scatter(gd, "tensor"), "dp").astype(F32)
-    first_lane = first_tap + BLK - 1
-    grad_conv = gconv.reshape(heads, 2 * BLK)[:, first_lane : first_lane + span]
-    gw, gwo = lax.psum((gw, gwo), ("dp", "tensor"))
-    gb, grad_conv, gbo, gg1, gs1, gbd, gg2, gs2, gbu = lax.psum(
-        (gb, grad_conv, gbo, gg1, gs1, gbd, gg2, gs2, gbu), ("dp", "tensor")
-    )
-    quads = gw.shape[0]
-    gw = gw.reshape(quads, width, 3, QUAD).transpose(1, 2, 0, 3).reshape(width, 3 * width).astype(F32)
-    gb = gb.reshape(quads, 3, QUAD).transpose(1, 0, 2).reshape(3 * width)
-    grad_b_up = lax.dynamic_index_in_dim(gbu, lax.axis_index("tensor"), 0, False)[0]
+    quads = width // QUAD
+    grads = grads[:, : 2 * width].astype(F32).reshape(quads + 1, 2, width, width // 2).transpose(0, 2, 1, 3)
+    grads = grads.reshape(quads + 1, width, width)
+    gwo = grads[0]
+    gw = grads[1:].reshape(quads, width, 3, QUAD).transpose(1, 2, 0, 3).reshape(width, 3 * width)
+    lines = width // PAIR
+    gg2, gs2, gbd, gg1, gs1, gbo = few[: 6 * lines].reshape(6, width)
+    gbu = few[6 * lines : 6 * lines + tensor_size * share // PAIR].reshape(tensor_size, share)
+    grad_b_up = lax.dynamic_index_in_dim(gbu, lax.axis_index("tensor"), 0, False)
+    base = small.shape[0]
+    gb = few[base : base + 3 * lines].reshape(quads, 3, QUAD).transpose(1, 0, 2).reshape(3 * width)
+    base += 3 * lines
+    first_lane = (first_tap + BLK - 1 + BLK) % (2 * BLK)
+    grad_conv = few[base : base + heads, first_lane : first_lane + span_of]
     return (
-        out, gt, gw, gb, grad_conv, gwo.astype(F32), gbo[0], gg1[0], gs1[0],
-        grad_up, grad_b_up, grad_down, gbd[0], gg2[0], gs2[0],
+        out, gt, gw, gb, grad_conv, gwo, gbo, gg1, gs1,
+        grad_up.astype(F32), grad_b_up, grad_down.astype(F32), gbd, gg2, gs2,
     )
 
 

time: 526 us -> 359 us (0.68)
  waiting for transfers between devices: 260 us -> 10.3 us
  Pallas kernels: 175 us -> 281 us
  blocking collectives: 48.7 us -> 7.16 us
  local copies, waits for them, and re-layouts: 20.8 us -> 42.5 us
    psum x2 -> x0, waiting for transfers between devices: 212 us -> none  [the longest x1 108 us: body(): gw, gwo = lax.psum((gw, gwo), ('dp', 'tensor'))]
    pallas_call x1, Pallas kernels: 54.3 us -> 159 us  [attend_back(): pl.pallas_call(functools.partial(attend_back_kernel, plan=(None, sizes, d...]
    psum x1 -> x0, blocking collectives: 41.7 us -> none  [body(): lax.psum((gb, grad_conv, gbo, gg1, gs1, gbd, gg2, gs2, gbu), ('dp', 'tens...]
    reduce_scatter x2 -> x0, waiting for transfers between devices: 35.7 us -> none  [the longest x1 35.7 us: body(): grad_down = lax.psum(lax.psum_scatter(gd, 'tensor'), 'dp').astype(F32)]
    transpose x0 -> x2, local copies, waits for them, and re-layouts: none -> 10.7 us  [the longest x1 7.38 us: body(): grads[:, :2 * width].astype(F32).reshape(quads + 1, 2, width, width // 2)]
    slice x1 -> x5, local copies, waits for them, and re-layouts: 0.07 us -> 8.69 us  [the longest x1 3.46 us: body(): grads[1:].reshape(quads, width, 3, QUAD).transpose(1, 2, 0, 3)]
    unnamed x46 -> x37, local copies, waits for them, and re-layouts: 7.17 us -> 14.2 us
  transfers between devices with their start and end apart: 6 -> 2, of which waited for: 4 -> 1; matrix products, arithmetic and copies ran while one was open for 4% -> 2% of each run, Pallas kernels for 21% -> 16%
where the time goes in v2:
time: 359 us; the launch traced here: 358 us
  Pallas kernels  281 us (78%)
  local copies, waits for them, and re-layouts  42.5 us (12%)
  between operations  14.2 us (4%)
  waiting for transfers between devices  10.3 us (3%)
  blocking collectives  7.16 us (2%)
    pallas_call x1, Pallas kernels, attend_back(): pl.pallas_call(functools.partial(attend_back_kernel, plan=(None, sizes, d...  159 us
    pallas_call x1, Pallas kernels, feed_forward(): pl.pallas_call(ffn_kernel, grid=(2 * parts,), in_specs=[whole(count, widt...  64.9 us
    pallas_call x1, Pallas kernels, attend(): pl.pallas_call(attend_kernel, grid=(seqs, quads), in_specs=[pl.BlockSpec(...  56.8 us
    unnamed x37, local copies, waits for them, and re-layouts  14.2 us
    all_gather x1, waiting for transfers between devices, body(): down_all = lax.all_gather(w_down, 'tensor')  8.94 us
    transpose x1, local copies, waits for them, and re-layouts, body(): grads[:, :2 * width].astype(F32).reshape(quads + 1, 2, width, width // 2)  7.38 us
  transfers between devices with their start and end apart: 2, of which 1 were waited for; matrix products, arithmetic and copies ran while one was open for 2% of the time, Pallas kernels for 16%

profile of v2, /device:TPU:0, one launch (start us, length us, event | category | flops | bytes accessed | tf_op | source)
XLA Modules:
  0.0 358.0 jit_solution(7862501868440725226)
XLA Ops:
  7.3 0.7 all-gather.7.cloned.1.call-update
  8.1 0.7 all-gather.9.cloned.1.call-update
  8.8 1.0 copy.47
  9.9 0.6 broadcast_in_dim.27.pad_ref
  10.7 0.6 reshape.77.tap_ref
  11.3 0.6 broadcast_in_dim.28.bq_ref.bk_ref.bv_ref
  11.9 0.6 broadcast_in_dim.29.bo_ref
  12.5 0.6 broadcast_in_dim.30.gain1_ref
  14.2 0.6 broadcast_in_dim.33.shift2_ref
  15.5 0.6 reshape.78.flip_ref
  16.1 56.8 %attend_forward.1 = (bf16[1024,768]{1,0:T(8,128)(2,1)}, bf16[1024,768]{1,0:T(8,128)(2,1)}, bf16[1024,768]{1,0:T(8,128)(2,1)}, bf16[1024,768]{1,0:T(8,128)(2,1)},...) custom-call(bf16[1024,768]{1,0:T(8,128)(2,1)} %x_ref.3, ...), custom_call_target="tpu_custom_call" | custom-call | tf_op jit(solution)/shard_map/attend_forward/pallas_call | solution.py:211
  72.9 7.2 %all-gather.3.bu_ref = bf16[4,1,768]{2,1,0:T(2,128)(2,1)} all-gather(bf16[1,1,768]{2,1,0:T(2,128)(2,1)S(1)} %reshape.90), channel_id=2, replica_groups=mesh['dp'=8,'tensor'=4] {'tensor'}, dimensions={0}, use_global_device_ids=true | all-gather | bytes 7680 | tf_op jit(solution)/shard_map/all_gather | solution.py:1036
  80.0 8.9 %all-gather.9.cloned.1.call-done = bf16[3072,768]{1,0:T(8,128)(2,1)} async-done(((bf16[768,768]{1,0:T(8,128)(2,1)}), bf16[3072,768]{1,0:T(8,128)(2,1)}) %all-gather.9.cloned.1.call-update) | async-done | bytes 4718608 | tf_op jit(solution)/shard_map/all_gather | solution.py:1035
  89.0 64.9 %feed_forward.1 = (bf16[1024,768]{1,0:T(8,128)(2,1)}, bf16[1024,768]{1,0:T(8,128)(2,1)}, bf16[1024,768]{1,0:T(8,128)(2,1)}, bf16[1536,384]{1,0:T(8,128)(2,1)}, b...) custom-call(f32[1024,768]{1,0:T(8,128)} %get-tuple-element.38.res_ref, ...), custom_call_target="tpu_custom_call" | custom-call | tf_op jit(solution)/shard_map/feed_forward/pallas_call | solution.py:455
  153.9 158.9 %attend_backward.1 = (bf16[1024,768]{1,0:T(8,128)(2,1)}, bf16[4,1536,384]{2,1,0:T(8,128)(2,1)}, bf16[768,768]{1,0:T(8,128)(2,1)}, bf16[768,768]{1,0:T(8,128)(2,1)}, f32[256,128]{1,0:T(8,128)}) custom-call(bf16[1024,768]{1,0:T(8,128)(2,1)} %get-tuple-element.41.dctx_ref, bf16[1024,768]{1,0:T(8,128)(2,1)} %get-tuple-element.42.att_ref, ...), custom_call_target="tpu_custom_call" | custom-call | tf_op jit(solution)/shard_map/attend_backward/pallas_call | solution.py:963
  312.8 7.4 %copy.41 = f32[4,2,768,384]{2,3,1,0:T(8,128)} copy(bf16[4,2,768,384]{3,2,1,0:T(8,128)(2,1)} %bitcast.38) | data formatting | bytes 14155776 | tf_op jit(solution)/shard_map/transpose | solution.py:1052
  320.2 3.5 slice.35
  323.6 1.8 slice.36
  325.5 1.3 slice.31
  326.8 0.7 slice.34
  327.5 1.4 slice_bitcast_fusion
  328.9 1.4 slice.32
  330.3 3.3 copy.42
  333.6 8.0 %copy.44 = f32[768,2304]{1,0:T(8,128)} copy(f32[768,2304]{0,1:T(8,128)} %bitcast.32) | data formatting | bytes 14155776
  341.6 1.9 copy.45
  343.5 1.6 convert_element_type.10
  345.2 1.6 convert_element_type.11
  346.8 0.6 reshape.83
  347.4 0.6 dynamic-slice_reduce_fusion
  348.0 1.1 copy.52
  349.2 0.8 copy-done.1
  350.0 1.1 copy.53
  (44 shorter events, 2.3 us)
Async XLA Ops:
  7.2 1.6 copy-start.6
  7.2 3.3 copy-start.5
  7.2 4.1 %copy-start.7 = (f32[2304]{0:T(1024)S(1)}, f32[2304]{0:T(1024)}, u32[]{:S(2)}) copy-start(f32[2304]{0:T(1024)} %param.19) | copy-start | bytes 27652
  7.2 4.7 %copy-start.8 = (f32[768]{0:T(1024)S(1)}, f32[768]{0:T(1024)}, u32[]{:S(2)}) copy-start(f32[768]{0:T(1024)} %param.22) | copy-start | bytes 9220
  7.2 5.2 %copy-start.14 = (bf16[768]{0:T(1024)(128)(2,1)S(1)}, bf16[768]{0:T(1024)(128)(2,1)}, u32[]{:S(2)}) copy-start(bf16[768]{0:T(1024)(128)(2,1)} %param.26) | copy-start | bytes 4612
  7.2 5.2 %copy-start.9 = (f32[768]{0:T(1024)S(1)}, f32[768]{0:T(1024)}, u32[]{:S(2)}) copy-start(f32[768]{0:T(1024)} %param.23) | copy-start | bytes 9220
  7.2 5.8 %copy-start.10 = (f32[768]{0:T(1024)S(1)}, f32[768]{0:T(1024)}, u32[]{:S(2)}) copy-start(f32[768]{0:T(1024)} %param.24) | copy-start | bytes 9220
  7.3 6.4 %copy-start.11 = (f32[768]{0:T(1024)S(1)}, f32[768]{0:T(1024)}, u32[]{:S(2)}) copy-start(f32[768]{0:T(1024)} %param.29) | copy-start | bytes 9220
  7.3 7.0 %copy-start.12 = (f32[768]{0:T(1024)S(1)}, f32[768]{0:T(1024)}, u32[]{:S(2)}) copy-start(f32[768]{0:T(1024)} %param.30) | copy-start | bytes 9220
  7.3 7.5 %copy-start.13 = (f32[768]{0:T(1024)S(1)}, f32[768]{0:T(1024)}, u32[]{:S(2)}) copy-start(f32[768]{0:T(1024)} %param.28) | copy-start | bytes 9220
  7.3 72.8 %all-gather.7.cloned.1.call-start = ((), (), s32[]{:S(2)}) async-start(), calls=%async_computation | async-start | bytes 5898240 | tf_op jit(solution)/shard_map/all_gather | solution.py:1034
  8.0 81.0 %all-gather.9.cloned.1.call-start = ((), (), s32[]{:S(2)}) async-start(), calls=%async_computation.1 | async-start | bytes 5898240 | tf_op jit(solution)/shard_map/all_gather | solution.py:1035
  341.6 1.9 copy-start.3
  343.5 1.7 copy-start.2
  345.2 1.6 copy-start.4
  345.2 2.8 copy-start
  348.0 2.0 copy-start.1
Sparse Core Ops, SparseCore 0:
  9.7 40.1 all-gather.6
  51.4 37.5 all-gather.8

commit v3 on v2

--- a/solution.py
+++ b/solution.py
@@ -110,10 +110,15 @@
 
 def attend_kernel(
     x_ref, col_ref, pad_ref, wq_ref, wk_ref, wv_ref, bq_ref, bk_ref, bv_ref, tap_ref, wo_ref, bo_ref,
+    wu_ref, wd_ref, bu_ref,
     q_ref, k_ref, v_ref, sq_ref, sk_ref, w_ref, s_ref, att_ref, inv_ref, ctx_ref, res_ref,
-    same_ref, near_ref, vv_ref,
+    up_ref, down_ref, bias_ref,
+    same_ref, near_ref, vv_ref, send_sem, recv_sem, copy_sem,
+    *, dp_size, tensor_size,
 ):
-    quad = pl.program_id(1)
+    row, quad = pl.program_id(0), pl.program_id(1)
+    quads, seqs = pl.num_programs(1), pl.num_programs(0)
+    ticks = gather_plan(dp_size, tensor_size, (wu_ref, wd_ref, bu_ref), (up_ref, down_ref, bias_ref), (send_sem, recv_sem), copy_sem)
     length = x_ref.shape[0]
     blocks = length // BLK
 
@@ -140,6 +145,14 @@
         v_ref[here] = (dot_nn(x, wv_ref[...]) + bv_ref[...]).astype(BF16)
 
     def one_pair(pair, carry):
+        turn = (row * quads + quad) * (QUAD // PAIR) + pair
+        for when, events in ticks.items():
+
+            @pl.when(turn == when)
+            def _(events=events):
+                for event in events:
+                    event()
+
         at = pl.ds(pl.multiple_of(pair * PAIR, PAIR), PAIR)
         v = v_ref[:, at]
         for half in range(2):
@@ -177,23 +190,82 @@
 
     lax.fori_loop(0, QUAD // PAIR, one_pair, 0)
 
+    @pl.when(quad == 0)
+    def _():
+        res_ref[...] = x_ref[...].astype(F32) + bo_ref[...]
+
     for start in range(0, length, BLK):
         here = slice(start, start + BLK)
-        grown = dot_nn(ctx_ref[here], wo_ref[...])
-
-        @pl.when(quad == 0)
-        def _():
-            res_ref[here] = grown + x_ref[here].astype(F32) + bo_ref[...]
-
-        @pl.when(quad > 0)
-        def _():
-            res_ref[here] += grown
+        res_ref[here] += dot_nn(ctx_ref[here], wo_ref[...])
+
+
+def gather_plan(dp_size, tensor_size, own, whole, sems, copy_sem):
+    axes = slice_axes(dp_size, tensor_size)
+    y, x, core = axes["y"], axes["x"], axes["core"]
+    mate = core.device(core.ahead(1))
+    number = iter(range(1000))
+
+    def mine(place):
+        return place * CORES + core.place
+
+    def rows_at(ref, place):
+        size = ref.shape[-2] // x.size
+        return span(place * size, size)
+
+    def at_y(which):
+        source, target = own[which], whole[which]
+        out = []
+        for j in range(1, y.size):
+            if which < 2:
+                block = rows_at(source, x.place)
+                pair = (source.at[block], target.at[mine(y.place), block])
+            else:
+                pair = (source, target.at[mine(y.place)])
+            out.append(send(*pair, sems, next(number), y.device(y.ahead(j))))
+        return out
+
+    def at_x(which):
+        target = whole[which]
+        out = []
+        for j in range(1, y.size):
+            block = target.at[mine(y.ahead(j)), rows_at(target, x.place)]
+            out += [send(block, block, sems, next(number), x.device(x.ahead(i))) for i in range(1, x.size)]
+        return out
+
+    def to_mate(which):
+        target = whole[which]
+        return [
+            send(target.at[mine(y.ahead(j))], target.at[mine(y.ahead(j))], sems, next(number), mate)
+            for j in range(1, y.size)
+        ]
+
+    keep = [pltpu.make_async_copy(own[i], whole[i].at[mine(y.place)], copy_sem.at[i]) for i in range(3)]
+    give = [send(own[i], whole[i].at[mine(y.place)], sems, next(number), mate) for i in range(3)]
+    ys, xs, mates = [at_y(i) for i in range(3)], [at_x(i) for i in range(2)], [to_mate(i) for i in range(3)]
+
+    def start(copies):
+        return [copy.start for copy in copies]
+
+    def wait(copies):
+        return [copy.wait for copy in copies]
+
+    steps = [
+        [lambda: greet(axes, ("core", "y", "x"))] + start(ys[0] + ys[2] + give + keep),
+        wait(ys[0] + ys[2]) + start(xs[0] + ys[1] + mates[2]),
+        wait(xs[0] + ys[1]) + start(mates[0] + xs[1]),
+        wait(xs[1]) + start(mates[1]),
+    ]
+    last = wait(mates[0] + mates[1] + mates[2] + give + keep)
+    return dict(zip(GATHER_TIMES, steps)) | {GATHER_TIMES[len(steps)]: last}
+
+
+GATHER_TIMES = (0, 4, 7, 10, 11)
 
 
 KCH = 256
 
 
-def attend(tokens, seg_col, seg_pad, w_qkv, b_qkv, taps, w_out, b_out, length):
+def attend(tokens, seg_col, seg_pad, w_qkv, vectors, taps, w_out, w_up, w_down, b_up, dp_size, tensor_size, length):
     count, width = tokens.shape
     seqs = count // length
     quads = width // QUAD
@@ -208,8 +280,10 @@
     def part(rows_of, k):
         return pl.BlockSpec((rows_of, QUAD), lambda r, p, k=k: (0, p + k * quads))
 
+    others = tensor_size // CORES - 1
+    copies = 3 + 6 * others + 2 * others * (dp_size // DEPTH - 1)
     return pl.pallas_call(
-        attend_kernel,
+        functools.partial(attend_kernel, dp_size=dp_size, tensor_size=tensor_size),
         grid=(seqs, quads),
         in_specs=[
             pl.BlockSpec((length, width), lambda r, p: (r, 0)),
@@ -219,22 +293,196 @@
             part(1, 0), part(1, 1), part(1, 2),
             pl.BlockSpec((1, per, 2 * BLK), lambda r, p: (p, 0, 0)),
             pl.BlockSpec((QUAD, width), lambda r, p: (p, 0)),
-            pl.BlockSpec((1, width), lambda r, p: (0, 0)),
+            pl.BlockSpec((1, width), lambda r, p: (0, 3)),
+        ]
+        + [
+            pl.BlockSpec(part.shape, lambda r, p: (0, 0), pipeline_mode=pl.Buffered(1))
+            for part in (w_up, w_down, b_up)
         ],
-        out_specs=[own] * 5 + [big_spec] * 2 + [own] * 3 + [pl.BlockSpec((length, width), lambda r, p: (r, 0))],
-        out_shape=[act] * 5 + [big] * 2 + [act] * 3 + [jax.ShapeDtypeStruct((count, width), F32)],
+        out_specs=[own] * 5 + [big_spec] * 2 + [own] * 3 + [pl.BlockSpec((length, width), lambda r, p: (r, 0))]
+        + [pl.BlockSpec(memory_space=pl.ANY)] * 3,
+        out_shape=[act] * 5 + [big] * 2 + [act] * 3 + [jax.ShapeDtypeStruct((count, width), F32)]
+        + [jax.ShapeDtypeStruct((tensor_size,) + part.shape, part.dtype) for part in (w_up, w_down, b_up)],
         scratch_shapes=[
             pltpu.VMEM((length, length), BF16),
             pltpu.VMEM((blocks, BLK, 2 * BLK), BF16),
             pltpu.VMEM((2, length + 2 * HALO, 2 * PAIR), BF16),
+            pltpu.SemaphoreType.DMA((copies,)),
+            pltpu.SemaphoreType.DMA((copies,)),
+            pltpu.SemaphoreType.DMA((3,)),
         ],
-        compiler_params=pltpu.CompilerParams(vmem_limit_bytes=56 * 2**20),
+        compiler_params=pltpu.CompilerParams(vmem_limit_bytes=56 * 2**20, collective_id=2, has_side_effects=True),
         name="attend_forward",
-    )(tokens, seg_col, seg_pad, w_qkv, w_qkv, w_qkv, b_qkv, b_qkv, b_qkv, taps, w_out, b_out)
+    )(tokens, seg_col, seg_pad, w_qkv, w_qkv, w_qkv, vectors, vectors, vectors, taps, w_out, vectors, w_up, w_down, b_up)
+
+
+DEPTH = 4
+CORES = 2
+
+
+class Axis:
+    def __init__(self, size, place, device):
+        self.size, self.place, self.device = size, place, device
+
+    def ahead(self, j):
+        return lax.rem(self.place + j, self.size)
+
+
+def slice_axes(dp_size, tensor_size):
+    dp, tensor = lax.axis_index("dp"), lax.axis_index("tensor")
+    across = dp_size // DEPTH
+    z, x = dp // across, lax.rem(dp, across)
+    y, core = tensor // CORES, lax.rem(tensor, CORES)
+    return {
+        "core": Axis(CORES, core, lambda p: (dp, y * CORES + p)),
+        "y": Axis(tensor_size // CORES, y, lambda p: (dp, p * CORES + core)),
+        "x": Axis(across, x, lambda p: (z * across + p, tensor)),
+        "z": Axis(DEPTH, z, lambda p: (p * across + x, tensor)),
+    }
+
+
+def greet(axes, names=("core", "y", "x", "z")):
+    barrier = pltpu.get_barrier_semaphore()
+    count = 0
+    for axis in (axes[name] for name in names):
+        for j in range(1, axis.size):
+            pl.semaphore_signal(
+                barrier, inc=1, device_id=axis.device(axis.ahead(j)), device_id_type=pl.DeviceIdType.MESH
+            )
+            count += 1
+    pl.semaphore_wait(barrier, count)
+
+
+def send(source, target, sems, at, device):
+    return pltpu.make_async_remote_copy(
+        src_ref=source, dst_ref=target, send_sem=sems[0].at[at], recv_sem=sems[1].at[at],
+        device_id=device, device_id_type=pl.DeviceIdType.MESH,
+    )
+
+
+def span(start, size):
+    if isinstance(start, int):
+        return pl.ds(start, size)
+    return pl.ds(pl.multiple_of(start, math.gcd(size, 16)), size)
+
+
+def add_rows(target, target_at, terms, size):
+    tile = next(t for t in (64, 48, 32, 24, 16, 12, 8) if size % t == 0)
+
+    def one(i, carry):
+        total = None
+        for ref, start in terms:
+            rows_of = ref[span(start + i * tile, tile)].astype(F32)
+            total = rows_of if total is None else total + rows_of
+        target[span(target_at + i * tile, tile)] = total.astype(target.dtype)
+        return carry
+
+    lax.fori_loop(0, size // tile, one, 0)
+
+
+class Reduction:
+    def __init__(self, axes, order, back, source, source_at, size, final, final_at, landings, sems, first_sem=0):
+        self.axes, self.order, self.back = axes, order, back
+        self.source, self.source_at, self.size = source, source_at, size
+        self.final, self.final_at = final, final_at
+        self.landings, self.sems = landings, sems
+        self.first_sem = first_sem
+
+    def plan(self):
+        size, at, out = self.size, self.final_at, []
+        for name in self.order:
+            axis = self.axes[name]
+            size //= axis.size
+            at = at + axis.place * size
+            out.append((axis, size, at))
+        return out
+
+    def copies(self, stage):
+        stages = self.plan()
+        sem = self.first_sem
+        for axis, _, _ in stages[:stage]:
+            sem += axis.size - 1
+        axis, size, _ = stages[stage]
+        held, held_at = (self.source, self.source_at) if stage == 0 else (self.landings[stage - 1].at[0], 0)
+        return [
+            send(
+                held.at[span(held_at + axis.ahead(j) * size, size)], self.landings[stage].at[j - 1],
+                self.sems, sem + j - 1, axis.device(axis.ahead(j)),
+            )
+            for j in range(1, axis.size)
+        ]
+
+    def settle(self, stage):
+        for copy in self.copies(stage):
+            copy.wait()
+        axis, size, final_at = self.plan()[stage]
+        held, held_at = (self.source, self.source_at) if stage == 0 else (self.landings[stage - 1].at[0], 0)
+        terms = [(held, held_at + axis.place * size)]
+        terms += [(self.landings[stage].at[j - 1], 0) for j in range(1, axis.size)]
+        if stage == len(self.order) - 1:
+            add_rows(self.final, final_at, terms, size)
+        else:
+            add_rows(self.landings[stage].at[0], 0, terms, size)
+
+    def gathers(self, which):
+        stages = self.plan()
+        sem = self.first_sem + sum(axis.size - 1 for axis, _, _ in stages)
+        for name in self.back[:which]:
+            sem += self.axes[name].size - 1
+        depth = self.order.index(self.back[which])
+        axis, size, at = stages[depth]
+        block = self.final.at[span(at, size)]
+        return [send(block, block, self.sems, sem + j - 1, axis.device(axis.ahead(j))) for j in range(1, axis.size)]
+
+    def events(self):
+        out = []
+        count = len(self.order)
+
+        def begin(copies):
+            for copy in copies:
+                copy.start()
+
+        for stage in range(count):
+            def event(stage=stage):
+                if stage > 0:
+                    self.settle(stage - 1)
+                begin(self.copies(stage))
+
+            out.append(event)
+        for which in range(len(self.back)):
+            def event(which=which):
+                if which == 0:
+                    self.settle(count - 1)
+                else:
+                    for copy in self.gathers(which - 1):
+                        copy.wait()
+                begin(self.gathers(which))
+
+            out.append(event)
+
+        def last():
+            for copy in self.gathers(len(self.back) - 1):
+                copy.wait()
+
+        out.append(last)
+        return out
+
+
+def landing_shapes(order, sizes, size, columns, dtype):
+    shapes = []
+    for name in order:
+        size //= sizes[name]
+        shapes.append(pltpu.VMEM((sizes[name] - 1, size, columns), dtype))
+    return shapes
+
+
+def copies_of(order, back, sizes):
+    return sum(sizes[name] - 1 for name in order) + sum(sizes[name] - 1 for name in back)
 
 GELU_A = math.sqrt(2.0 / math.pi)
 GELU_B = 0.044715
 TILE = 256
+UNROLL = 4
 
 
 def gelu_terms(pre):
@@ -261,7 +509,7 @@
 def ffn_kernel(
     res_ref, cot_ref, ctx_ref, wo_ref, gain1_ref, shift1_ref, gain2_ref, shift2_ref, bd_ref, bu_ref, wu_ref, wd_ref,
     out_ref, dproj_ref, dctx_ref, gwo_ref, pu_ref, pd_ref, small_ref,
-    low_ref, acc_ref, hid_ref, slope_ref, dffn_ref, dpre_ref, sendu_ref, sendd_ref, recvu_ref, recvd_ref,
+    low_ref, acc_ref, hid_ref, slope_ref, dffn_ref, dpre_ref, sendu_ref, sendd_ref, recvu_ref, recvd_ref, pdown_ref, yland_ref,
     send_sem, recv_sem,
 ):
     parts = pl.num_programs(0) // 2
@@ -271,30 +519,36 @@
     tiles = count // TILE
     f = part_order(step, parts)
     late = jnp.maximum(step - parts, 0)
-    heights = parts // 2
-    slot = lax.rem(late, heights)
-    tensor = lax.axis_index("tensor")
-    mate = (lax.axis_index("dp"), tensor + 1 - 2 * lax.rem(tensor, 2))
-
-    def to_mate(which):
-        return (
-            pltpu.make_async_remote_copy(
-                src_ref=sendu_ref.at[which], dst_ref=recvu_ref.at[which],
-                send_sem=send_sem.at[0, which], recv_sem=recv_sem.at[0, which],
-                device_id=mate, device_id_type=pl.DeviceIdType.MESH,
-            ),
-            pltpu.make_async_remote_copy(
-                src_ref=sendd_ref.at[which], dst_ref=recvd_ref.at[which],
-                send_sem=send_sem.at[1, which], recv_sem=recv_sem.at[1, which],
-                device_id=mate, device_id_type=pl.DeviceIdType.MESH,
-            ),
-        )
+    heights = parts // CORES
+    slot = late // CORES
+    dp, tensor = lax.axis_index("dp"), lax.axis_index("tensor")
+    height, core = tensor // CORES, lax.rem(tensor, CORES)
+    mate = (dp, height * CORES + 1 - core)
+
+    def up_to_mate(which):
+        return send(sendu_ref.at[which], recvu_ref.at[which], (send_sem.at[0], recv_sem.at[0]), which, mate)
+
+    def down_to_mate(which):
+        return send(sendd_ref.at[which], recvd_ref.at[which], (send_sem.at[1], recv_sem.at[1]), which, mate)
+
+    def to_height(which):
+        there = (dp, lax.rem(height + 1 + which, heights) * CORES + core)
+        return send(pdown_ref.at[which], yland_ref.at[which], (send_sem.at[2], recv_sem.at[2]), which, there)
+
+    def down_part(late):
+        part = part_order(parts + late, parts)
+        piece = math.gcd(TILE, share)
+        for start in range(0, share, piece):
+            cut = slice(start, start + piece)
+            yield cut, dot_tn(hid_ref[part, :, cut], dffn_ref[...]).astype(BF16)
 
     @pl.when(step == 0)
     def _():
         barrier = pltpu.get_barrier_semaphore()
-        pl.semaphore_signal(barrier, inc=1, device_id=mate, device_id_type=pl.DeviceIdType.MESH)
-        pl.semaphore_wait(barrier, 1)
+        peers = [mate] + [(dp, lax.rem(height + j, heights) * CORES + core) for j in range(1, heights)]
+        for peer in peers:
+            pl.semaphore_signal(barrier, inc=1, device_id=peer, device_id_type=pl.DeviceIdType.MESH)
+        pl.semaphore_wait(barrier, len(peers))
 
     def put_row(row, values):
         for i in range(values.shape[1] // PAIR):
@@ -308,9 +562,10 @@
         def one(t, carry):
             unit, _ = norm_stats(res_ref[at(t)])
             low_ref[at(t)] = (unit * gain1_ref[...] + shift1_ref[...]).astype(BF16)
+            acc_ref[at(t)] = jnp.zeros((TILE, width), F32)
             return carry
 
-        lax.fori_loop(0, tiles, one, 0)
+        lax.fori_loop(0, tiles, one, 0, unroll=UNROLL)
 
     @pl.when(step < parts)
     def _():
@@ -320,19 +575,10 @@
             hidden = hidden.astype(BF16)
             hid_ref[f, at(t)] = hidden
             slope_ref[f, at(t)] = slope.astype(BF16)
-            grown = dot_nn(hidden, wd_ref[0])
-
-            @pl.when(step == 0)
-            def _():
-                acc_ref[at(t)] = grown
-
-            @pl.when(step > 0)
-            def _():
-                acc_ref[at(t)] += grown
-
+            acc_ref[at(t)] += dot_nn(hidden, wd_ref[0])
             return carry
 
-        lax.fori_loop(0, tiles, one, 0)
+        lax.fori_loop(0, tiles, one, 0, unroll=UNROLL)
 
     @pl.when(step == parts)
     def _():
@@ -353,10 +599,24 @@
             )
 
         zero = jnp.zeros((1, width), F32)
-        sums = lax.fori_loop(0, tiles, one, (zero, zero, zero))
+        sums = lax.fori_loop(0, tiles, one, (zero, zero, zero), unroll=UNROLL)
         small_ref[...] = jnp.zeros_like(small_ref)
         for i, values in enumerate(sums):
             put_row(i * (width // PAIR), values)
+
+        def theirs(which, carry):
+            for cut, values in down_part(CORES * which):
+                sendd_ref[which, cut] = values
+            down_to_mate(which).start()
+            return carry
+
+        def ours(which, carry):
+            for cut, values in down_part(CORES * which + 1):
+                pdown_ref[which, cut] = values
+            return carry
+
+        lax.fori_loop(0, heights, theirs, 0)
+        lax.fori_loop(0, heights, ours, 0)
 
     @pl.when(step >= parts)
     def _():
@@ -367,42 +627,32 @@
             acc_ref[at(t)] += dot_nt(d_pre, wu_ref[0])
             return total + column_sum(d_pre.astype(F32))
 
-        bias = lax.fori_loop(0, tiles, one, jnp.zeros((1, share), F32))
+        bias = lax.fori_loop(0, tiles, one, jnp.zeros((1, share), F32), unroll=UNROLL)
         put_row(6 * (width // PAIR) + f * (share // PAIR), bias)
 
-        def grads(store_up, store_down):
+        for which in range(heights):
+
+            @pl.when(late == which)
+            def _(which=which):
+                down_to_mate(which).wait()
+                add_rows(pdown_ref.at[which], 0, [(pdown_ref.at[which], 0), (recvd_ref.at[which], 0)], share)
+                if which < heights - 1:
+                    to_height(which).start()
+
+        @pl.when(lax.rem(late, CORES) == 0)
+        def _():
             for start in range(0, width, TILE):
                 cut = slice(start, start + TILE)
-                store_up(cut, dot_tn(low_ref[:, cut], dpre_ref[...]))
-            piece = math.gcd(TILE, share)
-            for start in range(0, share, piece):
-                cut = slice(start, start + piece)
-                store_down(cut, dot_tn(hid_ref[f, :, cut], dffn_ref[...]))
-
-        @pl.when(late < heights)
+                sendu_ref[slot, cut] = dot_tn(low_ref[:, cut], dpre_ref[...]).astype(BF16)
+            up_to_mate(slot).start()
+
+        @pl.when(lax.rem(late, CORES) == 1)
         def _():
-            def up(cut, values):
-                sendu_ref[slot, cut] = values.astype(BF16)
-
-            def down(cut, values):
-                sendd_ref[slot, cut] = values.astype(BF16)
-
-            grads(up, down)
-            for copy in to_mate(slot):
-                copy.start()
-
-        @pl.when(late >= heights)
-        def _():
-            for copy in to_mate(slot):
-                copy.wait()
-
-            def up(cut, values):
+            up_to_mate(slot).wait()
+            for start in range(0, width, TILE):
+                cut = slice(start, start + TILE)
+                values = dot_tn(low_ref[:, cut], dpre_ref[...])
                 pu_ref[slot, cut] = (values + recvu_ref[slot, cut].astype(F32)).astype(BF16)
-
-            def down(cut, values):
-                pd_ref[slot, cut] = (values + recvd_ref[slot, cut].astype(F32)).astype(BF16)
-
-            grads(up, down)
 
     @pl.when(step == 2 * parts - 1)
     def _():
@@ -419,26 +669,29 @@
             )
 
         zero = jnp.zeros((1, width), F32)
-        sums = lax.fori_loop(0, tiles, one, (zero, zero, zero))
+        sums = lax.fori_loop(0, tiles, one, (zero, zero, zero), unroll=UNROLL)
         for i, values in enumerate(sums):
             put_row((3 + i) * (width // PAIR), values)
         for start in range(0, width, TILE):
             values = dot_tn(ctx_ref[:, start : start + TILE], dproj_ref[...]).astype(BF16)
             gwo_ref[start : start + TILE] = values[:, : width // 2]
             gwo_ref[width + start : width + start + TILE] = values[:, width // 2 :]
+        for which in range(heights - 1):
+            to_height(which).wait()
+        terms = [(pdown_ref.at[heights - 1], 0)] + [(yland_ref.at[which], 0) for which in range(heights - 1)]
+        add_rows(pd_ref, 0, terms, share)
 
 
 def part_order(step, parts):
     tensor = lax.axis_index("tensor")
-    height, core = tensor // 2, lax.rem(tensor, 2)
-    heights = parts // 2
+    height, core = tensor // CORES, lax.rem(tensor, CORES)
     late = jnp.maximum(step - parts, 0)
-    there = lax.rem(height + 1 + lax.rem(late, heights), heights)
-    whose = jnp.where(late < heights, 1 - core, core)
-    return jnp.where(step < parts, step, there * 2 + whose)
-
-
-def feed_forward(res, cot, ctx, w_out, gain1, shift1, gain2, shift2, b_down, b_up, w_up, w_down):
+    there = lax.rem(height + 1 + late // CORES, parts // CORES)
+    whose = jnp.where(lax.rem(late, CORES) == 0, 1 - core, core)
+    return jnp.where(step < parts, step, there * CORES + whose)
+
+
+def feed_forward(res, cot, ctx, w_out, vectors, b_up, w_up, w_down):
     count, width = res.shape
     parts, _, share = w_up.shape
     heights = parts // 2
@@ -457,15 +710,15 @@
         grid=(2 * parts,),
         in_specs=[whole(count, width)] * 3
         + [whole(width, width)]
-        + [whole(1, width)] * 5
+        + [pl.BlockSpec((1, width), lambda s, k=k: (0, k), pipeline_mode=pl.Buffered(1)) for k in range(4, 9)]
         + [per_part(1, share), per_part(width, share), per_part(share, width)],
         out_specs=[whole(count, width)] * 3
-        + [whole(2 * width, width // 2), whole(heights, width, share), whole(heights, share, width), whole(smalls, PAIR)],
+        + [whole(2 * width, width // 2), whole(heights, width, share), whole(share, width), whole(smalls, PAIR)],
         out_shape=[act] * 3
         + [
             jax.ShapeDtypeStruct((2 * width, width // 2), BF16),
             jax.ShapeDtypeStruct((heights, width, share), BF16),
-            jax.ShapeDtypeStruct((heights, share, width), BF16),
+            jax.ShapeDtypeStruct((share, width), BF16),
             jax.ShapeDtypeStruct((smalls, PAIR), F32),
         ],
         scratch_shapes=[
@@ -479,183 +732,21 @@
             pltpu.VMEM((heights, share, width), BF16),
             pltpu.VMEM((heights, width, share), BF16),
             pltpu.VMEM((heights, share, width), BF16),
-            pltpu.SemaphoreType.DMA((2, heights)),
-            pltpu.SemaphoreType.DMA((2, heights)),
+            pltpu.VMEM((heights, share, width), BF16),
+            pltpu.VMEM((heights - 1, share, width), BF16),
+            pltpu.SemaphoreType.DMA((3, heights)),
+            pltpu.SemaphoreType.DMA((3, heights)),
         ],
         compiler_params=pltpu.CompilerParams(vmem_limit_bytes=60 * 2**20, collective_id=0, has_side_effects=True),
         name="feed_forward",
-    )(res, cot, ctx, w_out, gain1, shift1, gain2, shift2, b_down, b_up, w_up, w_down)
-
-
-DEPTH = 4
-CORES = 2
-
-
-class Axis:
-    def __init__(self, size, place, device):
-        self.size, self.place, self.device = size, place, device
-
-    def ahead(self, j):
-        return lax.rem(self.place + j, self.size)
-
-
-def slice_axes(dp_size, tensor_size):
-    dp, tensor = lax.axis_index("dp"), lax.axis_index("tensor")
-    across = dp_size // DEPTH
-    z, x = dp // across, lax.rem(dp, across)
-    y, core = tensor // CORES, lax.rem(tensor, CORES)
-    return {
-        "core": Axis(CORES, core, lambda p: (dp, y * CORES + p)),
-        "y": Axis(tensor_size // CORES, y, lambda p: (dp, p * CORES + core)),
-        "x": Axis(across, x, lambda p: (z * across + p, tensor)),
-        "z": Axis(DEPTH, z, lambda p: (p * across + x, tensor)),
-    }
-
-
-def greet(axes):
-    barrier = pltpu.get_barrier_semaphore()
-    count = 0
-    for axis in axes.values():
-        for j in range(1, axis.size):
-            pl.semaphore_signal(
-                barrier, inc=1, device_id=axis.device(axis.ahead(j)), device_id_type=pl.DeviceIdType.MESH
-            )
-            count += 1
-    pl.semaphore_wait(barrier, count)
-
-
-def send(source, target, sems, at, device):
-    return pltpu.make_async_remote_copy(
-        src_ref=source, dst_ref=target, send_sem=sems[0].at[at], recv_sem=sems[1].at[at],
-        device_id=device, device_id_type=pl.DeviceIdType.MESH,
-    )
-
-
-def span(start, size):
-    if isinstance(start, int):
-        return pl.ds(start, size)
-    return pl.ds(pl.multiple_of(start, math.gcd(size, 16)), size)
-
-
-def add_rows(target, target_at, terms, size):
-    tile = next(t for t in (64, 48, 32, 24, 16, 12, 8) if size % t == 0)
-
-    def one(i, carry):
-        total = None
-        for ref, start in terms:
-            rows_of = ref[span(start + i * tile, tile)].astype(F32)
-            total = rows_of if total is None else total + rows_of
-        target[span(target_at + i * tile, tile)] = total.astype(target.dtype)
-        return carry
-
-    lax.fori_loop(0, size // tile, one, 0)
-
-
-class Reduction:
-    def __init__(self, axes, order, back, source, source_at, size, final, final_at, landings, sems, first_sem=0):
-        self.axes, self.order, self.back = axes, order, back
-        self.source, self.source_at, self.size = source, source_at, size
-        self.final, self.final_at = final, final_at
-        self.landings, self.sems = landings, sems
-        self.first_sem = first_sem
-
-    def plan(self):
-        size, at, out = self.size, self.final_at, []
-        for name in self.order:
-            axis = self.axes[name]
-            size //= axis.size
-            at = at + axis.place * size
-            out.append((axis, size, at))
-        return out
-
-    def copies(self, stage):
-        stages = self.plan()
-        sem = self.first_sem
-        for axis, _, _ in stages[:stage]:
-            sem += axis.size - 1
-        axis, size, _ = stages[stage]
-        held, held_at = (self.source, self.source_at) if stage == 0 else (self.landings[stage - 1].at[0], 0)
-        return [
-            send(
-                held.at[span(held_at + axis.ahead(j) * size, size)], self.landings[stage].at[j - 1],
-                self.sems, sem + j - 1, axis.device(axis.ahead(j)),
-            )
-            for j in range(1, axis.size)
-        ]
-
-    def settle(self, stage):
-        for copy in self.copies(stage):
-            copy.wait()
-        axis, size, final_at = self.plan()[stage]
-        held, held_at = (self.source, self.source_at) if stage == 0 else (self.landings[stage - 1].at[0], 0)
-        terms = [(held, held_at + axis.place * size)]
-        terms += [(self.landings[stage].at[j - 1], 0) for j in range(1, axis.size)]
-        if stage == len(self.order) - 1:
-            add_rows(self.final, final_at, terms, size)
-        else:
-            add_rows(self.landings[stage].at[0], 0, terms, size)
-
-    def gathers(self, which):
-        stages = self.plan()
-        sem = self.first_sem + sum(axis.size - 1 for axis, _, _ in stages)
-        for name in self.back[:which]:
-            sem += self.axes[name].size - 1
-        depth = self.order.index(self.back[which])
-        axis, size, at = stages[depth]
-        block = self.final.at[span(at, size)]
-        return [send(block, block, self.sems, sem + j - 1, axis.device(axis.ahead(j))) for j in range(1, axis.size)]
-
-    def events(self):
-        out = []
-        count = len(self.order)
-
-        def begin(copies):
-            for copy in copies:
-                copy.start()
-
-        for stage in range(count):
-            def event(stage=stage):
-                if stage > 0:
-                    self.settle(stage - 1)
-                begin(self.copies(stage))
-
-            out.append(event)
-        for which in range(len(self.back)):
-            def event(which=which):
-                if which == 0:
-                    self.settle(count - 1)
-                else:
-                    for copy in self.gathers(which - 1):
-                        copy.wait()
-                begin(self.gathers(which))
-
-            out.append(event)
-
-        def last():
-            for copy in self.gathers(len(self.back) - 1):
-                copy.wait()
-
-        out.append(last)
-        return out
-
-
-def landing_shapes(order, sizes, size, columns, dtype):
-    shapes = []
-    for name in order:
-        size //= sizes[name]
-        shapes.append(pltpu.VMEM((sizes[name] - 1, size, columns), dtype))
-    return shapes
-
-
-def copies_of(order, back, sizes):
-    return sum(sizes[name] - 1 for name in order) + sum(sizes[name] - 1 for name in back)
+    )(res, cot, ctx, w_out, *[vectors] * 5, b_up, w_up, w_down)
 
 
 def attend_back_kernel(
     dctx_ref, att_ref, inv_ref, q_ref, k_ref, v_ref, sq_ref, sk_ref, w_ref, s_ref, x_ref, col_ref, pad_ref,
-    wq_ref, wk_ref, wv_ref, flip_ref, dproj_ref, gwo_ref, pu_ref, pd_ref, small_ref,
+    wqkv_ref, flip_ref, dproj_ref, gwo_ref, pu_ref, pd_ref, small_ref,
     gt_ref, all_out, up_out, down_out, few_out,
-    near_ref, vv_ref, dpad_ref, dcos_ref, dq_ref, dk_ref, dv_ref, joined_ref, gwacc_ref, gtacc_ref, conv_ref,
+    near_ref, vv_ref, dpad_ref, dcos_ref, dq_ref, dk_ref, dv_ref, joined_ref, gwacc_ref, conv_ref,
     gwlow_ref, gb_ref, mini_ref, all_ref, up_ref, down_ref, few_ref, out_sem, *links,
     plan, quads, seqs,
 ):
@@ -668,7 +759,7 @@
     axes = slice_axes(dp_size, tensor_size)
     ticks = schedule(axes, sizes, quads, seqs, gwo_ref, pu_ref, pd_ref, gwlow_ref, mini_ref, all_ref, up_ref, down_ref, few_ref, links,
         (all_out, up_out, down_out, few_out, out_sem))
-    calls = quads * seqs * (QUAD // PAIR)
+    calls = quads * seqs * (QUAD // HEAD)
 
     build_near(col_ref[...], pad_ref[0], near_ref)
     for half in range(2):
@@ -693,15 +784,6 @@
             gwlow_ref[:, filled:] = jnp.zeros((quads, gwlow_ref.shape[1] - filled, gwlow_ref.shape[2]), BF16)
 
     def one_pair(pair, carry):
-        tick = (quad * seqs + row) * (QUAD // PAIR) + pair
-        for when in range(calls):
-            if ticks.get(when):
-
-                @pl.when(tick == when)
-                def _(when=when):
-                    for event in ticks[when]:
-                        event()
-
         at = pl.ds(pl.multiple_of(pair * PAIR, PAIR), PAIR)
         inverse = inv_ref[:, at].astype(F32)
         d_ctx = dctx_ref[:, at]
@@ -710,7 +792,16 @@
         both = jnp.concatenate([d_summed, d_total], 1)
         dk = jnp.zeros((length, PAIR), F32)
         dv = jnp.zeros((length, PAIR), F32)
+        turn = (quad * seqs + row) * (QUAD // PAIR) + pair
         for half in range(2):
+            for when in range(half, calls, 2):
+                if ticks.get(when):
+
+                    @pl.when(turn == when // 2)
+                    def _(when=when):
+                        for event in ticks[when]:
+                            event()
+
             head = pair * 2 + half
             mask = head_mask(half, (length, PAIR))
             vv_ref[half, inside, :PAIR] = v_ref[:, at] * mask
@@ -750,16 +841,16 @@
         unit = k_ref[:, at].astype(F32)
         d_key = sk_ref[:, at].astype(F32) * (grad - unit * head_sum(grad * unit))
         for part, values in enumerate((d_query, d_key, dv_ref[...])):
-            joined_ref[:, pl.ds(pl.multiple_of(part * QUAD + pair * PAIR, PAIR), PAIR)] = values.astype(BF16)
+            joined_ref[quad, row, :, pl.ds(pl.multiple_of(part * QUAD + pair * PAIR, PAIR), PAIR)] = values.astype(BF16)
         return carry
 
     lax.fori_loop(0, QUAD // PAIR, one_pair, 0)
 
-    gb_ref[quad, :1] += column_sum(joined_ref[...].astype(F32))
+    gb_ref[quad, :1] += column_sum(joined_ref[quad, row].astype(F32))
     width = gwacc_ref.shape[0]
     for start in range(0, width, TILE):
         cut = slice(start, start + TILE)
-        gwacc_ref[cut] += dot_tn(x_ref[:, cut], joined_ref[...])
+        gwacc_ref[cut] += dot_tn(x_ref[:, cut], joined_ref[quad, row])
 
     @pl.when(row == seqs - 1)
     def _():
@@ -785,29 +876,19 @@
 
     @pl.when(last)
     def _():
-        for event in ticks[calls]:
+        for event in ticks.get(calls, ()):
             event()
 
-    for start in range(0, length, TILE):
-        here = pl.ds(pl.multiple_of(row * length + start, TILE), TILE)
-        cut = slice(start, start + TILE)
-        grown = (
-            dot_nt(joined_ref[cut, :QUAD], wq_ref[...])
-            + dot_nt(joined_ref[cut, QUAD : 2 * QUAD], wk_ref[...])
-            + dot_nt(joined_ref[cut, 2 * QUAD :], wv_ref[...])
-        )
-
-        @pl.when(quad == 0)
-        def _():
-            gtacc_ref[here] = grown + dproj_ref[cut].astype(F32)
-
-        @pl.when(quad > 0)
-        def _():
-            gtacc_ref[here] += grown
-
     @pl.when(quad == quads - 1)
     def _():
-        gt_ref[...] = gtacc_ref[pl.ds(pl.multiple_of(row * length, TILE), length)].astype(BF16)
+        for start in range(0, length, TILE):
+            cut = slice(start, start + TILE)
+            grown = dproj_ref[cut].astype(F32)
+            for q in range(quads):
+                for part in range(3):
+                    to = part * width + q * QUAD
+                    grown += dot_nt(joined_ref[q, row, cut, part * QUAD : (part + 1) * QUAD], wqkv_ref[:, to : to + QUAD])
+            gt_ref[cut] = grown.astype(BF16)
 
     @pl.when(last)
     def _():
@@ -817,14 +898,26 @@
                     event()
 
 
+FFN_TIMES = (
+    ((3, 7, 14, 21, 34), (0, 4, 8, 16, 25)),
+    ((0, 8, 12, 20, 37, 50), (5, 17, 29, 48, 57, 61)),
+)
+ALL_TIMES = (
+    (6, 8, 15, 19, 26, 39, 47, 52, 56),
+    (10, 12, 16, 19, 27, 40, 46, 53, 58),
+    (16, 18, 22, 32, 44, 51, 55, 60, 62),
+    (25, 30, 36, 42, 49, 54, 59, 63, 64),
+)
+MINI_TIMES = (25, 28, 31, 33, 35, 38, 41, 43, 45)
 FFN_ROWS = 384
 FFN_ORDER = ("y", "x", "z")
 FFN_BACK = ("z", "x")
 ORDERS = (("core", "x", "y", "z"), ("core", "y", "x", "z"))
+CHOICE = (1, 0, 1, 1)
 
 
 def all_order(index):
-    order = ORDERS[index % 2]
+    order = ORDERS[CHOICE[index]]
     return order, order[::-1]
 
 
@@ -866,11 +959,11 @@
     out = []
     devices = math.prod(sizes.values())
     y = sizes["y"]
-    for height, columns in ((width, share), (share, width)):
+    for height, columns, order in ((share, width, FFN_ORDER[1:]), (width, share, FFN_ORDER)):
         for _ in range(height // FFN_ROWS):
-            shapes = [pltpu.VMEM((y - 1, FFN_ROWS, columns), BF16)]
+            shapes = [pltpu.VMEM((y - 1, FFN_ROWS, columns), BF16)] if order is FFN_ORDER else []
             shapes += landing_shapes(FFN_ORDER[1:], sizes, FFN_ROWS, columns, BF16)
-            out.append((shapes, copies_of(FFN_ORDER, FFN_BACK, sizes)))
+            out.append((shapes, copies_of(order, FFN_BACK, sizes)))
     for index in range(quads + 1):
         order, back = all_order(index)
         out.append((landing_shapes(order, sizes, padded(2 * width, devices), width // 2, BF16), copies_of(order, back, sizes)))
@@ -885,9 +978,8 @@
 
 def schedule(axes, sizes, quads, seqs, gwo_ref, pu_ref, pd_ref, gwlow_ref, mini_ref, all_ref, up_ref, down_ref, few_ref, links, outs):
     all_out, up_out, down_out, few_out, out_sem = outs
-    calls = quads * seqs * (QUAD // PAIR)
-    per_quad = seqs * (QUAD // PAIR)
-    width, share = pu_ref.shape[1], pu_ref.shape[2]
+    calls = quads * seqs * (QUAD // HEAD)
+    share, width = pd_ref.shape
     devices = math.prod(sizes.values())
     groups = link_plan(sizes, width, share, quads)
     taken, position = [], 0
@@ -906,14 +998,16 @@
         stores.append(store)
 
     number = 0
-    begin = (0, 0, 3, 6)
-    for source, final, place in ((pu_ref, up_ref, up_out), (pd_ref, down_ref, down_out)):
-        for start in range(0, source.shape[1], FFN_ROWS):
+    for source, final, place in ((pd_ref, down_ref, down_out), (pu_ref, up_ref, up_out)):
+        for start in range(0, final.shape[0], FFN_ROWS):
             landings, sems = taken[number]
-            reduction = FfnReduction(axes, FFN_ORDER, FFN_BACK, source, start, FFN_ROWS, final, start, landings, sems)
-            done = 3 * (number + 1)
-            enlist(reduction, (begin[number], done, done + 2, done + 4, done + 6, done + 8),
-                   final.at[span(start, FFN_ROWS)], place.at[span(start, FFN_ROWS)])
+            block = span(start, FFN_ROWS)
+            if source is pd_ref:
+                reduction = Reduction(axes, FFN_ORDER[1:], FFN_BACK, source, start, FFN_ROWS, final, start, landings, sems)
+            else:
+                reduction = FfnReduction(axes, FFN_ORDER, FFN_BACK, source, start, FFN_ROWS, final, start, landings, sems)
+            times = FFN_TIMES[source is pu_ref][start // FFN_ROWS]
+            enlist(reduction, times, final.at[block], place.at[block])
             number += 1
     size = padded(2 * width, devices)
     for index in range(quads + 1):
@@ -921,14 +1015,12 @@
         order, back = all_order(index)
         source = gwo_ref if index == 0 else gwlow_ref.at[index - 1]
         reduction = Reduction(axes, order, back, source, 0, size, all_ref.at[index], 0, landings, sems)
-        first = index * per_quad
-        enlist(reduction, (first, first + 1, first + 3, first + 5, first + 6, first + 7, first + 9, first + 11, first + 12),
-               all_ref.at[index], all_out.at[index])
+        enlist(reduction, ALL_TIMES[index], all_ref.at[index], all_out.at[index])
         number += 1
     landings, sems = taken[number]
     order, back = all_order(quads)
     reduction = Reduction(axes, order, back, mini_ref, 0, 8 * devices, few_ref, 0, landings, sems)
-    enlist(reduction, (calls, calls + 1, calls + 3, calls + 5, calls + 6, calls + 7, calls + 9, calls + 11, calls + 12), few_ref, few_out)
+    enlist(reduction, MINI_TIMES, few_ref, few_out)
     ticks[max(ticks) + 1] = [store.wait for store in stores]
     return ticks
 
@@ -943,12 +1035,9 @@
     big = pl.BlockSpec((1, per, length, length), lambda p, r: (r, p, 0, 0))
     wide = pl.BlockSpec((length, width), lambda p, r: (r, 0))
 
-    def part(k):
-        return pl.BlockSpec((width, QUAD), lambda p, r, k=k: (0, p + k * quads))
-
     sizes = {"core": CORES, "y": tensor_size // CORES, "x": dp_size // DEPTH, "z": DEPTH}
     devices = dp_size * tensor_size
-    share = pu.shape[2]
+    share = pd.shape[0]
     grown = padded(2 * width, devices)
     gwo = jnp.pad(gwo, ((0, grown - gwo.shape[0]), (0, 0)))
     minis = 8 * devices
@@ -969,7 +1058,7 @@
             wide,
             pl.BlockSpec((length, 1), lambda p, r: (r, 0)),
             pl.BlockSpec((1, 1, length + 2 * HALO), lambda p, r: (r, 0, 0)),
-            part(0), part(1), part(2),
+            whole(width, 3 * width),
             taps_spec,
             wide,
             whole(*gwo.shape), whole(*pu.shape), whole(*pd.shape), whole(*small.shape),
@@ -993,9 +1082,8 @@
             pltpu.VMEM((length, PAIR), F32),
             pltpu.VMEM((length, PAIR), F32),
             pltpu.VMEM((length, PAIR), F32),
-            pltpu.VMEM((length, 3 * QUAD), BF16),
+            pltpu.VMEM((quads, seqs, length, 3 * QUAD), BF16),
             pltpu.VMEM((width, 3 * QUAD), F32),
-            pltpu.VMEM((count, width), F32),
             pltpu.VMEM((per, BLK, 2 * BLK), F32),
             pltpu.VMEM((quads, grown, width // 2), BF16),
             pltpu.VMEM((quads, 8, 3 * QUAD), F32),
@@ -1009,7 +1097,93 @@
         + scratch,
         compiler_params=pltpu.CompilerParams(vmem_limit_bytes=60 * 2**20, collective_id=1, has_side_effects=True),
         name="attend_backward",
-    )(dctx, att, inv, q, k, v, sq, sk, weight, slope, tokens, seg_col, seg_pad, w_qkv, w_qkv, w_qkv, flipped, dproj, gwo, pu, pd, small)
+    )(dctx, att, inv, q, k, v, sq, sk, weight, slope, tokens, seg_col, seg_pad, w_qkv, flipped, dproj, gwo, pu, pd, small)
+
+
+def spread_kernel(low_ref, high_ref, up_ref, down_ref, few_ref, gw_ref, gwo_ref, gup_ref, gdown_ref, *vectors, first_lane, base):
+    width = gwo_ref.shape[1]
+    half = width // 2
+    quads = low_ref.shape[0] - 1
+    gwo_ref[:, :half] = low_ref[0].astype(F32)
+    gwo_ref[:, half:] = high_ref[0].astype(F32)
+    for quad in range(quads):
+        for part in range(3):
+            for start in range(part * QUAD, (part + 1) * QUAD, PAIR):
+                side, lane = (low_ref, start) if start < half else (high_ref, start - half)
+                to = part * width + quad * QUAD + start - part * QUAD
+                gw_ref[:, to : to + PAIR] = side[1 + quad, :, lane : lane + PAIR].astype(F32)
+    gup_ref[...] = up_ref[...].astype(F32)
+    gdown_ref[...] = down_ref[...].astype(F32)
+
+    @pl.when(pl.program_id(0) == 0)
+    def _():
+        gb_ref, conv_ref, *six, gbu_ref = vectors
+        lines = width // PAIR
+
+        def copy_line(target, to, line):
+            target[:, to * PAIR : (to + 1) * PAIR] = few_ref[pl.ds(line, 1)]
+
+        for number, target in enumerate(six):
+            for i in range(lines):
+                copy_line(target, i, number * lines + i)
+        share = gbu_ref.shape[1] // PAIR
+        mine = lax.axis_index("tensor") * share
+        for i in range(share):
+            copy_line(gbu_ref, i, 6 * lines + mine + i)
+        per = QUAD // PAIR
+        for quad in range(quads):
+            for part in range(3):
+                for i in range(per):
+                    copy_line(gb_ref, (part * width + quad * QUAD) // PAIR + i, base + (quad * 3 + part) * per + i)
+        heads, taps = conv_ref.shape
+        kept = few_ref[base + 3 * lines : base + 3 * lines + heads]
+        conv_ref[...] = pltpu.roll(kept, PAIR - first_lane, 1)[:, :taps]
+
+
+def spread_out(grads, up, down, few, width, heads, taps, first_lane, base):
+    chunks = grads.shape[0]
+    quads = chunks - 1
+    steps = 6
+    rows_of = width // steps
+    share = up.shape[1]
+    down_rows = share // steps
+
+    def whole(*shape):
+        return pl.BlockSpec(shape, lambda s: (0,) * len(shape))
+
+    def by_rows(count, columns):
+        return pl.BlockSpec((count, columns), lambda s: (s, 0))
+
+    row = jax.ShapeDtypeStruct((1, width), F32)
+    return pl.pallas_call(
+        functools.partial(spread_kernel, first_lane=first_lane, base=base),
+        grid=(steps,),
+        in_specs=[
+            pl.BlockSpec((chunks, rows_of, width // 2), lambda s: (0, s, 0)),
+            pl.BlockSpec((chunks, rows_of, width // 2), lambda s: (0, steps + s, 0)),
+            by_rows(rows_of, share),
+            by_rows(down_rows, width),
+            whole(*few.shape),
+        ],
+        out_specs=[
+            by_rows(rows_of, 3 * width), by_rows(rows_of, width), by_rows(rows_of, share), by_rows(down_rows, width),
+            whole(1, 3 * width), whole(heads, taps),
+        ]
+        + [whole(1, width)] * 6
+        + [whole(1, share)],
+        out_shape=[
+            jax.ShapeDtypeStruct((width, 3 * width), F32),
+            jax.ShapeDtypeStruct((width, width), F32),
+            jax.ShapeDtypeStruct((width, share), F32),
+            jax.ShapeDtypeStruct((share, width), F32),
+            jax.ShapeDtypeStruct((1, 3 * width), F32),
+            jax.ShapeDtypeStruct((heads, taps), F32),
+        ]
+        + [row] * 6
+        + [jax.ShapeDtypeStruct((1, share), F32)],
+        compiler_params=pltpu.CompilerParams(vmem_limit_bytes=40 * 2**20),
+        name="spread_out",
+    )(grads, grads, up, down, few)
 
 
 def body(
@@ -1031,40 +1205,25 @@
     seg_pad = jnp.pad(segment_ids, ((0, 0), (HALO, HALO)), constant_values=-1)[:, None, :]
     taps, flipped = spread(conv_kernel), spread(conv_kernel[:, ::-1])
 
-    up_all = lax.all_gather(w_up, "tensor")
-    down_all = lax.all_gather(w_down, "tensor")
-    bias_all = lax.all_gather(b_up, "tensor")[:, None, :]
     dp_size, tensor_size = lax.axis_size("dp"), lax.axis_size("tensor")
-    share = w_up.shape[1]
-
-    q, k, v, sq, sk, weight, slope, att, inv, ctx, res = attend(
-        tokens, seg_col, seg_pad, w_qkv, b_qkv[None], taps, w_out, b_out[None], length
+    vectors = jnp.concatenate([b_qkv, b_out, norm1_gain, norm1_bias, norm2_gain, norm2_bias, b_down])[None]
+
+    q, k, v, sq, sk, weight, slope, att, inv, ctx, res, up_all, down_all, bias_all = attend(
+        tokens, seg_col, seg_pad, w_qkv, vectors, taps, w_out, w_up, w_down, b_up.astype(F32)[None],
+        dp_size, tensor_size, length,
     )
-    out, dproj, dctx, gwo, pu, pd, small = feed_forward(
-        res, cotangent, ctx, w_out, norm1_gain[None], norm1_bias[None], norm2_gain[None], norm2_bias[None],
-        b_down[None], bias_all, up_all, down_all,
-    )
+    out, dproj, dctx, gwo, pu, pd, small = feed_forward(res, cotangent, ctx, w_out, vectors, bias_all, up_all, down_all)
     gt, grads, grad_up, grad_down, few = attend_back(
         dctx, att, inv, q, k, v, sq, sk, weight, slope, tokens, seg_col, seg_pad, w_qkv, flipped, dproj,
         gwo, pu, pd, small, dp_size, tensor_size, length,
     )
-    quads = width // QUAD
-    grads = grads[:, : 2 * width].astype(F32).reshape(quads + 1, 2, width, width // 2).transpose(0, 2, 1, 3)
-    grads = grads.reshape(quads + 1, width, width)
-    gwo = grads[0]
-    gw = grads[1:].reshape(quads, width, 3, QUAD).transpose(1, 2, 0, 3).reshape(width, 3 * width)
-    lines = width // PAIR
-    gg2, gs2, gbd, gg1, gs1, gbo = few[: 6 * lines].reshape(6, width)
-    gbu = few[6 * lines : 6 * lines + tensor_size * share // PAIR].reshape(tensor_size, share)
-    grad_b_up = lax.dynamic_index_in_dim(gbu, lax.axis_index("tensor"), 0, False)
-    base = small.shape[0]
-    gb = few[base : base + 3 * lines].reshape(quads, 3, QUAD).transpose(1, 0, 2).reshape(3 * width)
-    base += 3 * lines
     first_lane = (first_tap + BLK - 1 + BLK) % (2 * BLK)
-    grad_conv = few[base : base + heads, first_lane : first_lane + span_of]
+    gw, gwo, grad_up, grad_down, gb, grad_conv, gg2, gs2, gbd, gg1, gs1, gbo, gbu = spread_out(
+        grads, grad_up, grad_down, few, width, heads, span_of, first_lane, small.shape[0]
+    )
     return (
-        out, gt, gw, gb, grad_conv, gwo, gbo, gg1, gs1,
-        grad_up.astype(F32), grad_b_up, grad_down.astype(F32), gbd, gg2, gs2,
+        out, gt, gw, gb[0], grad_conv, gwo, gbo[0], gg1[0], gs1[0],
+        grad_up, gbu[0], grad_down, gbd[0], gg2[0], gs2[0],
     )
 
 

time: 359 us -> 291 us (0.81)
  local copies, waits for them, and re-layouts: 42.5 us -> 20.9 us
  Pallas kernels: 281 us -> 264 us
  between operations: 14.2 us -> 0.71 us
  waiting for transfers between devices: 10.3 us -> 0 us
  blocking collectives: 7.16 us -> 0 us
    pallas_call x1, Pallas kernels: 159 us -> 131 us  [attend_back(): pl.pallas_call(functools.partial(attend_back_kernel, plan=(None, sizes, d...]
    pallas_call x1 -> x2, Pallas kernels: 56.8 us -> 67.6 us  [the longest x1 61.9 us: attend(): pl.pallas_call(functools.partial(attend_kernel, dp_size=dp_size, tensor_s...]
    transpose x2 -> x0, local copies, waits for them, and re-layouts: 10.7 us -> none  [the longest x1 7.38 us: body(): grads[:, :2 * width].astype(F32).reshape(quads + 1, 2, width, width // 2)]
    all_gather x2 -> x0, waiting for transfers between devices: 8.95 us -> none  [the longest x1 8.94 us: body(): down_all = lax.all_gather(w_down, 'tensor')]
    slice x5 -> x0, local copies, waits for them, and re-layouts: 8.69 us -> none  [the longest x1 3.46 us: body(): grads[1:].reshape(quads, width, 3, QUAD).transpose(1, 2, 0, 3)]
    all_gather x1 -> x0, blocking collectives: 7.16 us -> none  [body(): bias_all = lax.all_gather(b_up, 'tensor')[:, None, :]]
    pallas_call x0 -> x8, other arithmetic: none -> 4.86 us  [spread_out(): pl.pallas_call(functools.partial(spread_kernel, first_lane=first_lane, ba...]
    unnamed x37 -> x24, local copies, waits for them, and re-layouts: 14.2 us -> 14.8 us
  transfers between devices with their start and end apart: 2 -> 0, of which waited for: 1 -> 0; matrix products, arithmetic and copies ran while one was open for 2% -> 0% of each run, Pallas kernels for 16% -> 0%
where the time goes in v3:
time: 291 us; the launch traced here: 290 us
  Pallas kernels  264 us (91%)
  local copies, waits for them, and re-layouts  20.9 us (7%)
  other arithmetic  4.86 us (2%)
    pallas_call x1, Pallas kernels, attend_back(): pl.pallas_call(functools.partial(attend_back_kernel, plan=(None, sizes, d...  131 us
    pallas_call x1, Pallas kernels, feed_forward(): pl.pallas_call(ffn_kernel, grid=(2 * parts,), in_specs=[whole(count, widt...  65.4 us
    pallas_call x1, Pallas kernels, attend(): pl.pallas_call(functools.partial(attend_kernel, dp_size=dp_size, tensor_s...  61.9 us
    unnamed x24, local copies, waits for them, and re-layouts  14.8 us

profile of v3, /device:TPU:0, one launch (start us, length us, event | category | flops | bytes accessed | tf_op | source)
XLA Modules:
  0.0 290.4 jit_solution(7698572492625281802)
XLA Ops:
  0.6 0.7 copy.33
  1.3 1.0 copy.34
  2.4 0.7 constant_dynamic-update-slice_fusion.6
  3.1 0.7 constant_dynamic-update-slice_fusion.5
  3.8 0.7 constant_dynamic-update-slice_fusion.4
  4.5 0.7 constant_dynamic-update-slice_fusion.3
  5.2 0.7 constant_dynamic-update-slice_fusion.2
  5.9 0.7 constant_dynamic-update-slice_fusion.1
  6.5 0.7 constant_dynamic-update-slice_fusion
  7.2 0.6 broadcast_in_dim.12.bq_ref.bk_ref.bv_ref.bo_ref.gain1_ref.shift1_ref.gain2_ref.shift2_ref.bd_ref
  7.9 0.8 pad.11
  9.2 0.8 pad.12
  10.0 0.6 reshape.40.tap_ref
  10.6 1.3 reshape.42.bu_ref
  11.9 61.9 %attend_forward.1 = (bf16[1024,768]{1,0:T(8,128)(2,1)}, bf16[1024,768]{1,0:T(8,128)(2,1)}, bf16[1024,768]{1,0:T(8,128)(2,1)}, bf16[1024,768]{1,0:T(8,128)(2,1)},...) custom-call(bf16[1024,768]{1,0:T(8,128)(2,1)} %x_ref.3, ...), custom_call_target="tpu_custom_call" | custom-call | tf_op jit(solution)/shard_map/attend_forward/pallas_call | solution.py:285
  73.8 65.4 %feed_forward.1 = (bf16[1024,768]{1,0:T(8,128)(2,1)}, bf16[1024,768]{1,0:T(8,128)(2,1)}, bf16[1024,768]{1,0:T(8,128)(2,1)}, bf16[1536,384]{1,0:T(8,128)(2,1)}, b...) custom-call(f32[1024,768]{1,0:T(8,128)} %get-tuple-element.54.res_ref, ...), custom_call_target="tpu_custom_call" | custom-call | tf_op jit(solution)/shard_map/feed_forward/pallas_call | solution.py:708
  139.3 0.6 reshape.41.flip_ref
  139.9 131.0 %attend_backward.1 = (bf16[1024,768]{1,0:T(8,128)(2,1)}, bf16[4,1536,384]{2,1,0:T(8,128)(2,1)}, bf16[768,768]{1,0:T(8,128)(2,1)}, bf16[768,768]{1,0:T(8,128)(2,1)}, f32[256,128]{1,0:T(8,128)}) custom-call(bf16[1024,768]{1,0:T(8,128)(2,1)} %get-tuple-element.60.dctx_ref, bf16[1024,768]{1,0:T(8,128)(2,1)} %get-tuple-element.61.att_ref, ...), custom_call_target="tpu_custom_call" | custom-call | tf_op jit(solution)/shard_map/attend_backward/pallas_call | solution.py:1052
  270.9 2.3 copy-done
  273.3 1.3 copy-done.1
  274.5 1.3 copy-done.2
  275.8 0.9 copy-done.3
  276.7 5.7 %spread_out.1 = (f32[768,2304]{1,0:T(8,128)}, f32[768,768]{1,0:T(8,128)}, f32[768,768]{1,0:T(8,128)}, f32[768,768]{1,0:T(8,128)}, f32[1,2304]{1,0:T(1,128)S(1)},...) custom-call(bf16[4,1536,384]{2,1,0:T(8,128)(2,1)S(1)} %copy-done, ...), custom_call_target="tpu_custom_call" | custom-call | tf_op jit(solution)/shard_map/spread_out/pallas_call | solution.py:1158
  282.4 0.6 reduce
  283.0 0.6 reduce.1
  283.6 0.6 reduce.2
  284.2 0.6 reduce.3
  284.8 0.6 reduce.4
  286.0 0.6 reduce.6
  287.2 1.1 copy.44
  288.4 0.8 copy-done.5
  289.2 1.1 copy.45
  (15 shorter events, 2.0 us)
Async XLA Ops:
  73.8 65.4 %copy-start.6 = (f32[12,35]{1,0:T(8,128)S(1)}, f32[12,35]{1,0:T(8,128)}, u32[]{:S(2)}) copy-start(f32[12,35]{1,0:T(8,128)} %param.20) | copy-start | bytes 5044
  270.9 2.3 copy-start
  273.3 1.3 copy-start.1
  274.5 1.3 copy-start.2
  275.8 0.9 copy-start.3
  276.7 10.5 %copy-start.4 = (bf16[1024,768]{1,0:T(8,128)(2,1)S(1)}, bf16[1024,768]{1,0:T(8,128)(2,1)}, u32[]{:S(2)}) copy-start(bf16[1024,768]{1,0:T(8,128)(2,1)} %get-tuple-element.108) | copy-start | bytes 4718596
  287.2 2.0 copy-start.5

commit v4 on v3

--- a/solution.py
+++ b/solution.py
@@ -87,19 +87,22 @@
     return centred * scaling, scaling
 
 
-def build_masks(seg_col, seg_pad, same_ref, near_ref):
+def segment_rows(seg_ref, row):
+    ids = seg_ref[pl.ds(row, 1)].astype(F32)
+    edge = jnp.full((1, HALO), -1.0, F32)
+    return jnp.concatenate([edge, ids, edge], 1), jnp.broadcast_to(ids, (PAIR, ids.shape[1])).T[:, :1]
+
+
+def build_same(seg_pad, seg_col, same_ref):
     length = seg_col.shape[0]
     for start in range(0, length, BLK):
         own = seg_col[start : start + BLK]
         same_ref[start : start + BLK, :] = jnp.where(
             own == seg_pad[:, HALO : HALO + length], 1.0, 0.0
         ).astype(BF16)
-        near_ref[start // BLK] = jnp.where(
-            own == seg_pad[:, start : start + 2 * BLK], 1.0, 0.0
-        ).astype(BF16)
-
-
-def build_near(seg_col, seg_pad, near_ref):
+
+
+def build_near(seg_pad, seg_col, near_ref):
     length = seg_col.shape[0]
     for start in range(0, length, BLK):
         own = seg_col[start : start + BLK]
@@ -108,41 +111,58 @@
         ).astype(BF16)
 
 
+def place_taps(kernel, reverse):
+    taps = kernel.shape[1]
+    shape = (taps, 2 * BLK)
+    tap = taps - 1 - rows(shape) if reverse else rows(shape)
+    return dot_nn(kernel.astype(BF16), (lanes(shape) == tap + HALO - taps // 2).astype(BF16))
+
+
 def attend_kernel(
-    x_ref, col_ref, pad_ref, wq_ref, wk_ref, wv_ref, bq_ref, bk_ref, bv_ref, tap_ref, wo_ref, bo_ref,
+    x_ref, seg_ref, wq_ref, wk_ref, wv_ref, b_ref, kernel_ref, wo_ref, bo_ref,
     wu_ref, wd_ref, bu_ref,
     q_ref, k_ref, v_ref, sq_ref, sk_ref, w_ref, s_ref, att_ref, inv_ref, ctx_ref, res_ref,
     up_ref, down_ref, bias_ref,
-    same_ref, near_ref, vv_ref, send_sem, recv_sem, copy_sem,
+    same_ref, near_ref, vv_ref, tap_ref, mine_ref, send_sem, recv_sem, copy_sem,
     *, dp_size, tensor_size,
 ):
     row, quad = pl.program_id(0), pl.program_id(1)
     quads, seqs = pl.num_programs(1), pl.num_programs(0)
-    ticks = gather_plan(dp_size, tensor_size, (wu_ref, wd_ref, bu_ref), (up_ref, down_ref, bias_ref), (send_sem, recv_sem), copy_sem)
+    ticks = gather_plan(dp_size, tensor_size, (wu_ref, wd_ref, mine_ref), (up_ref, down_ref, bias_ref), (send_sem, recv_sem), copy_sem)
     length = x_ref.shape[0]
     blocks = length // BLK
 
+    @pl.when((row == 0) & (quad == 0))
+    def _():
+        tap_ref[...] = place_taps(kernel_ref[...], False)
+        mine_ref[...] = bu_ref[...].astype(F32)[None, :]
+
     @pl.when(quad == 0)
     def _():
-        build_masks(col_ref[...], pad_ref[0], same_ref, near_ref)
+        seg_pad, seg_col = segment_rows(seg_ref, row)
+        build_same(seg_pad, seg_col, same_ref)
+        build_near(seg_pad, seg_col, near_ref)
         for half in range(2):
             edge = jnp.zeros((HALO, 2 * PAIR), BF16)
             vv_ref[half, :HALO] = edge
             vv_ref[half, HALO + length :] = edge
             vv_ref[half, HALO : HALO + length, PAIR:] = head_mask(half, (length, PAIR))
 
+    def bias(part):
+        start = pl.multiple_of(part * x_ref.shape[1] + quad * QUAD, QUAD)
+        return b_ref[pl.ds(start, QUAD)][None, :]
+
     for start in range(0, length, BLK):
         here = slice(start, start + BLK)
         x = x_ref[here]
-        for w, b, unit, scale, factor in (
-            (wq_ref, bq_ref, q_ref, sq_ref, SHRINK),
-            (wk_ref, bk_ref, k_ref, sk_ref, 1.0),
+        for number, (w, unit, scale, factor) in enumerate(
+            ((wq_ref, q_ref, sq_ref, SHRINK), (wk_ref, k_ref, sk_ref, 1.0))
         ):
-            part = dot_nn(x, w[...]) + b[...]
+            part = dot_nn(x, w[...]) + bias(number)
             scaling = lax.rsqrt(head_sum(part * part) + EPS_UNIT)
             unit[here] = (part * (scaling * factor)).astype(BF16)
             scale[here] = scaling.astype(BF16)
-        v_ref[here] = (dot_nn(x, wv_ref[...]) + bv_ref[...]).astype(BF16)
+        v_ref[here] = (dot_nn(x, wv_ref[...]) + bias(2)).astype(BF16)
 
     def one_pair(pair, carry):
         turn = (row * quads + quad) * (QUAD // PAIR) + pair
@@ -179,7 +199,7 @@
                     w_ref[0, head, here, :low] = jnp.zeros((BLK, low), BF16)
                 if high < length:
                     w_ref[0, head, here, high:] = jnp.zeros((BLK, length - high), BF16)
-                taps = band(tap_ref[0, pl.ds(head, 1)], BLK).astype(BF16) * near_ref[block]
+                taps = band(tap_ref[pl.ds(quad * (QUAD // HEAD) + head, 1)], BLK).astype(BF16) * near_ref[block]
                 near += dot_nn(taps, vv_ref[half, block * BLK : block * BLK + 2 * BLK, :PAIR])
             inverse = 1.0 / (1.0 + total[:, PAIR:])
             attended = total[:, :PAIR] * inverse
@@ -192,7 +212,7 @@
 
     @pl.when(quad == 0)
     def _():
-        res_ref[...] = x_ref[...].astype(F32) + bo_ref[...]
+        res_ref[...] = x_ref[...].astype(F32) + bo_ref[...][None, :]
 
     for start in range(0, length, BLK):
         here = slice(start, start + BLK)
@@ -208,40 +228,46 @@
     def mine(place):
         return place * CORES + core.place
 
-    def rows_at(ref, place):
-        size = ref.shape[-2] // x.size
-        return span(place * size, size)
-
-    def at_y(which):
-        source, target = own[which], whole[which]
+    def half_of(ref, piece):
+        size = ref.shape[-2] // 2
+        return span(piece % 2 * size, size)
+
+    def rows_at(ref, piece, place):
+        size = ref.shape[-2] // (2 * x.size)
+        return span(piece % 2 * x.size * size + place * size, size)
+
+    def at_y(piece):
+        source, target = own[piece // 2], whole[piece // 2]
         out = []
         for j in range(1, y.size):
-            if which < 2:
-                block = rows_at(source, x.place)
+            if piece < 4:
+                block = rows_at(source, piece, x.place)
                 pair = (source.at[block], target.at[mine(y.place), block])
             else:
                 pair = (source, target.at[mine(y.place)])
             out.append(send(*pair, sems, next(number), y.device(y.ahead(j))))
         return out
 
-    def at_x(which):
-        target = whole[which]
+    def at_x(piece):
+        target = whole[piece // 2]
         out = []
         for j in range(1, y.size):
-            block = target.at[mine(y.ahead(j)), rows_at(target, x.place)]
+            block = target.at[mine(y.ahead(j)), rows_at(target, piece, x.place)]
             out += [send(block, block, sems, next(number), x.device(x.ahead(i))) for i in range(1, x.size)]
         return out
 
-    def to_mate(which):
-        target = whole[which]
-        return [
-            send(target.at[mine(y.ahead(j))], target.at[mine(y.ahead(j))], sems, next(number), mate)
-            for j in range(1, y.size)
-        ]
+    def to_mate(piece):
+        target = whole[piece // 2]
+        out = []
+        for j in range(1, y.size):
+            block = target.at[mine(y.ahead(j))]
+            block = block.at[half_of(target, piece)] if piece < 4 else block
+            out.append(send(block, block, sems, next(number), mate))
+        return out
 
     keep = [pltpu.make_async_copy(own[i], whole[i].at[mine(y.place)], copy_sem.at[i]) for i in range(3)]
     give = [send(own[i], whole[i].at[mine(y.place)], sems, next(number), mate) for i in range(3)]
-    ys, xs, mates = [at_y(i) for i in range(3)], [at_x(i) for i in range(2)], [to_mate(i) for i in range(3)]
+    ys, xs, mates = [at_y(i) for i in range(5)], [at_x(i) for i in range(4)], [to_mate(i) for i in range(5)]
 
     def start(copies):
         return [copy.start for copy in copies]
@@ -250,24 +276,26 @@
         return [copy.wait for copy in copies]
 
     steps = [
-        [lambda: greet(axes, ("core", "y", "x"))] + start(ys[0] + ys[2] + give + keep),
-        wait(ys[0] + ys[2]) + start(xs[0] + ys[1] + mates[2]),
-        wait(xs[0] + ys[1]) + start(mates[0] + xs[1]),
-        wait(xs[1]) + start(mates[1]),
+        [lambda: greet(axes, ("core", "y", "x"))] + start(ys[0] + ys[1] + ys[4] + give + keep),
+        wait(ys[0] + ys[4]) + start(xs[0] + ys[2] + mates[4]),
+        wait(ys[1]) + start(xs[1] + ys[3]),
+        wait(ys[2] + xs[0]) + start(xs[2] + mates[0]),
+        wait(ys[3] + xs[1]) + start(xs[3] + mates[1]),
+        wait(xs[2] + xs[3]) + start(mates[2] + mates[3]),
     ]
-    last = wait(mates[0] + mates[1] + mates[2] + give + keep)
+    last = wait([copy for piece in mates for copy in piece] + give + keep)
     return dict(zip(GATHER_TIMES, steps)) | {GATHER_TIMES[len(steps)]: last}
 
 
-GATHER_TIMES = (0, 4, 7, 10, 11)
+GATHER_TIMES = (0, 4, 5, 7, 8, 10, 11)
 
 
 KCH = 256
 
 
-def attend(tokens, seg_col, seg_pad, w_qkv, vectors, taps, w_out, w_up, w_down, b_up, dp_size, tensor_size, length):
+def attend(tokens, segment_ids, w_qkv, b_qkv, kernel, w_out, b_out, w_up, w_down, b_up, dp_size, tensor_size):
     count, width = tokens.shape
-    seqs = count // length
+    seqs, length = segment_ids.shape
     quads = width // QUAD
     heads = width // HEAD
     per = QUAD // HEAD
@@ -280,40 +308,44 @@
     def part(rows_of, k):
         return pl.BlockSpec((rows_of, QUAD), lambda r, p, k=k: (0, p + k * quads))
 
+    def whole(*shape):
+        return pl.BlockSpec(shape, lambda r, p: (0,) * len(shape), pipeline_mode=pl.Buffered(1))
+
     others = tensor_size // CORES - 1
-    copies = 3 + 6 * others + 2 * others * (dp_size // DEPTH - 1)
+    copies = 3 + 10 * others + 4 * others * (dp_size // DEPTH - 1)
     return pl.pallas_call(
         functools.partial(attend_kernel, dp_size=dp_size, tensor_size=tensor_size),
         grid=(seqs, quads),
         in_specs=[
             pl.BlockSpec((length, width), lambda r, p: (r, 0)),
-            pl.BlockSpec((length, 1), lambda r, p: (r, 0)),
-            pl.BlockSpec((1, 1, length + 2 * HALO), lambda r, p: (r, 0, 0)),
+            whole(*segment_ids.shape),
             part(width, 0), part(width, 1), part(width, 2),
-            part(1, 0), part(1, 1), part(1, 2),
-            pl.BlockSpec((1, per, 2 * BLK), lambda r, p: (p, 0, 0)),
+            whole(*b_qkv.shape),
+            whole(*kernel.shape),
             pl.BlockSpec((QUAD, width), lambda r, p: (p, 0)),
-            pl.BlockSpec((1, width), lambda r, p: (0, 3)),
+            whole(*b_out.shape),
         ]
         + [
-            pl.BlockSpec(part.shape, lambda r, p: (0, 0), pipeline_mode=pl.Buffered(1))
-            for part in (w_up, w_down, b_up)
+            whole(*each.shape) for each in (w_up, w_down, b_up)
         ],
         out_specs=[own] * 5 + [big_spec] * 2 + [own] * 3 + [pl.BlockSpec((length, width), lambda r, p: (r, 0))]
         + [pl.BlockSpec(memory_space=pl.ANY)] * 3,
         out_shape=[act] * 5 + [big] * 2 + [act] * 3 + [jax.ShapeDtypeStruct((count, width), F32)]
-        + [jax.ShapeDtypeStruct((tensor_size,) + part.shape, part.dtype) for part in (w_up, w_down, b_up)],
+        + [jax.ShapeDtypeStruct((tensor_size,) + part.shape, BF16) for part in (w_up, w_down)]
+        + [jax.ShapeDtypeStruct((tensor_size, 1, b_up.shape[0]), F32)],
         scratch_shapes=[
             pltpu.VMEM((length, length), BF16),
             pltpu.VMEM((blocks, BLK, 2 * BLK), BF16),
             pltpu.VMEM((2, length + 2 * HALO, 2 * PAIR), BF16),
+            pltpu.VMEM((heads, 2 * BLK), F32),
+            pltpu.VMEM((1, b_up.shape[0]), F32),
             pltpu.SemaphoreType.DMA((copies,)),
             pltpu.SemaphoreType.DMA((copies,)),
             pltpu.SemaphoreType.DMA((3,)),
         ],
         compiler_params=pltpu.CompilerParams(vmem_limit_bytes=56 * 2**20, collective_id=2, has_side_effects=True),
         name="attend_forward",
-    )(tokens, seg_col, seg_pad, w_qkv, w_qkv, w_qkv, vectors, vectors, vectors, taps, w_out, vectors, w_up, w_down, b_up)
+    )(tokens, segment_ids, w_qkv, w_qkv, w_qkv, b_qkv, kernel, w_out, b_out, w_up, w_down, b_up)
 
 
 DEPTH = 4
@@ -561,7 +593,7 @@
     def _():
         def one(t, carry):
             unit, _ = norm_stats(res_ref[at(t)])
-            low_ref[at(t)] = (unit * gain1_ref[...] + shift1_ref[...]).astype(BF16)
+            low_ref[at(t)] = (unit * gain1_ref[...][None, :] + shift1_ref[...][None, :]).astype(BF16)
             acc_ref[at(t)] = jnp.zeros((TILE, width), F32)
             return carry
 
@@ -584,11 +616,11 @@
     def _():
         def one(t, sums):
             unit, _ = norm_stats(res_ref[at(t)])
-            first = unit * gain1_ref[...] + shift1_ref[...]
-            unit, scaling = norm_stats(first + acc_ref[at(t)] + bd_ref[...])
-            out_ref[at(t)] = (unit * gain2_ref[...] + shift2_ref[...]).astype(BF16)
+            first = unit * gain1_ref[...][None, :] + shift1_ref[...][None, :]
+            unit, scaling = norm_stats(first + acc_ref[at(t)] + bd_ref[...][None, :])
+            out_ref[at(t)] = (unit * gain2_ref[...][None, :] + shift2_ref[...][None, :]).astype(BF16)
             grad = cot_ref[at(t)].astype(F32)
-            d_res = norm_backward(grad, unit, scaling, gain2_ref[...])
+            d_res = norm_backward(grad, unit, scaling, gain2_ref[...][None, :])
             d_ffn = d_res.astype(BF16)
             acc_ref[at(t)] = d_res
             dffn_ref[at(t)] = d_ffn
@@ -659,7 +691,7 @@
         def one(t, sums):
             unit, scaling = norm_stats(res_ref[at(t)])
             grad = acc_ref[at(t)]
-            d_proj = norm_backward(grad, unit, scaling, gain1_ref[...]).astype(BF16)
+            d_proj = norm_backward(grad, unit, scaling, gain1_ref[...][None, :]).astype(BF16)
             dproj_ref[at(t)] = d_proj
             dctx_ref[at(t)] = dot_nt(d_proj, wo_ref[...]).astype(BF16)
             return (
@@ -691,7 +723,7 @@
     return jnp.where(step < parts, step, there * CORES + whose)
 
 
-def feed_forward(res, cot, ctx, w_out, vectors, b_up, w_up, w_down):
+def feed_forward(res, cot, ctx, w_out, gain1, shift1, gain2, shift2, b_down, b_up, w_up, w_down):
     count, width = res.shape
     parts, _, share = w_up.shape
     heights = parts // 2
@@ -710,7 +742,7 @@
         grid=(2 * parts,),
         in_specs=[whole(count, width)] * 3
         + [whole(width, width)]
-        + [pl.BlockSpec((1, width), lambda s, k=k: (0, k), pipeline_mode=pl.Buffered(1)) for k in range(4, 9)]
+        + [whole(width)] * 5
         + [per_part(1, share), per_part(width, share), per_part(share, width)],
         out_specs=[whole(count, width)] * 3
         + [whole(2 * width, width // 2), whole(heights, width, share), whole(share, width), whole(smalls, PAIR)],
@@ -739,15 +771,15 @@
         ],
         compiler_params=pltpu.CompilerParams(vmem_limit_bytes=60 * 2**20, collective_id=0, has_side_effects=True),
         name="feed_forward",
-    )(res, cot, ctx, w_out, *[vectors] * 5, b_up, w_up, w_down)
+    )(res, cot, ctx, w_out, gain1, shift1, gain2, shift2, b_down, b_up, w_up, w_down)
 
 
 def attend_back_kernel(
-    dctx_ref, att_ref, inv_ref, q_ref, k_ref, v_ref, sq_ref, sk_ref, w_ref, s_ref, x_ref, col_ref, pad_ref,
-    wqkv_ref, flip_ref, dproj_ref, gwo_ref, pu_ref, pd_ref, small_ref,
+    dctx_ref, att_ref, inv_ref, q_ref, k_ref, v_ref, sq_ref, sk_ref, w_ref, s_ref, x_ref, seg_ref,
+    wqkv_ref, kernel_ref, dproj_ref, gwo_ref, pu_ref, pd_ref, small_ref,
     gt_ref, all_out, up_out, down_out, few_out,
     near_ref, vv_ref, dpad_ref, dcos_ref, dq_ref, dk_ref, dv_ref, joined_ref, gwacc_ref, conv_ref,
-    gwlow_ref, gb_ref, mini_ref, all_ref, up_ref, down_ref, few_ref, out_sem, *links,
+    gwlow_ref, gb_ref, flip_ref, mini_ref, all_ref, up_ref, down_ref, few_ref, out_sem, *links,
     plan, quads, seqs,
 ):
     quad, row = pl.program_id(0), pl.program_id(1)
@@ -761,7 +793,7 @@
         (all_out, up_out, down_out, few_out, out_sem))
     calls = quads * seqs * (QUAD // HEAD)
 
-    build_near(col_ref[...], pad_ref[0], near_ref)
+    build_near(*segment_rows(seg_ref, row), near_ref)
     for half in range(2):
         edge = jnp.zeros((HALO, PAIR), BF16)
         for ref in (vv_ref, dpad_ref):
@@ -777,6 +809,7 @@
     @pl.when((quad == 0) & (row == 0))
     def _():
         gb_ref[...] = jnp.zeros_like(gb_ref)
+        flip_ref[...] = place_taps(kernel_ref[...], True)
         mini_ref[...] = jnp.zeros_like(mini_ref)
         mini_ref[: small_ref.shape[0]] = small_ref[...]
         filled = 2 * gwacc_ref.shape[0]
@@ -824,7 +857,7 @@
                     dq_ref[here] += grown
                 window = slice(block * BLK, block * BLK + 2 * BLK)
                 near = near_ref[block]
-                taps = band(flip_ref[0, pl.ds(head, 1)], BLK).astype(BF16) * near
+                taps = band(flip_ref[pl.ds(quad * (QUAD // HEAD) + head, 1)], BLK).astype(BF16) * near
                 grown = dot_nn(taps, dpad_ref[half, window])
                 if half == 0:
                     dv_ref[here] = grown
@@ -898,27 +931,46 @@
                     event()
 
 
-FFN_TIMES = (
-    ((3, 7, 14, 21, 34), (0, 4, 8, 16, 25)),
-    ((0, 8, 12, 20, 37, 50), (5, 17, 29, 48, 57, 61)),
+FFN_PLAN = (
+    (
+        (("x", "z"), (4, 9, 15, 24, 54)),
+        (("z", "x"), (3, 27, 30, 50, 59)),
+    ),
+    (
+        (("x", "z"), (0, 8, 15, 21, 34, 43)),
+        (("x", "z"), (7, 19, 23, 29, 38, 56)),
+    ),
 )
-ALL_TIMES = (
-    (6, 8, 15, 19, 26, 39, 47, 52, 56),
-    (10, 12, 16, 19, 27, 40, 46, 53, 58),
-    (16, 18, 22, 32, 44, 51, 55, 60, 62),
-    (25, 30, 36, 42, 49, 54, 59, 63, 64),
+ALL_PLAN = (
+    (
+        (3, 1, (2, 4, 11, 13, 16, 29, 35, 45, 55)),
+    ),
+    (
+        (3, 0, (10, 11, 17, 26, 31, 41, 47, 52, 59)),
+    ),
+    (
+        (3, 0, (19, 21, 28, 37, 42, 48, 51, 57, 60)),
+    ),
+    (
+        (3, 1, (24, 25, 32, 36, 39, 44, 48, 55, 58)),
+    ),
 )
-MINI_TIMES = (25, 28, 31, 33, 35, 38, 41, 43, 45)
+MINI_ORDER = 1
+MINI_TIMES = (25, 27, 33, 40, 46, 49, 52, 53, 55)
 FFN_ROWS = 384
-FFN_ORDER = ("y", "x", "z")
-FFN_BACK = ("z", "x")
 ORDERS = (("core", "x", "y", "z"), ("core", "y", "x", "z"))
-CHOICE = (1, 0, 1, 1)
-
-
-def all_order(index):
-    order = ORDERS[CHOICE[index]]
-    return order, order[::-1]
+
+
+def all_parts(index, size, devices):
+    parts = ALL_PLAN[index]
+    if sum(units for units, _, _ in parts) * 16 * devices != size:
+        parts = ((size // (16 * devices), parts[-1][1], parts[-1][2]),)
+    out, start = [], 0
+    for units, order, times in parts:
+        rows_of = units * 16 * devices
+        out.append((start, rows_of, ORDERS[order], times))
+        start += rows_of
+    return out
 
 
 class FfnReduction(Reduction):
@@ -959,16 +1011,18 @@
     out = []
     devices = math.prod(sizes.values())
     y = sizes["y"]
-    for height, columns, order in ((share, width, FFN_ORDER[1:]), (width, share, FFN_ORDER)):
-        for _ in range(height // FFN_ROWS):
-            shapes = [pltpu.VMEM((y - 1, FFN_ROWS, columns), BF16)] if order is FFN_ORDER else []
-            shapes += landing_shapes(FFN_ORDER[1:], sizes, FFN_ROWS, columns, BF16)
-            out.append((shapes, copies_of(order, FFN_BACK, sizes)))
+    for late, (height, columns) in enumerate(((share, width), (width, share))):
+        for start in range(0, height, FFN_ROWS):
+            order = FFN_PLAN[late][start // FFN_ROWS][0]
+            shapes = [pltpu.VMEM((y - 1, FFN_ROWS, columns), BF16)] if late else []
+            shapes += landing_shapes(order, sizes, FFN_ROWS, columns, BF16)
+            out.append((shapes, copies_of((("y",) if late else ()) + order, order, sizes)))
+    size = padded(2 * width, devices)
     for index in range(quads + 1):
-        order, back = all_order(index)
-        out.append((landing_shapes(order, sizes, padded(2 * width, devices), width // 2, BF16), copies_of(order, back, sizes)))
-    order, back = all_order(quads)
-    out.append((landing_shapes(order, sizes, 8 * devices, PAIR, F32), copies_of(order, back, sizes)))
+        for _, rows_of, order, _ in all_parts(index, size, devices):
+            out.append((landing_shapes(order, sizes, rows_of, width // 2, BF16), copies_of(order, order, sizes)))
+    order = ORDERS[MINI_ORDER]
+    out.append((landing_shapes(order, sizes, 8 * devices, PAIR, F32), copies_of(order, order, sizes)))
     return out
 
 
@@ -998,36 +1052,36 @@
         stores.append(store)
 
     number = 0
-    for source, final, place in ((pd_ref, down_ref, down_out), (pu_ref, up_ref, up_out)):
+    for late, (source, final, place) in enumerate(((pd_ref, down_ref, down_out), (pu_ref, up_ref, up_out))):
         for start in range(0, final.shape[0], FFN_ROWS):
             landings, sems = taken[number]
             block = span(start, FFN_ROWS)
-            if source is pd_ref:
-                reduction = Reduction(axes, FFN_ORDER[1:], FFN_BACK, source, start, FFN_ROWS, final, start, landings, sems)
-            else:
-                reduction = FfnReduction(axes, FFN_ORDER, FFN_BACK, source, start, FFN_ROWS, final, start, landings, sems)
-            times = FFN_TIMES[source is pu_ref][start // FFN_ROWS]
+            order, times = FFN_PLAN[late][start // FFN_ROWS]
+            kind = FfnReduction if late else Reduction
+            whole_order = ("y",) + order if late else order
+            reduction = kind(axes, whole_order, order[::-1], source, start, FFN_ROWS, final, start, landings, sems)
             enlist(reduction, times, final.at[block], place.at[block])
             number += 1
     size = padded(2 * width, devices)
     for index in range(quads + 1):
-        landings, sems = taken[number]
-        order, back = all_order(index)
         source = gwo_ref if index == 0 else gwlow_ref.at[index - 1]
-        reduction = Reduction(axes, order, back, source, 0, size, all_ref.at[index], 0, landings, sems)
-        enlist(reduction, ALL_TIMES[index], all_ref.at[index], all_out.at[index])
-        number += 1
+        for start, rows_of, order, times in all_parts(index, size, devices):
+            landings, sems = taken[number]
+            final = all_ref.at[index]
+            reduction = Reduction(axes, order, order[::-1], source, start, rows_of, final, start, landings, sems)
+            enlist(reduction, times, final.at[span(start, rows_of)], all_out.at[index, span(start, rows_of)])
+            number += 1
     landings, sems = taken[number]
-    order, back = all_order(quads)
-    reduction = Reduction(axes, order, back, mini_ref, 0, 8 * devices, few_ref, 0, landings, sems)
+    order = ORDERS[MINI_ORDER]
+    reduction = Reduction(axes, order, order[::-1], mini_ref, 0, 8 * devices, few_ref, 0, landings, sems)
     enlist(reduction, MINI_TIMES, few_ref, few_out)
     ticks[max(ticks) + 1] = [store.wait for store in stores]
     return ticks
 
 
-def attend_back(dctx, att, inv, q, k, v, sq, sk, weight, slope, tokens, seg_col, seg_pad, w_qkv, flipped, dproj, gwo, pu, pd, small, dp_size, tensor_size, length):
+def attend_back(dctx, att, inv, q, k, v, sq, sk, weight, slope, tokens, segment_ids, w_qkv, kernel, dproj, gwo, pu, pd, small, dp_size, tensor_size):
     count, width = tokens.shape
-    seqs = count // length
+    seqs, length = segment_ids.shape
     quads = width // QUAD
     per = QUAD // HEAD
     blocks = length // BLK
@@ -1048,7 +1102,6 @@
     def whole(*shape):
         return pl.BlockSpec(shape, lambda p, r: (0,) * len(shape), pipeline_mode=pl.Buffered(1))
 
-    taps_spec = pl.BlockSpec((1, per, 2 * BLK), lambda p, r: (p, 0, 0))
     return pl.pallas_call(
         functools.partial(attend_back_kernel, plan=(None, sizes, dp_size, tensor_size), quads=quads, seqs=seqs),
         grid=(quads, seqs),
@@ -1056,10 +1109,9 @@
         + [big] * 2
         + [
             wide,
-            pl.BlockSpec((length, 1), lambda p, r: (r, 0)),
-            pl.BlockSpec((1, 1, length + 2 * HALO), lambda p, r: (r, 0, 0)),
+            whole(*segment_ids.shape),
             whole(width, 3 * width),
-            taps_spec,
+            whole(*kernel.shape),
             wide,
             whole(*gwo.shape), whole(*pu.shape), whole(*pd.shape), whole(*small.shape),
         ],
@@ -1087,20 +1139,21 @@
             pltpu.VMEM((per, BLK, 2 * BLK), F32),
             pltpu.VMEM((quads, grown, width // 2), BF16),
             pltpu.VMEM((quads, 8, 3 * QUAD), F32),
+            pltpu.VMEM((width // HEAD, 2 * BLK), F32),
             pltpu.VMEM((minis, PAIR), F32),
             pltpu.VMEM((quads + 1, grown, width // 2), BF16),
             pltpu.VMEM((width, share), BF16),
             pltpu.VMEM((share, width), BF16),
             pltpu.VMEM((minis, PAIR), F32),
-            pltpu.SemaphoreType.DMA((quads + 2 + (width + share) // FFN_ROWS,)),
+            pltpu.SemaphoreType.DMA((len(link_plan(sizes, width, share, quads)),)),
         ]
         + scratch,
         compiler_params=pltpu.CompilerParams(vmem_limit_bytes=60 * 2**20, collective_id=1, has_side_effects=True),
         name="attend_backward",
-    )(dctx, att, inv, q, k, v, sq, sk, weight, slope, tokens, seg_col, seg_pad, w_qkv, flipped, dproj, gwo, pu, pd, small)
-
-
-def spread_kernel(low_ref, high_ref, up_ref, down_ref, few_ref, gw_ref, gwo_ref, gup_ref, gdown_ref, *vectors, first_lane, base):
+    )(dctx, att, inv, q, k, v, sq, sk, weight, slope, tokens, segment_ids, w_qkv, kernel, dproj, gwo, pu, pd, small)
+
+
+def spread_kernel(low_ref, high_ref, up_ref, down_ref, few_ref, a_ref, b_ref, gw_ref, gwo_ref, gup_ref, gdown_ref, a_out, b_out, *vectors, first_lane, base):
     width = gwo_ref.shape[1]
     half = width // 2
     quads = low_ref.shape[0] - 1
@@ -1112,6 +1165,8 @@
                 side, lane = (low_ref, start) if start < half else (high_ref, start - half)
                 to = part * width + quad * QUAD + start - part * QUAD
                 gw_ref[:, to : to + PAIR] = side[1 + quad, :, lane : lane + PAIR].astype(F32)
+    a_out[...] = a_ref[...]
+    b_out[...] = b_ref[...]
     gup_ref[...] = up_ref[...].astype(F32)
     gdown_ref[...] = down_ref[...].astype(F32)
 
@@ -1121,12 +1176,12 @@
         lines = width // PAIR
 
         def copy_line(target, to, line):
-            target[:, to * PAIR : (to + 1) * PAIR] = few_ref[pl.ds(line, 1)]
+            target[to * PAIR : (to + 1) * PAIR] = few_ref[line]
 
         for number, target in enumerate(six):
             for i in range(lines):
                 copy_line(target, i, number * lines + i)
-        share = gbu_ref.shape[1] // PAIR
+        share = gbu_ref.shape[0] // PAIR
         mine = lax.axis_index("tensor") * share
         for i in range(share):
             copy_line(gbu_ref, i, 6 * lines + mine + i)
@@ -1140,10 +1195,10 @@
         conv_ref[...] = pltpu.roll(kept, PAIR - first_lane, 1)[:, :taps]
 
 
-def spread_out(grads, up, down, few, width, heads, taps, first_lane, base):
+def spread_out(grads, up, down, few, out, gt, width, heads, taps, first_lane, base):
     chunks = grads.shape[0]
     quads = chunks - 1
-    steps = 6
+    steps = 8
     rows_of = width // steps
     share = up.shape[1]
     down_rows = share // steps
@@ -1154,7 +1209,7 @@
     def by_rows(count, columns):
         return pl.BlockSpec((count, columns), lambda s: (s, 0))
 
-    row = jax.ShapeDtypeStruct((1, width), F32)
+    row = jax.ShapeDtypeStruct((width,), F32)
     return pl.pallas_call(
         functools.partial(spread_kernel, first_lane=first_lane, base=base),
         grid=(steps,),
@@ -1164,67 +1219,54 @@
             by_rows(rows_of, share),
             by_rows(down_rows, width),
             whole(*few.shape),
+            by_rows(out.shape[0] // steps, width), by_rows(out.shape[0] // steps, width),
         ],
         out_specs=[
             by_rows(rows_of, 3 * width), by_rows(rows_of, width), by_rows(rows_of, share), by_rows(down_rows, width),
-            whole(1, 3 * width), whole(heads, taps),
+            by_rows(out.shape[0] // steps, width), by_rows(out.shape[0] // steps, width),
+            whole(3 * width), whole(heads, taps),
         ]
-        + [whole(1, width)] * 6
-        + [whole(1, share)],
+        + [whole(width)] * 6
+        + [whole(share)],
         out_shape=[
             jax.ShapeDtypeStruct((width, 3 * width), F32),
             jax.ShapeDtypeStruct((width, width), F32),
             jax.ShapeDtypeStruct((width, share), F32),
             jax.ShapeDtypeStruct((share, width), F32),
-            jax.ShapeDtypeStruct((1, 3 * width), F32),
+            jax.ShapeDtypeStruct(out.shape, out.dtype),
+            jax.ShapeDtypeStruct(gt.shape, gt.dtype),
+            jax.ShapeDtypeStruct((3 * width,), F32),
             jax.ShapeDtypeStruct((heads, taps), F32),
         ]
         + [row] * 6
-        + [jax.ShapeDtypeStruct((1, share), F32)],
-        compiler_params=pltpu.CompilerParams(vmem_limit_bytes=40 * 2**20),
+        + [jax.ShapeDtypeStruct((share,), F32)],
+        compiler_params=pltpu.CompilerParams(vmem_limit_bytes=60 * 2**20),
         name="spread_out",
-    )(grads, grads, up, down, few)
+    )(grads, grads, up, down, few, out, gt)
 
 
 def body(
     tokens, segment_ids, w_qkv, b_qkv, conv_kernel, w_out, b_out, norm1_gain, norm1_bias,
     w_up, b_up, w_down, b_down, norm2_gain, norm2_bias, cotangent,
 ):
-    seqs, length = segment_ids.shape
     width = tokens.shape[1]
-    heads, span_of = conv_kernel.shape
-    per = QUAD // HEAD
-    radius = span_of // 2
-    first_tap = HALO - radius
-
-    def spread(kernel):
-        padded = jnp.pad(kernel, ((0, 0), (first_tap, 2 * BLK - first_tap - span_of)))
-        return padded.reshape(heads // per, per, 2 * BLK)
-
-    seg_col = segment_ids.reshape(-1, 1)
-    seg_pad = jnp.pad(segment_ids, ((0, 0), (HALO, HALO)), constant_values=-1)[:, None, :]
-    taps, flipped = spread(conv_kernel), spread(conv_kernel[:, ::-1])
-
+    heads, taps = conv_kernel.shape
     dp_size, tensor_size = lax.axis_size("dp"), lax.axis_size("tensor")
-    vectors = jnp.concatenate([b_qkv, b_out, norm1_gain, norm1_bias, norm2_gain, norm2_bias, b_down])[None]
-
     q, k, v, sq, sk, weight, slope, att, inv, ctx, res, up_all, down_all, bias_all = attend(
-        tokens, seg_col, seg_pad, w_qkv, vectors, taps, w_out, w_up, w_down, b_up.astype(F32)[None],
-        dp_size, tensor_size, length,
+        tokens, segment_ids, w_qkv, b_qkv, conv_kernel, w_out, b_out, w_up, w_down, b_up, dp_size, tensor_size
     )
-    out, dproj, dctx, gwo, pu, pd, small = feed_forward(res, cotangent, ctx, w_out, vectors, bias_all, up_all, down_all)
+    out, dproj, dctx, gwo, pu, pd, small = feed_forward(
+        res, cotangent, ctx, w_out, norm1_gain, norm1_bias, norm2_gain, norm2_bias, b_down, bias_all, up_all, down_all
+    )
     gt, grads, grad_up, grad_down, few = attend_back(
-        dctx, att, inv, q, k, v, sq, sk, weight, slope, tokens, seg_col, seg_pad, w_qkv, flipped, dproj,
-        gwo, pu, pd, small, dp_size, tensor_size, length,
+        dctx, att, inv, q, k, v, sq, sk, weight, slope, tokens, segment_ids, w_qkv, conv_kernel, dproj,
+        gwo, pu, pd, small, dp_size, tensor_size,
     )
-    first_lane = (first_tap + BLK - 1 + BLK) % (2 * BLK)
-    gw, gwo, grad_up, grad_down, gb, grad_conv, gg2, gs2, gbd, gg1, gs1, gbo, gbu = spread_out(
-        grads, grad_up, grad_down, few, width, heads, span_of, first_lane, small.shape[0]
+    first_lane = (HALO - taps // 2 + BLK - 1 + BLK) % (2 * BLK)
+    gw, gwo, grad_up, grad_down, out, gt, gb, grad_conv, gg2, gs2, gbd, gg1, gs1, gbo, gbu = spread_out(
+        grads, grad_up, grad_down, few, out, gt, width, heads, taps, first_lane, small.shape[0]
     )
-    return (
-        out, gt, gw, gb[0], grad_conv, gwo, gbo[0], gg1[0], gs1[0],
-        grad_up, gbu[0], grad_down, gbd[0], gg2[0], gs2[0],
-    )
+    return (out, gt, gw, gb, grad_conv, gwo, gbo, gg1, gs1, grad_up, gbu, grad_down, gbd, gg2, gs2)
 
 
 def solution(mesh):

time: 291 us -> 255 us (0.88)
  local copies, waits for them, and re-layouts: 20.9 us -> 0 us
  Pallas kernels: 264 us -> 254 us
  other arithmetic: 4.86 us -> 0 us
    unnamed x24 -> x0, local copies, waits for them, and re-layouts: 14.8 us -> none
    pallas_call x1, Pallas kernels: 131 us -> 116 us  [attend_back(): pl.pallas_call(functools.partial(attend_back_kernel, plan=(None, sizes, d...]
    pallas_call x1, Pallas kernels: 5.67 us -> 11.3 us  [spread_out(): pl.pallas_call(functools.partial(spread_kernel, first_lane=first_lane, ba...]
    pallas_call x8 -> x0, other arithmetic: 4.86 us -> none  [spread_out(): pl.pallas_call(functools.partial(spread_kernel, first_lane=first_lane, ba...]
where the time goes in v4:
time: 255 us
  Pallas kernels  254 us (100%)
    pallas_call x1, Pallas kernels, attend_back(): pl.pallas_call(functools.partial(attend_back_kernel, plan=(None, sizes, d...  116 us
    pallas_call x1, Pallas kernels, feed_forward(): pl.pallas_call(ffn_kernel, grid=(2 * parts,), in_specs=[whole(count, widt...  65.3 us
    pallas_call x1, Pallas kernels, attend(): pl.pallas_call(functools.partial(attend_kernel, dp_size=dp_size, tensor_s...  61.1 us
    pallas_call x1, Pallas kernels, spread_out(): pl.pallas_call(functools.partial(spread_kernel, first_lane=first_lane, ba...  11.3 us

profile of v4, /device:TPU:0, one launch (start us, length us, event | category | flops | bytes accessed | tf_op | source)
XLA Modules:
  0.0 254.8 jit_solution(1755537675400744954)
XLA Ops:
  0.6 61.1 %attend_forward.1 = (bf16[1024,768]{1,0:T(8,128)(2,1)}, bf16[1024,768]{1,0:T(8,128)(2,1)}, bf16[1024,768]{1,0:T(8,128)(2,1)}, bf16[1024,768]{1,0:T(8,128)(2,1)},...) custom-call(bf16[1024,768]{1,0:T(8,128)(2,1)} %x_ref.3, ...), custom_call_target="tpu_custom_call" | custom-call | tf_op jit(solution)/shard_map/attend_forward/pallas_call | solution.py:316
  61.7 65.3 %feed_forward.1 = (bf16[1024,768]{1,0:T(8,128)(2,1)}, bf16[1024,768]{1,0:T(8,128)(2,1)}, bf16[1024,768]{1,0:T(8,128)(2,1)}, bf16[1536,384]{1,0:T(8,128)(2,1)}, b...) custom-call(f32[1024,768]{1,0:T(8,128)} %get-tuple-element.56.res_ref, ...), custom_call_target="tpu_custom_call" | custom-call | tf_op jit(solution)/shard_map/feed_forward/pallas_call | solution.py:740
  127.0 116.3 %attend_backward.1 = (bf16[1024,768]{1,0:T(8,128)(2,1)}, bf16[4,1536,384]{2,1,0:T(8,128)(2,1)}, bf16[768,768]{1,0:T(8,128)(2,1)}, bf16[768,768]{1,0:T(8,128)(2,1)}, f32[256,128]{1,0:T(8,128)}) custom-call(bf16[1024,768]{1,0:T(8,128)(2,1)} %get-tuple-element.61.dctx_ref, bf16[1024,768]{1,0:T(8,128)(2,1)} %get-tuple-element.62.att_ref, ...), custom_call_target="tpu_custom_call" | custom-call | tf_op jit(solution)/shard_map/attend_backward/pallas_call | solution.py:1105
  243.3 11.3 %spread_out.1 = (f32[768,2304]{1,0:T(8,128)}, f32[768,768]{1,0:T(8,128)}, f32[768,768]{1,0:T(8,128)}, f32[768,768]{1,0:T(8,128)}, bf16[1024,768]{1,0:T(8,128)(2,...) custom-call(bf16[4,1536,384]{2,1,0:T(8,128)(2,1)} %get-tuple-element, ...), custom_call_target="tpu_custom_call" | custom-call | tf_op jit(solution)/shard_map/spread_out/pallas_call | solution.py:1213

commit v5 on v4

--- a/solution.py
+++ b/solution.py
@@ -152,8 +152,8 @@
         start = pl.multiple_of(part * x_ref.shape[1] + quad * QUAD, QUAD)
         return b_ref[pl.ds(start, QUAD)][None, :]
 
-    for start in range(0, length, BLK):
-        here = slice(start, start + BLK)
+    for start in range(0, length, ROWS):
+        here = slice(start, start + ROWS)
         x = x_ref[here]
         for number, (w, unit, scale, factor) in enumerate(
             ((wq_ref, q_ref, sq_ref, SHRINK), (wk_ref, k_ref, sk_ref, 1.0))
@@ -214,8 +214,8 @@
     def _():
         res_ref[...] = x_ref[...].astype(F32) + bo_ref[...][None, :]
 
-    for start in range(0, length, BLK):
-        here = slice(start, start + BLK)
+    for start in range(0, length, ROWS):
+        here = slice(start, start + ROWS)
         res_ref[here] += dot_nn(ctx_ref[here], wo_ref[...])
 
 
@@ -291,6 +291,7 @@
 
 
 KCH = 256
+ROWS = 256
 
 
 def attend(tokens, segment_ids, w_qkv, b_qkv, kernel, w_out, b_out, w_up, w_down, b_up, dp_size, tensor_size):
@@ -471,7 +472,8 @@
         count = len(self.order)
 
         def begin(copies):
-            for copy in copies:
+            first = len(copies) // 2
+            for copy in copies[first:] + copies[:first]:
                 copy.start()
 
         for stage in range(count):
@@ -539,10 +541,10 @@
 
 
 def ffn_kernel(
-    res_ref, cot_ref, ctx_ref, wo_ref, gain1_ref, shift1_ref, gain2_ref, shift2_ref, bd_ref, bu_ref, wu_ref, wd_ref,
+    res_ref, cot_hbm, ctx_hbm, wo_hbm, gain1_ref, shift1_ref, gain2_ref, shift2_ref, bd_ref, bu_ref, wu_ref, wd_ref,
     out_ref, dproj_ref, dctx_ref, gwo_ref, pu_ref, pd_ref, small_ref,
     low_ref, acc_ref, hid_ref, slope_ref, dffn_ref, dpre_ref, sendu_ref, sendd_ref, recvu_ref, recvd_ref, pdown_ref, yland_ref,
-    send_sem, recv_sem,
+    send_sem, recv_sem, cot_ref, ctx_ref, wo_ref, load_sem,
 ):
     parts = pl.num_programs(0) // 2
     step = pl.program_id(0)
@@ -574,8 +576,21 @@
             cut = slice(start, start + piece)
             yield cut, dot_tn(hid_ref[part, :, cut], dffn_ref[...]).astype(BF16)
 
+    def ready(which):
+        down_to_mate(which).wait()
+        add_rows(pdown_ref.at[which], 0, [(pdown_ref.at[which], 0), (recvd_ref.at[which], 0)], share)
+        if which < heights - 1:
+            to_height(which).start()
+
+    loads = [
+        pltpu.make_async_copy(source, target, load_sem.at[i])
+        for i, (source, target) in enumerate(((cot_hbm, cot_ref), (ctx_hbm, ctx_ref), (wo_hbm, wo_ref)))
+    ]
+
     @pl.when(step == 0)
     def _():
+        for load in loads:
+            load.start()
         barrier = pltpu.get_barrier_semaphore()
         peers = [mate] + [(dp, lax.rem(height + j, heights) * CORES + core) for j in range(1, heights)]
         for peer in peers:
@@ -614,6 +629,8 @@
 
     @pl.when(step == parts)
     def _():
+        loads[0].wait()
+
         def one(t, sums):
             unit, _ = norm_stats(res_ref[at(t)])
             first = unit * gain1_ref[...][None, :] + shift1_ref[...][None, :]
@@ -647,8 +664,11 @@
                 pdown_ref[which, cut] = values
             return carry
 
-        lax.fori_loop(0, heights, theirs, 0)
-        lax.fori_loop(0, heights, ours, 0)
+        for which in range(heights):
+            theirs(which, 0)
+            if which > 0:
+                ready(which - 1)
+            ours(which, 0)
 
     @pl.when(step >= parts)
     def _():
@@ -662,14 +682,9 @@
         bias = lax.fori_loop(0, tiles, one, jnp.zeros((1, share), F32), unroll=UNROLL)
         put_row(6 * (width // PAIR) + f * (share // PAIR), bias)
 
-        for which in range(heights):
-
-            @pl.when(late == which)
-            def _(which=which):
-                down_to_mate(which).wait()
-                add_rows(pdown_ref.at[which], 0, [(pdown_ref.at[which], 0), (recvd_ref.at[which], 0)], share)
-                if which < heights - 1:
-                    to_height(which).start()
+        @pl.when(late == 0)
+        def _():
+            ready(heights - 1)
 
         @pl.when(lax.rem(late, CORES) == 0)
         def _():
@@ -688,6 +703,9 @@
 
     @pl.when(step == 2 * parts - 1)
     def _():
+        loads[1].wait()
+        loads[2].wait()
+
         def one(t, sums):
             unit, scaling = norm_stats(res_ref[at(t)])
             grad = acc_ref[at(t)]
@@ -740,8 +758,8 @@
     return pl.pallas_call(
         ffn_kernel,
         grid=(2 * parts,),
-        in_specs=[whole(count, width)] * 3
-        + [whole(width, width)]
+        in_specs=[whole(count, width)]
+        + [pl.BlockSpec(memory_space=pl.ANY)] * 3
         + [whole(width)] * 5
         + [per_part(1, share), per_part(width, share), per_part(share, width)],
         out_specs=[whole(count, width)] * 3
@@ -768,6 +786,10 @@
             pltpu.VMEM((heights - 1, share, width), BF16),
             pltpu.SemaphoreType.DMA((3, heights)),
             pltpu.SemaphoreType.DMA((3, heights)),
+            pltpu.VMEM((count, width), BF16),
+            pltpu.VMEM((count, width), BF16),
+            pltpu.VMEM((width, width), BF16),
+            pltpu.SemaphoreType.DMA((3,)),
         ],
         compiler_params=pltpu.CompilerParams(vmem_limit_bytes=60 * 2**20, collective_id=0, has_side_effects=True),
         name="feed_forward",
@@ -776,10 +798,10 @@
 
 def attend_back_kernel(
     dctx_ref, att_ref, inv_ref, q_ref, k_ref, v_ref, sq_ref, sk_ref, w_ref, s_ref, x_ref, seg_ref,
-    wqkv_ref, kernel_ref, dproj_ref, gwo_ref, pu_ref, pd_ref, small_ref,
+    wqkv_hbm, kernel_ref, dproj_ref, gwo_ref, pu_ref, pd_ref, small_ref,
     gt_ref, all_out, up_out, down_out, few_out,
     near_ref, vv_ref, dpad_ref, dcos_ref, dq_ref, dk_ref, dv_ref, joined_ref, gwacc_ref, conv_ref,
-    gwlow_ref, gb_ref, flip_ref, mini_ref, all_ref, up_ref, down_ref, few_ref, out_sem, *links,
+    gwlow_ref, gb_ref, flip_ref, mini_ref, all_ref, up_ref, down_ref, few_ref, out_sem, wqkv_ref, load_sem, *links,
     plan, quads, seqs,
 ):
     quad, row = pl.program_id(0), pl.program_id(1)
@@ -806,8 +828,11 @@
         conv_ref[...] = jnp.zeros_like(conv_ref)
         gwacc_ref[...] = jnp.zeros_like(gwacc_ref)
 
+    load = pltpu.make_async_copy(wqkv_hbm, wqkv_ref, load_sem)
+
     @pl.when((quad == 0) & (row == 0))
     def _():
+        load.start()
         gb_ref[...] = jnp.zeros_like(gb_ref)
         flip_ref[...] = place_taps(kernel_ref[...], True)
         mini_ref[...] = jnp.zeros_like(mini_ref)
@@ -823,8 +848,8 @@
         d_summed = (d_ctx.astype(F32) * inverse).astype(BF16)
         d_total = (-d_summed.astype(F32) * att_ref[:, at].astype(F32)).astype(BF16)
         both = jnp.concatenate([d_summed, d_total], 1)
-        dk = jnp.zeros((length, PAIR), F32)
-        dv = jnp.zeros((length, PAIR), F32)
+        dk = jnp.zeros((PAIR, length), F32)
+        dv = jnp.zeros((PAIR, length), F32)
         turn = (quad * seqs + row) * (QUAD // PAIR) + pair
         for half in range(2):
             for when in range(half, calls, 2):
@@ -864,13 +889,13 @@
                 else:
                     dv_ref[here] += grown
                 conv_ref[head] += near.astype(F32) * dot_nt(d_ctx[here], vv_ref[half, window, :PAIR])
-            dk += dot_tn(dcos_ref[...], q_ref[:, at] * mask)
-            dv += dot_tn(w_ref[0, head], d_summed * mask)
-        dv_ref[...] += dv
+            dk += dot_tn(q_ref[:, at] * mask, dcos_ref[...])
+            dv += dot_tn(d_summed * mask, w_ref[0, head])
+        dv_ref[...] += dv.T
         grad = SLOPE * dq_ref[...]
         unit = q_ref[:, at].astype(F32)
         d_query = sq_ref[:, at].astype(F32) * (SHRINK * grad - unit * (head_sum(grad * unit) / SHRINK))
-        grad = SLOPE * dk
+        grad = SLOPE * dk.T
         unit = k_ref[:, at].astype(F32)
         d_key = sk_ref[:, at].astype(F32) * (grad - unit * head_sum(grad * unit))
         for part, values in enumerate((d_query, d_key, dv_ref[...])):
@@ -911,6 +936,10 @@
     def _():
         for event in ticks.get(calls, ()):
             event()
+
+    @pl.when((quad == quads - 1) & (row == 0))
+    def _():
+        load.wait()
 
     @pl.when(quad == quads - 1)
     def _():
@@ -1110,7 +1139,7 @@
         + [
             wide,
             whole(*segment_ids.shape),
-            whole(width, 3 * width),
+            pl.BlockSpec(memory_space=pl.ANY),
             whole(*kernel.shape),
             wide,
             whole(*gwo.shape), whole(*pu.shape), whole(*pd.shape), whole(*small.shape),
@@ -1146,6 +1175,8 @@
             pltpu.VMEM((share, width), BF16),
             pltpu.VMEM((minis, PAIR), F32),
             pltpu.SemaphoreType.DMA((len(link_plan(sizes, width, share, quads)),)),
+            pltpu.VMEM((width, 3 * width), BF16),
+            pltpu.SemaphoreType.DMA,
         ]
         + scratch,
         compiler_params=pltpu.CompilerParams(vmem_limit_bytes=60 * 2**20, collective_id=1, has_side_effects=True),

time: 255 us -> 247 us (0.969)
  Pallas kernels: 254 us -> 245 us
    pallas_call x1, Pallas kernels: 65.3 us -> 59.8 us  [feed_forward(): pl.pallas_call(ffn_kernel, grid=(2 * parts,), in_specs=[whole(count, widt...]
where the time goes in v5:
time: 247 us; the launch traced here: 246 us
  Pallas kernels  245 us (99%)
    pallas_call x1, Pallas kernels, attend_back(): pl.pallas_call(functools.partial(attend_back_kernel, plan=(None, sizes, d...  114 us
    pallas_call x1, Pallas kernels, attend(): pl.pallas_call(functools.partial(attend_kernel, dp_size=dp_size, tensor_s...  60.3 us
    pallas_call x1, Pallas kernels, feed_forward(): pl.pallas_call(ffn_kernel, grid=(2 * parts,), in_specs=[whole(count, widt...  59.8 us
    pallas_call x1, Pallas kernels, spread_out(): pl.pallas_call(functools.partial(spread_kernel, first_lane=first_lane, ba...  11.3 us

profile of v5, /device:TPU:0, one launch (start us, length us, event | category | flops | bytes accessed | tf_op | source)
XLA Modules:
  0.0 246.1 jit_solution(6599038577535306803)
XLA Ops:
  0.6 60.3 %attend_forward.1 = (bf16[1024,768]{1,0:T(8,128)(2,1)}, bf16[1024,768]{1,0:T(8,128)(2,1)}, bf16[1024,768]{1,0:T(8,128)(2,1)}, bf16[1024,768]{1,0:T(8,128)(2,1)},...) custom-call(bf16[1024,768]{1,0:T(8,128)(2,1)} %x_ref.3, ...), custom_call_target="tpu_custom_call" | custom-call | tf_op jit(solution)/shard_map/attend_forward/pallas_call | solution.py:317
  61.0 59.8 %feed_forward.1 = (bf16[1024,768]{1,0:T(8,128)(2,1)}, bf16[1024,768]{1,0:T(8,128)(2,1)}, bf16[1024,768]{1,0:T(8,128)(2,1)}, bf16[1536,384]{1,0:T(8,128)(2,1)}, b...) custom-call(f32[1024,768]{1,0:T(8,128)} %get-tuple-element.56.res_ref, ...), custom_call_target="tpu_custom_call" | custom-call | tf_op jit(solution)/shard_map/feed_forward/pallas_call | solution.py:758
  120.8 113.8 %attend_backward.1 = (bf16[1024,768]{1,0:T(8,128)(2,1)}, bf16[4,1536,384]{2,1,0:T(8,128)(2,1)}, bf16[768,768]{1,0:T(8,128)(2,1)}, bf16[768,768]{1,0:T(8,128)(2,1)}, f32[256,128]{1,0:T(8,128)}) custom-call(bf16[1024,768]{1,0:T(8,128)(2,1)} %get-tuple-element.61.dctx_ref, bf16[1024,768]{1,0:T(8,128)(2,1)} %get-tuple-element.62.att_ref, ...), custom_call_target="tpu_custom_call" | custom-call | tf_op jit(solution)/shard_map/attend_backward/pallas_call | solution.py:1134
  234.6 11.3 %spread_out.1 = (f32[768,2304]{1,0:T(8,128)}, f32[768,768]{1,0:T(8,128)}, f32[768,768]{1,0:T(8,128)}, f32[768,768]{1,0:T(8,128)}, bf16[1024,768]{1,0:T(8,128)(2,...) custom-call(bf16[4,1536,384]{2,1,0:T(8,128)(2,1)} %get-tuple-element, ...), custom_call_target="tpu_custom_call" | custom-call | tf_op jit(solution)/shard_map/spread_out/pallas_call | solution.py:1244

commit v6 on v5

--- a/solution.py
+++ b/solution.py
@@ -962,30 +962,30 @@
 
 FFN_PLAN = (
     (
-        (("x", "z"), (4, 9, 15, 24, 54)),
-        (("z", "x"), (3, 27, 30, 50, 59)),
+        (("z", "x"), (1, 28, 42, 44, 57)),
+        (("x", "z"), (1, 7, 14, 38, 48)),
     ),
     (
-        (("x", "z"), (0, 8, 15, 21, 34, 43)),
-        (("x", "z"), (7, 19, 23, 29, 38, 56)),
+        (("x", "z"), (0, 8, 13, 17, 24, 36)),
+        (("x", "z"), (6, 16, 23, 42, 48, 55)),
     ),
 )
 ALL_PLAN = (
     (
-        (3, 1, (2, 4, 11, 13, 16, 29, 35, 45, 55)),
+        (3, 1, (2, 4, 13, 16, 21, 27, 33, 43, 54)),
     ),
     (
-        (3, 0, (10, 11, 17, 26, 31, 41, 47, 52, 59)),
+        (3, 0, (13, 18, 24, 29, 31, 41, 43, 51, 53)),
     ),
     (
-        (3, 0, (19, 21, 28, 37, 42, 48, 51, 57, 60)),
+        (3, 1, (17, 18, 23, 26, 29, 34, 41, 46, 47)),
     ),
     (
-        (3, 1, (24, 25, 32, 36, 39, 44, 48, 55, 58)),
+        (3, 1, (24, 25, 30, 35, 39, 42, 45, 50, 52)),
     ),
 )
 MINI_ORDER = 1
-MINI_TIMES = (25, 27, 33, 40, 46, 49, 52, 53, 55)
+MINI_TIMES = (29, 31, 32, 37, 40, 42, 49, 52, 56)
 FFN_ROWS = 384
 ORDERS = (("core", "x", "y", "z"), ("core", "y", "x", "z"))
 

time: 247 us -> 240 us (0.972)
  Pallas kernels: 245 us -> 239 us
    pallas_call x1, Pallas kernels: 114 us -> 108 us  [attend_back(): pl.pallas_call(functools.partial(attend_back_kernel, plan=(None, sizes, d...]
where the time goes in v6:
time: 240 us
  Pallas kernels  239 us (100%)
    pallas_call x1, Pallas kernels, attend_back(): pl.pallas_call(functools.partial(attend_back_kernel, plan=(None, sizes, d...  108 us
    pallas_call x1, Pallas kernels, attend(): pl.pallas_call(functools.partial(attend_kernel, dp_size=dp_size, tensor_s...  60.3 us
    pallas_call x1, Pallas kernels, feed_forward(): pl.pallas_call(ffn_kernel, grid=(2 * parts,), in_specs=[whole(count, widt...  59.8 us
    pallas_call x1, Pallas kernels, spread_out(): pl.pallas_call(functools.partial(spread_kernel, first_lane=first_lane, ba...  11.3 us

profile of v6, /device:TPU:0, one launch (start us, length us, event | category | flops | bytes accessed | tf_op | source)
XLA Modules:
  0.0 239.9 jit_solution(5747340141711953466)
XLA Ops:
  0.6 60.3 %attend_forward.1 = (bf16[1024,768]{1,0:T(8,128)(2,1)}, bf16[1024,768]{1,0:T(8,128)(2,1)}, bf16[1024,768]{1,0:T(8,128)(2,1)}, bf16[1024,768]{1,0:T(8,128)(2,1)},...) custom-call(bf16[1024,768]{1,0:T(8,128)(2,1)} %x_ref.3, ...), custom_call_target="tpu_custom_call" | custom-call | tf_op jit(solution)/shard_map/attend_forward/pallas_call | solution.py:317
  61.0 59.8 %feed_forward.1 = (bf16[1024,768]{1,0:T(8,128)(2,1)}, bf16[1024,768]{1,0:T(8,128)(2,1)}, bf16[1024,768]{1,0:T(8,128)(2,1)}, bf16[1536,384]{1,0:T(8,128)(2,1)}, b...) custom-call(f32[1024,768]{1,0:T(8,128)} %get-tuple-element.56.res_ref, ...), custom_call_target="tpu_custom_call" | custom-call | tf_op jit(solution)/shard_map/feed_forward/pallas_call | solution.py:758
  120.8 107.6 %attend_backward.1 = (bf16[1024,768]{1,0:T(8,128)(2,1)}, bf16[4,1536,384]{2,1,0:T(8,128)(2,1)}, bf16[768,768]{1,0:T(8,128)(2,1)}, bf16[768,768]{1,0:T(8,128)(2,1)}, f32[256,128]{1,0:T(8,128)}) custom-call(bf16[1024,768]{1,0:T(8,128)(2,1)} %get-tuple-element.61.dctx_ref, bf16[1024,768]{1,0:T(8,128)(2,1)} %get-tuple-element.62.att_ref, ...), custom_call_target="tpu_custom_call" | custom-call | tf_op jit(solution)/shard_map/attend_backward/pallas_call | solution.py:1134
  228.4 11.3 %spread_out.1 = (f32[768,2304]{1,0:T(8,128)}, f32[768,768]{1,0:T(8,128)}, f32[768,768]{1,0:T(8,128)}, f32[768,768]{1,0:T(8,128)}, bf16[1024,768]{1,0:T(8,128)(2,...) custom-call(bf16[4,1536,384]{2,1,0:T(8,128)(2,1)} %get-tuple-element, ...), custom_call_target="tpu_custom_call" | custom-call | tf_op jit(solution)/shard_map/spread_out/pallas_call | solution.py:1244

commit v7 on v6

--- a/solution.py
+++ b/solution.py
@@ -1229,7 +1229,7 @@
 def spread_out(grads, up, down, few, out, gt, width, heads, taps, first_lane, base):
     chunks = grads.shape[0]
     quads = chunks - 1
-    steps = 8
+    steps = 16
     rows_of = width // steps
     share = up.shape[1]
     down_rows = share // steps

time: 240 us -> 244 us (1.017)
  Pallas kernels: 239 us -> 243 us
    pallas_call x1, Pallas kernels: 11.3 us -> 15.2 us  [spread_out(): pl.pallas_call(functools.partial(spread_kernel, first_lane=first_lane, ba...]
where the time goes in v7:
time: 244 us
  Pallas kernels  243 us (100%)
    pallas_call x1, Pallas kernels, attend_back(): pl.pallas_call(functools.partial(attend_back_kernel, plan=(None, sizes, d...  108 us
    pallas_call x1, Pallas kernels, attend(): pl.pallas_call(functools.partial(attend_kernel, dp_size=dp_size, tensor_s...  60.3 us
    pallas_call x1, Pallas kernels, feed_forward(): pl.pallas_call(ffn_kernel, grid=(2 * parts,), in_specs=[whole(count, widt...  59.8 us
    pallas_call x1, Pallas kernels, spread_out(): pl.pallas_call(functools.partial(spread_kernel, first_lane=first_lane, ba...  15.2 us

profile of v7, /device:TPU:0, one launch (start us, length us, event | category | flops | bytes accessed | tf_op | source)
XLA Modules:
  0.0 243.7 jit_solution(10880482378990009682)
XLA Ops:
  0.6 60.3 %attend_forward.1 = (bf16[1024,768]{1,0:T(8,128)(2,1)}, bf16[1024,768]{1,0:T(8,128)(2,1)}, bf16[1024,768]{1,0:T(8,128)(2,1)}, bf16[1024,768]{1,0:T(8,128)(2,1)},...) custom-call(bf16[1024,768]{1,0:T(8,128)(2,1)} %x_ref.3, ...), custom_call_target="tpu_custom_call" | custom-call | tf_op jit(solution)/shard_map/attend_forward/pallas_call | solution.py:317
  61.0 59.8 %feed_forward.1 = (bf16[1024,768]{1,0:T(8,128)(2,1)}, bf16[1024,768]{1,0:T(8,128)(2,1)}, bf16[1024,768]{1,0:T(8,128)(2,1)}, bf16[1536,384]{1,0:T(8,128)(2,1)}, b...) custom-call(f32[1024,768]{1,0:T(8,128)} %get-tuple-element.56.res_ref, ...), custom_call_target="tpu_custom_call" | custom-call | tf_op jit(solution)/shard_map/feed_forward/pallas_call | solution.py:758
  120.8 107.6 %attend_backward.1 = (bf16[1024,768]{1,0:T(8,128)(2,1)}, bf16[4,1536,384]{2,1,0:T(8,128)(2,1)}, bf16[768,768]{1,0:T(8,128)(2,1)}, bf16[768,768]{1,0:T(8,128)(2,1)}, f32[256,128]{1,0:T(8,128)}) custom-call(bf16[1024,768]{1,0:T(8,128)(2,1)} %get-tuple-element.61.dctx_ref, bf16[1024,768]{1,0:T(8,128)(2,1)} %get-tuple-element.62.att_ref, ...), custom_call_target="tpu_custom_call" | custom-call | tf_op jit(solution)/shard_map/attend_backward/pallas_call | solution.py:1134
  228.4 15.2 %spread_out.1 = (f32[768,2304]{1,0:T(8,128)}, f32[768,768]{1,0:T(8,128)}, f32[768,768]{1,0:T(8,128)}, f32[768,768]{1,0:T(8,128)}, bf16[1024,768]{1,0:T(8,128)(2,...) custom-call(bf16[4,1536,384]{2,1,0:T(8,128)(2,1)} %get-tuple-element, ...), custom_call_target="tpu_custom_call" | custom-call | tf_op jit(solution)/shard_map/spread_out/pallas_call | solution.py:1244
